TPU v7x, 32 devices: a whole 2x2x4 slice. The times are simulated.
32 devices in a mesh: seq: 8 (over y, x, core), head: 4 (over z).
Axes of the slice: x: 2, y: 2, z: 4, core: 2. Of those that a mesh axis runs over, the one named last changes fastest.
Arguments:
- tokens: bfloat16 [8192, 2048], P('seq', 'head'), may hold values from -6 to 6
- prenorm: bfloat16 [2048], P('head'), may hold values from 0.5 to 1.5
- gating: bfloat16 [2048, 4096], P(None, 'head'), may hold values from -0.125 to 0.125
- values: bfloat16 [2048, 4096], P(None, 'head'), may hold values from -0.125 to 0.125
- control: bfloat16 [2048, 256], replicated, may hold values from -0.125 to 0.125
- timestep: bfloat16 [2048, 64], P(None, 'head'), may hold values from -0.125 to 0.125
- kernel: float32 [4, 4096], P(None, 'head'), may hold values from -3 to 3
- offset: float32 [4096], P('head'), may hold values from -1.8 to 1.8
- filters: float32 [4, 256], replicated, may hold values from -3 to 3
- baseline: float32 [256], replicated, may hold values from -1.8 to 1.8
- timing: float32 [64], P('head'), may hold values from -5 to -4
- damping: float32 [64], P('head')
- direct: float32 [64], P('head'), may hold values from 0.5 to 1.5
- postnorm: float32 [4096], P('head'), may hold values from 0.5 to 1.5
- readout: bfloat16 [2048, 4096], P(None, 'head'), may hold values from -0.09375 to 0.09375
- doc_starts: int32 [8192], P('seq'), may hold values from 0 to 1, as said below
- cotangent: bfloat16 [8192, 2048], P('seq', 'head'), may hold values from -6 to 6
Outputs:
- mixed: bfloat16 [8192, 2048], P('seq', 'head')
- tokens_gradient: float32 [8192, 2048], P('seq', 'head')
- prenorm_gradient: float32 [2048], replicated
- gating_gradient: float32 [2048, 4096], P('seq', 'head')
- values_gradient: float32 [2048, 4096], P('seq', 'head')
- control_gradient: float32 [2048, 256], replicated
- timestep_gradient: float32 [2048, 64], P('seq', 'head')
- kernel_gradient: float32 [4, 4096], replicated
- offset_gradient: float32 [4096], replicated
- filters_gradient: float32 [4, 256], replicated
- baseline_gradient: float32 [256], replicated
- timing_gradient: float32 [64], replicated
- damping_gradient: float32 [64], replicated
- direct_gradient: float32 [64], replicated
- postnorm_gradient: float32 [4096], replicated
- readout_gradient: float32 [2048, 4096], P('seq', 'head')
Inputs may be any that keep to these rules, and one draw needn't show every extreme that they name: `doc_starts`: token 0 starts a document.
All inputs are finite; a program needn't handle non-finite values.
Results may differ from a plain program's by a relative error of at most 0.012.
Values may be sent and summed in bfloat16 or wider, within the bound.
No kernel may reach another device: no remote copies, remote signals or barrier semaphores. Data moves between devices by JAX's collectives and lax.ppermute only.
A program may use at most 256 MiB of HBM per device.

v0:
```python
import jax
import jax.numpy as jnp
from jax import lax
from jax.sharding import PartitionSpec as P

D = 2048
HEADS = 64
HDIM = 64
STATE = 128
SPAN = 256
INNER = 4096


epsilon = 1e-05
highest = lax.Precision.HIGHEST


def shifted(value, axis, steps):
    count = lax.axis_size(axis)
    leading, last = (max(0, -steps), min(count, count - steps))
    return lax.ppermute(value, axis, [(source, source + steps) for source in range(leading, last)])


def prefix_2(part, axis, combine, identity, reverse):
    count = lax.axis_size(axis)
    place = lax.axis_index(axis)
    ahead = count - 1 - place if reverse else place
    gathered = jax.tree.map(lambda a: lax.all_gather(a, axis), part)
    state = jax.tree.map(lambda a, e: jnp.zeros_like(a) + jnp.asarray(e, a.dtype), part, identity)

    def one(step, state):
        source = count - 1 - step if reverse else step
        return combine(
            state, jax.tree.map(lambda a: lax.dynamic_index_in_dim(a, source, 0, False), gathered)
        )

    return lax.fori_loop(0, ahead, one, state)


def causal_conv(extended, weights, biases, length):
    summed = biases
    for offset_index in range(weights.shape[0]):
        summed = summed + weights[offset_index] * lax.slice_in_dim(
            extended, offset_index, offset_index + length, axis=extended.ndim - 2
        )
    return summed


def spanned_scan(signal, writers, readers, step_size, log_decay, starts, incoming):
    length, head_count = step_size.shape
    blocks = length // SPAN
    signal_blocks = signal.reshape(blocks, SPAN, head_count, HDIM)
    write_blocks = writers.reshape(blocks, SPAN, -1)
    read_blocks = readers.reshape(blocks, SPAN, -1)
    step_blocks = jnp.swapaxes(step_size.reshape(blocks, SPAN, head_count), 1, 2)
    cumulative = jnp.cumsum(jnp.swapaxes(log_decay.reshape(blocks, SPAN, head_count), 1, 2), axis=2)
    segment = jnp.cumsum(starts.reshape(blocks, SPAN), axis=1)
    places = jnp.arange(SPAN)
    linked = (segment[:, :, None] == segment[:, None, :]) & (places[:, None] >= places[None, :])
    spread = cumulative[:, :, :, None] - cumulative[:, :, None, :]
    decays = jnp.exp(jnp.where(linked[:, None], spread, -1e30))
    scores = jnp.einsum("ktn,ksn->kts", read_blocks, write_blocks, precision=highest)
    mixing = decays * scores[:, None] * step_blocks[:, :, None, :]
    within = jnp.einsum("khts,kshp->kthp", mixing, signal_blocks, precision=highest)
    ending = segment == segment[:, -1:]
    toward = (
        jnp.exp(jnp.where(ending[:, None, :], cumulative[:, :, -1:] - cumulative, -1e30))
        * step_blocks
    )
    produced = jnp.einsum(
        "khs,kshp,ksn->khpn", toward, signal_blocks, write_blocks, precision=highest
    )
    passing = jnp.exp(cumulative[:, :, -1]) * (segment[:, -1] == 0)[:, None]
    entering = jnp.exp(cumulative) * (segment == 0)[:, None, :]
    current = incoming
    entries = []
    for position in range(blocks):
        entries.append(current)
        current = passing[position][:, None, None] * current + produced[position]
    carried = jnp.einsum(
        "khq,kqn,khpn->kqhp", entering, read_blocks, jnp.stack(entries), precision=highest
    )
    return ((within + carried).reshape(length, head_count * HDIM), current)


def activate(
    projected,
    shared,
    timestep_in,
    edge_values,
    edge_shared,
    kernel,
    offset,
    filters,
    baseline,
    timing,
    damping,
):
    length = projected.shape[0]
    signal = jax.nn.silu(
        causal_conv(jnp.concatenate([edge_values, projected], axis=0), kernel, offset, length)
    )
    control_out = jax.nn.silu(
        causal_conv(jnp.concatenate([edge_shared, shared], axis=0), filters, baseline, length)
    )
    step_size = jax.nn.softplus(timestep_in + timing)
    log_decay = -step_size * jnp.exp(damping)
    return (signal, control_out[:, :STATE], control_out[:, STATE:], step_size, log_decay)


def combine(earlier, later):
    return (earlier[0] * later[0], later[0][:, None, None] * earlier[1] + later[1])


def embed(piece, whole_shape, axis_number):
    begin = lax.axis_index("head") * piece.shape[axis_number]
    return lax.dynamic_update_slice_in_dim(
        jnp.zeros(whole_shape, jnp.float32), piece, begin, axis_number
    )


def shards(
    tokens,
    prenorm,
    gating,
    values,
    control,
    timestep,
    kernel,
    offset,
    filters,
    baseline,
    timing,
    damping,
    direct,
    postnorm,
    readout,
    doc_starts,
    cotangent,
):
    contract_last = (((1,), (1,)), ((), ()))
    contract_first = (((0,), (0,)), ((), ()))
    gathered, gain_full = (
        lax.all_gather(tokens, "head", axis=1, tiled=True),
        lax.all_gather(prenorm, "head", axis=0, tiled=True),
    )
    residual = gathered.astype(jnp.float32)
    scale = lax.rsqrt(jnp.mean(residual * residual, axis=1, keepdims=True) + epsilon)
    unit_rows = residual * scale
    normed = (unit_rows * gain_full.astype(jnp.float32)).astype(jnp.bfloat16)
    gate_in = jnp.dot(normed, gating, preferred_element_type=jnp.float32)
    projected = jnp.dot(normed, values, preferred_element_type=jnp.float32)
    shared = jnp.dot(normed, control, preferred_element_type=jnp.float32)
    timestep_in = jnp.dot(normed, timestep, preferred_element_type=jnp.float32)
    width = kernel.shape[0] - 1
    length = tokens.shape[0]
    edge_values, edge_shared = shifted(
        (projected[length - width :], shared[length - width :]), "seq", 1
    )
    outputs, activate_back = jax.vjp(
        activate,
        projected,
        shared,
        timestep_in,
        edge_values,
        edge_shared,
        kernel,
        offset,
        filters,
        baseline,
        timing,
        damping,
    )
    signal, writers, readers, step_size, log_decay = outputs
    head_count = step_size.shape[1]
    running = jnp.cumsum(log_decay, axis=0)
    counted = jnp.cumsum(doc_starts)
    passing = jnp.exp(running[-1]) * (counted[-1] == 0)
    toward = (
        jnp.exp(jnp.where((counted == counted[-1])[:, None], running[-1] - running, -1e30))
        * step_size
    )
    produced = jnp.einsum(
        "th,thp,tn->hpn",
        toward,
        signal.reshape(length, head_count, HDIM),
        writers,
        precision=highest,
    )
    identity = (jnp.ones_like(passing), jnp.zeros_like(produced))
    prefix = prefix_2((passing, produced), "seq", combine, identity, False)

    def scan_local(signal_in, writers_in, readers_in, step_in, decay_in, incoming):
        return spanned_scan(
            signal_in, writers_in, readers_in, step_in, decay_in, doc_starts, incoming
        )

    scan_out, scan_back = jax.vjp(
        scan_local, signal, writers, readers, step_size, log_decay, prefix[1]
    )
    skip = jnp.repeat(direct, HDIM)
    full = scan_out[0] + skip * signal
    gate = jax.nn.silu(gate_in)
    gated = full * gate
    squares = lax.psum(jnp.sum(gated * gated, axis=1), "head")
    inverse = lax.rsqrt(squares / INNER + epsilon)[:, None]
    unit_gated = gated * inverse
    normalized = (unit_gated * postnorm).astype(jnp.bfloat16)
    partial_rows = lax.dot_general(
        normalized, readout, contract_last, preferred_element_type=jnp.float32
    )
    branch = lax.psum_scatter(partial_rows, "head", scatter_dimension=1, tiled=True)
    mixed = (tokens.astype(jnp.float32) + branch).astype(jnp.bfloat16)
    upstream = lax.all_gather(cotangent, "head", axis=1, tiled=True)
    norm_cot = jnp.dot(upstream, readout, preferred_element_type=jnp.float32)
    readout_local = lax.dot_general(
        upstream, normalized, contract_first, preferred_element_type=jnp.float32
    )
    postnorm_local = jnp.sum(norm_cot * unit_gated, axis=0)
    scaled_cot = norm_cot * postnorm
    inner_sum = lax.psum(jnp.sum(scaled_cot * unit_gated, axis=1), "head")
    gated_cot = inverse * (scaled_cot - unit_gated * (inner_sum / INNER)[:, None])
    full_cot = gated_cot * gate
    sigmoid_gate = jax.nn.sigmoid(gate_in)
    gate_cot = gated_cot * full * sigmoid_gate * (1.0 + gate_in * (1.0 - sigmoid_gate))
    direct_local = jnp.sum((full_cot * signal).reshape(length, head_count, HDIM), axis=(0, 2))
    entering = jnp.exp(running) * (counted == 0)[:, None]
    pending = jnp.einsum(
        "th,thp,tn->hpn",
        entering,
        full_cot.reshape(length, head_count, HDIM),
        readers,
        precision=highest,
    )
    suffix = prefix_2((passing, pending), "seq", combine, identity, True)
    signal_cot, writer_cot, reader_cot, step_cot, decay_cot, ignored = scan_back(
        (full_cot, suffix[1])
    )
    signal_cot = signal_cot + skip * full_cot
    back = activate_back((signal_cot, writer_cot, reader_cot, step_cot, decay_cot))
    values_cot, shared_cot, timestep_cot, edge_values_cot, edge_shared_cot = (
        back[0],
        back[1],
        back[2],
        back[3],
        back[4],
    )
    kernel_local, offset_local, filters_local, baseline_local, timing_local, damping_local = (
        back[5],
        back[6],
        back[7],
        back[8],
        back[9],
        back[10],
    )
    later_values, later_shared = shifted((edge_values_cot, edge_shared_cot), "seq", -1)
    values_cot = values_cot.at[length - width :].add(later_values)
    shared_cot = shared_cot.at[length - width :].add(later_shared)
    gate_low = gate_cot.astype(jnp.bfloat16)
    values_low = values_cot.astype(jnp.bfloat16)
    shared_low = shared_cot.astype(jnp.bfloat16)
    timestep_low = timestep_cot.astype(jnp.bfloat16)
    normed_cot = lax.dot_general(
        gate_low, gating, contract_last, preferred_element_type=jnp.float32
    )
    normed_cot = normed_cot + lax.dot_general(
        values_low, values, contract_last, preferred_element_type=jnp.float32
    )
    normed_cot = normed_cot + lax.dot_general(
        shared_low, control, contract_last, preferred_element_type=jnp.float32
    )
    normed_cot = normed_cot + lax.dot_general(
        timestep_low, timestep, contract_last, preferred_element_type=jnp.float32
    )
    gating_local = lax.dot_general(
        normed, gate_low, contract_first, preferred_element_type=jnp.float32
    )
    values_local = lax.dot_general(
        normed, values_low, contract_first, preferred_element_type=jnp.float32
    )
    control_local = lax.dot_general(
        normed, shared_low, contract_first, preferred_element_type=jnp.float32
    )
    timestep_local = lax.dot_general(
        normed, timestep_low, contract_first, preferred_element_type=jnp.float32
    )
    share = tokens.shape[1]
    normed_total = lax.psum(normed_cot, "head")
    scaled_rows = normed_total * gain_full.astype(jnp.float32)
    row_mean = jnp.mean(scaled_rows * unit_rows, axis=1, keepdims=True)
    token_full = scale * (scaled_rows - unit_rows * row_mean)
    begin = lax.axis_index("head") * share
    token_local = lax.dynamic_slice_in_dim(token_full, begin, share, 1)
    prenorm_local = lax.dynamic_slice_in_dim(
        jnp.sum(normed_total * unit_rows, axis=0), begin, share, 0
    )
    tokens_gradient = cotangent.astype(jnp.float32) + token_local
    gating_gradient, values_gradient, timestep_gradient, readout_gradient = (
        lax.psum_scatter(gating_local, "seq", scatter_dimension=0, tiled=True),
        lax.psum_scatter(values_local, "seq", scatter_dimension=0, tiled=True),
        lax.psum_scatter(timestep_local, "seq", scatter_dimension=0, tiled=True),
        lax.psum_scatter(readout_local, "seq", scatter_dimension=0, tiled=True),
    )
    totals = lax.psum(
        (
            control_local,
            filters_local,
            baseline_local,
            embed(prenorm_local, (D,), 0),
            embed(kernel_local, (kernel.shape[0], INNER), 1),
            embed(offset_local, (INNER,), 0),
            embed(timing_local, (HEADS,), 0),
            embed(damping_local, (HEADS,), 0),
            embed(direct_local, (HEADS,), 0),
            embed(postnorm_local, (INNER,), 0),
        ),
        ("seq", "head"),
    )
    return (
        mixed,
        tokens_gradient,
        totals[3],
        gating_gradient,
        values_gradient,
        totals[0],
        timestep_gradient,
        totals[4],
        totals[5],
        totals[1],
        totals[2],
        totals[6],
        totals[7],
        totals[8],
        totals[9],
        readout_gradient,
    )


def solution(mesh):
    return jax.shard_map(
        shards,
        mesh=mesh,
        in_specs=(
            P("seq", "head"),
            P("head"),
            P(None, "head"),
            P(None, "head"),
            P(),
            P(None, "head"),
            P(None, "head"),
            P("head"),
            P(),
            P(),
            P("head"),
            P("head"),
            P("head"),
            P("head"),
            P(None, "head"),
            P("seq"),
            P("seq", "head"),
        ),
        out_specs=(
            P("seq", "head"),
            P("seq", "head"),
            P(),
            P("seq", "head"),
            P("seq", "head"),
            P(),
            P("seq", "head"),
            P(),
            P(),
            P(),
            P(),
            P(),
            P(),
            P(),
            P(),
            P("seq", "head"),
        ),
        check_vma=False,
    )
```

profile of v0, /device:TPU:4, one launch (start us, length us, event | category | flops | bytes accessed | tf_op | source)
XLA Modules:
  0.0 1301.9 jit_solution(17325820973571066875)
XLA Ops:
  11.8 12.2 all-gather.2
  26.5 65.1 %all-gather.9.cloned.1.call-done = bf16[1024,2048]{1,0:T(8,128)(2,1)} async-done(((bf16[1024,512]{1,0:T(8,128)(2,1)}), bf16[1024,2048]{1,0:T(8,128)(2,1)}) %all-gather.9.cloned.1.call-update) | async-done | bytes 4194320 | tf_op jit(solution)/shard_map/all_gather | solution.py:144
  192.2 20.5 %fusion.29 = f32[4,256,16,64]{1,3,2,0:T(8,128)} fusion(f32[4,16,64,256]{3,2,1,0:T(8,128)S(1)} %fusion.72, f32[4,256,16]{1,2,0:T(8,128)S(1)} %get-tuple-element.344, f32[4,16,256]{2,1,0:T(8,128)S(1)} %bitcast.369, f32[4,256,256]{2,1,0:T(8,128)S(1)} %copy-done.46, f32[4,16,256]{2,1,0:T(8,128)S(1)} %copy-done.57, pred[4,256,256]{2,1,0:T(8,128)(4,1)S(1)} %copy-done.53, ...), kind=kOutput, calls=%fused_computation.49 | convolution fusion | flops 3240099840 | bytes 14090240 | tf_op jit(solution)/shard_map/jvp(khts,kshp->kthp)/dot_general | solution.py:64
  228.4 15.0 %multiply_reduce_fusion.13 = (f32[1024]{0:T(1024)}, f32[1024,1024]{1,0:T(8,128)}, f32[1024,1024]{1,0:T(8,128)}) fusion(f32[1024,1024]{1,0:T(8,128)} %reshape.458, f32[1024,1024]{1,0:T(8,128)} %get-tuple-element.321, f32[1024]{0:T(1024)S(1)} %mul.639, bf16[1024,2048]{1,0:T(8,128)(2,1)} %copy-done.5, bf16[2048,1024]{1,0:T(8,128)(2,1)} %param.27), kind=kOutput, calls=%fused_computation.65 | convolution fusion | flops 4308597760 | bytes 25174016 | tf_op jit(solution)/shard_map/dot_general | solution.py:151
  243.4 13.1 %psum.91 = f32[1024]{0:T(1024)} all-reduce(f32[1024]{0:T(1024)} %get-tuple-element.315), channel_id=1, replica_groups=mesh['seq'=8,'head'=4] {'head'}, use_global_device_ids=true, to_apply=%region_12.13 | all-reduce | flops 1024 | bytes 8192 | tf_op jit(solution)/shard_map/psum | solution.py:205
  259.2 12.0 multiply_reduce_fusion.6
  271.2 9.9 psum.92
  281.8 11.7 multiply_reduce_fusion.7
  311.3 9.4 fusion.68
  320.8 29.6 %fusion.7 = (f32[4,16,256]{2,1,0:T(8,128)}, f32[4,16,256]{2,1,0:T(8,128)}, f32[4,16,256]{2,1,0:T(8,128)}, f32[4,256,256]{2,1,0:T(8,128)S(1)}) fusion(f32[4,16,256]{2,1,0:T(8,128)S(1)} %bitcast.370, f32[4,256,256]{2,1,0:T(8,128)S(1)} %copy-done.47, f32[4,16,256]{2,1,0:T(8,128)S(1)} %copy-done.58, pred[4,256,256]{2,1,0:T(8,128)(4,1)S(1)} %copy-done.54, ...), kind=kOutput, calls=%fused_computation.15 | convolution fusion | flops 3275440128 | bytes 11075584 | tf_op jit(solution)/shard_map/transpose(jvp(khts,kshp->kthp))/dot_general | solution.py:64
  389.0 9.4 multiply_reduce_fusion.5
  399.8 10.1 reduce-window.49
  427.6 16.0 %bitcast_add_fusion.2 = f32[4,256,16,64]{1,3,2,0:T(8,128)} fusion(f32[4,256,16,64]{1,3,2,0:T(8,128)S(1)} %copy-done.34, f32[4,256,16]{1,2,0:T(8,128)S(1)} %get-tuple-element.345, f32[4,16,256]{2,1,0:T(8,128)S(1)} %bitcast.371, f32[4,256,256]{2,1,0:T(8,128)S(1)} %copy-done.48, f32[4,16,256]{2,1,0:T(8,128)S(1)} %copy-done.59, ...), kind=kOutput, calls=%fused_computation.43 | convolution fusion | flops 3240099840 | bytes 14090240 | tf_op jit(solution)/shard_map/transpose(jvp(khts,kshp->kthp))/dot_general | solution.py:64
  462.3 12.7 multiply_reduce_fusion.10
  512.9 10.9 add_add_fusion
  523.9 11.2 fusion.130
  544.1 10.7 fusion.148
  569.9 245.7 %all-reduce.33.cloned.1.call-done = f32[1024,2048]{1,0:T(8,128)} async-done(((f32[1024,2048]{1,0:T(8,128)}), f32[1024,2048]{1,0:T(8,128)}) %all-reduce.33.cloned.1.call-update) | async-done | bytes 8388624 | tf_op jit(solution)/shard_map/psum | solution.py:288
  823.4 46.4 %all-reduce.28 = (f32[2048]{0:T(1024)}, f32[4096]{0:T(1024)}, f32[4,256]{1,0:T(4,128)}, f32[256]{0:T(256)}, f32[64]{0:T(128)}, /*index=5*/f32[64]{0:T(128)}, f32[64]{0:T(128)}, f32[4096]{0:T(1024)}) all-reduce(f32[2048]{0:T(1024)S(1)} %dynamic-slice_dynamic-update-slice_fusion, ...), channel_id=1, replica_groups=mesh['seq'=8,'head'=4] {'seq','head'}, use_global_device_ids=true, to_apply=%region_32.33 | all-reduce | flops 11712 | bytes 93696 | tf_op jit(solution)/shard_map/psum | solution.py:304
  873.9 88.6 %reduce-scatter.6.cloned.1.call-done = f32[1024,512]{1,0:T(8,128)} async-done(((f32[1024,2048]{1,0:T(8,128)}), f32[1024,512]{1,0:T(8,128)}) %reduce-scatter.6.cloned.1.call-update) | async-done | bytes 2097168 | tf_op jit(solution)/shard_map/reduce_scatter | solution.py:212
  965.4 35.1 %reduce-scatter.12.cloned.1.call-done = f32[256,16]{0,1:T(8,128)} async-done(((f32[2048,16]{0,1:T(8,128)}), f32[256,16]{0,1:T(8,128)}) %reduce-scatter.12.cloned.1.call-update) | async-done | bytes 16400 | tf_op jit(solution)/shard_map/reduce_scatter | solution.py:301
  1000.5 141.0 %all-reduce.35.cloned.1.call-done = (f32[2048,256]{1,0:T(8,128)}, f32[4,4096]{1,0:T(4,128)}) async-done(((f32[2048,256]{1,0:T(8,128)}, f32[4,4096]{1,0:T(4,128)}), (f32[2048,256]{1,0:T(8,128)}, f32[4,4096]{1,0:T(4,128)})) %all-reduce.35.cloned.1.call-update) | async-done | bytes 2162704 | tf_op jit(solution)/shard_map/psum | solution.py:304
  1141.5 74.6 %reduce-scatter.8.cloned.1.call-done = f32[256,1024]{1,0:T(8,128)} async-done(((f32[2048,1024]{1,0:T(8,128)}), f32[256,1024]{1,0:T(8,128)}) %reduce-scatter.8.cloned.1.call-update) | async-done | bytes 1048592 | tf_op jit(solution)/shard_map/reduce_scatter | solution.py:299
  1216.2 75.3 %reduce-scatter.10.cloned.1.call-done = f32[256,1024]{1,0:T(8,128)} async-done(((f32[2048,1024]{1,0:T(8,128)}), f32[256,1024]{1,0:T(8,128)}) %reduce-scatter.10.cloned.1.call-update) | async-done | bytes 1048592 | tf_op jit(solution)/shard_map/reduce_scatter | solution.py:300
  (417 shorter events, 312.3 us)
Async XLA Ops:
  7.2 100.4 %copy-start = (bf16[2048,256]{1,0:T(8,128)(2,1)S(1)}, bf16[2048,256]{1,0:T(8,128)(2,1)}, u32[]{:S(2)}) copy-start(bf16[2048,256]{1,0:T(8,128)(2,1)} %param.29) | copy-start | bytes 3145732
  7.2 84.4 %all-gather.9.cloned.1.call-start = ((), (), s32[]{:S(2)}) async-start(), calls=%async_computation.5 | async-start | bytes 5242880 | tf_op jit(solution)/shard_map/all_gather | solution.py:144
  7.9 168.5 %all-gather.13.cloned.1.call-start = ((), (), s32[]{:S(2)}) async-start(), calls=%async_computation.13 | async-start | bytes 4718592 | tf_op jit(solution)/shard_map/all_gather | solution.py:28
  8.6 115.1 %copy-start.97 = (f32[16]{0:T(128)}, f32[16]{0:T(128)S(1)}, u32[]{:S(2)}) copy-start(f32[16]{0:T(128)S(1)} %exp.51) | copy-start | bytes 196
  26.5 99.1 %copy-start.73 = (f32[1,1024]{1,0:T(1,128)}, f32[1,1024]{1,0:T(1,128)S(1)}, u32[]{:S(2)}) copy-start(f32[1,1024]{1,0:T(1,128)S(1)} %get-tuple-element.346) | copy-start | bytes 12292
  111.2 12.6 collective-permute-start.1
  119.6 6.0 collective-permute-start
  142.1 117.1 %all-gather.11.cloned.1.call-start = ((), (), s32[]{:S(2)}) async-start(), calls=%async_computation.7 | async-start | bytes 5242880 | tf_op jit(solution)/shard_map/all_gather | solution.py:214
  142.8 233.1 %all-gather.15.cloned.1.call-start = ((), (), s32[]{:S(2)}) async-start(), calls=%async_computation.14 | async-start | bytes 4718592 | tf_op jit(solution)/shard_map/all_gather | solution.py:28
  185.9 125.4 %copy-start.27 = (f32[16,64,128]{2,1,0:T(8,128)}, f32[16,64,128]{2,1,0:T(8,128)S(1)}, u32[]{:S(2)}) copy-start(f32[16,64,128]{2,1,0:T(8,128)S(1)} %get-tuple-element.319) | copy-start | bytes 1572868
  305.4 261.9 %reduce-scatter.14.cloned.1.call-start = ((), (), s32[]{:S(2)}) async-start(), calls=%async_computation.12 | async-start | bytes 9437184 | tf_op jit(solution)/shard_map/reduce_scatter | solution.py:302
  375.8 439.8 %all-reduce.33.cloned.1.call-start = ((), (), s32[]{:S(2)}) async-start(), calls=%async_computation.8 | async-start | bytes 16777216 | tf_op jit(solution)/shard_map/psum | solution.py:288
  423.9 79.6 %collective-permute-start.3 = (f32[3,256]{1,0:T(4,128)S(1)}, f32[3,256]{1,0:T(4,128)S(1)}, u32[]{:S(2)}, u32[]{:S(2)}) collective-permute-start(f32[3,256]{1,0:T(4,128)S(1)} %pad_add_fusion.6), channel_id=1, source_target_pairs={{4,0},{8,4},{12,8},{16,12},{20,16},{24,20},{28,24},{5,1},{9,5},{13... | collective-permute-start | bytes 9224 | tf_op jit(solution)/shard_map/ppermute | solution.py:21
  495.9 7.9 collective-permute-start.2
  523.9 438.7 %reduce-scatter.6.cloned.1.call-start = ((), (), s32[]{:S(2)}) async-start(), calls=%async_computation.6 | async-start | bytes 10485760 | tf_op jit(solution)/shard_map/reduce_scatter | solution.py:212
  535.2 465.4 %reduce-scatter.12.cloned.1.call-start = ((), (), s32[]{:S(2)}) async-start(), calls=%async_computation.11 | async-start | bytes 147456 | tf_op jit(solution)/shard_map/reduce_scatter | solution.py:301
  538.9 602.6 %all-reduce.35.cloned.1.call-start = ((), (), s32[]{:S(2)}) async-start(), calls=%async_computation.15 | async-start | bytes 4325376 | tf_op jit(solution)/shard_map/psum | solution.py:304
  544.0 672.2 %reduce-scatter.8.cloned.1.call-start = ((), (), s32[]{:S(2)}) async-start(), calls=%async_computation.9 | async-start | bytes 9437184 | tf_op jit(solution)/shard_map/reduce_scatter | solution.py:299
  554.8 736.7 %reduce-scatter.10.cloned.1.call-start = ((), (), s32[]{:S(2)}) async-start(), calls=%async_computation.10 | async-start | bytes 9437184 | tf_op jit(solution)/shard_map/reduce_scatter | solution.py:300
  565.4 250.2 %copy-start.61 = (f32[4,1,512]{2,1,0:T(1,128)S(1)}, f32[4,1,512]{2,1,0:T(1,128)}, u32[]{:S(2)}) copy-start(f32[4,1,512]{2,1,0:T(1,128)} %copy-done.60) | copy-start | bytes 24580
  565.4 250.2 %copy-start.69 = (f32[1024]{0:T(1024)S(1)}, f32[1024]{0:T(1024)}, u32[]{:S(2)}) copy-start(f32[1024]{0:T(1024)} %copy-done.68) | copy-start | bytes 12292
  569.9 300.0 %copy-start.37 = (bf16[1024,512]{1,0:T(8,128)(2,1)S(1)}, bf16[1024,512]{1,0:T(8,128)(2,1)}, u32[]{:S(2)}) copy-start(bf16[1024,512]{1,0:T(8,128)(2,1)} %param.41) | copy-start | bytes 3145732
  823.3 139.3 %copy-start.38 = (bf16[1024,512]{1,0:T(8,128)(2,1)S(1)}, bf16[1024,512]{1,0:T(8,128)(2,1)}, u32[]{:S(2)}) copy-start(bf16[1024,512]{1,0:T(8,128)(2,1)} %param.25) | copy-start | bytes 3145732
  1141.5 153.0 %copy-start.67 = (f32[4,4096]{1,0:T(4,128)S(1)}, f32[4,4096]{1,0:T(4,128)}, u32[]{:S(2)}) copy-start(f32[4,4096]{1,0:T(4,128)} %get-tuple-element.489) | copy-start | bytes 196612
  (100 other events, 1635.7 us)
Sparse Core Ops, SparseCore 0:
  9.6 81.9 all-gather.8
  142.2 34.1 all-gather.12
  178.0 81.1 all-gather.10
  305.6 36.3 all-gather.14
  375.9 70.9 reduce-scatter.13
  524.0 291.5 all-reduce.32
  818.0 144.4 reduce-scatter.5
  966.4 34.1 reduce-scatter.11
  1006.7 134.7 all-reduce.34
  1145.8 70.3 reduce-scatter.7
  1220.2 71.2 reduce-scatter.9
where the time goes:
time: 1310 us; the launch traced here: 1300 us
  waiting for transfers between devices  731 us (56%)
  matrix products  243 us (19%)
  other arithmetic  118 us (9%)
  blocking collectives  90.6 us (7%)
  local copies, waits for them, and re-layouts  86.9 us (7%)
  between operations  16.2 us (1%)
  starting transfers between devices  15.6 us (1%)
    psum x1, waiting for transfers between devices, shards(): normed_total = lax.psum(normed_cot, 'head')  246 us
    psum x1, waiting for transfers between devices, shards(): lax.psum((control_local, filters_local, baseline_local, embed(prenorm_loc...  141 us
    reduce_scatter x1, waiting for transfers between devices, shards(): lax.psum_scatter(partial_rows, 'head', scatter_dimension=1, tiled=True)  88.6 us
    reduce_scatter x1, waiting for transfers between devices, shards(): lax.psum_scatter(values_local, 'seq', scatter_dimension=0, tiled=True)  75.3 us
    reduce_scatter x1, waiting for transfers between devices, shards(): lax.psum_scatter(gating_local, 'seq', scatter_dimension=0, tiled=True)  74.6 us
    dot_general x3, matrix products, spanned_scan(): jnp.einsum('khts,kshp->kthp', mixing, signal_blocks, precision=highest)  66.2 us
    all_gather x1, waiting for transfers between devices, shards(): lax.all_gather(tokens, 'head', axis=1, tiled=True)  65.1 us
    psum x1, blocking collectives, shards(): lax.psum((control_local, filters_local, baseline_local, embed(prenorm_loc...  46.4 us
  transfers between devices with their start and end apart: 15, of which 9 were waited for; matrix products, arithmetic and copies ran while one was open for 28% of the time, Pallas kernels for 0%

commit v1 on v0

--- a/solution.py
+++ b/solution.py
@@ -12,7 +12,6 @@
 
 
 epsilon = 1e-05
-highest = lax.Precision.HIGHEST
 
 
 def shifted(value, axis, steps):
@@ -21,20 +20,171 @@
     return lax.ppermute(value, axis, [(source, source + steps) for source in range(leading, last)])
 
 
-def prefix_2(part, axis, combine, identity, reverse):
-    count = lax.axis_size(axis)
-    place = lax.axis_index(axis)
-    ahead = count - 1 - place if reverse else place
-    gathered = jax.tree.map(lambda a: lax.all_gather(a, axis), part)
-    state = jax.tree.map(lambda a, e: jnp.zeros_like(a) + jnp.asarray(e, a.dtype), part, identity)
-
-    def one(step, state):
-        source = count - 1 - step if reverse else step
-        return combine(
-            state, jax.tree.map(lambda a: lax.dynamic_index_in_dim(a, source, 0, False), gathered)
+def rotation(count, steps):
+    return [(source, (source + steps) % count) for source in range(count)]
+
+
+def flips(count, bit):
+    return [(source, source ^ (1 << bit)) for source in range(count)]
+
+
+def bits_of(count):
+    return count.bit_length() - 1
+
+
+def gather_blocks(block, axis):
+    count = lax.axis_size(axis)
+    half = count // 2
+    rows = block.shape[0] // 2
+    found = [None] * count
+    found[0] = block
+    left = right = block
+    for step in range(1, half):
+        left = lax.ppermute(left, axis, rotation(count, 1))
+        right = lax.ppermute(right, axis, rotation(count, -1))
+        found[count - step] = left
+        found[step] = right
+    far_low = lax.ppermute(left[:rows], axis, rotation(count, 1))
+    far_high = lax.ppermute(right[rows:], axis, rotation(count, -1))
+    found[half] = jnp.concatenate([far_low, far_high], axis=0)
+    return found
+
+
+def gather_columns(block, axis):
+    count = lax.axis_size(axis)
+    me = lax.axis_index(axis)
+    width = block.shape[1]
+    whole = jnp.zeros((block.shape[0], count * width), block.dtype)
+    for step, piece in enumerate(gather_blocks(block, axis)):
+        whole = lax.dynamic_update_slice_in_dim(whole, piece, (me + step) % count * width, 1)
+    return whole
+
+
+def scatter_columns(whole, axis):
+    count = lax.axis_size(axis)
+    me = lax.axis_index(axis)
+    half = count // 2
+    width = whole.shape[1] // count
+    rows = whole.shape[0] // 2
+
+    def part(step):
+        return lax.dynamic_slice_in_dim(whole, (me + step) % count * width, width, 1)
+
+    far = part(half)
+    ahead = lax.ppermute(far[:rows].astype(jnp.bfloat16), axis, rotation(count, 1))
+    behind = lax.ppermute(far[rows:].astype(jnp.bfloat16), axis, rotation(count, -1))
+    first = True
+    for step in range(half - 1, 0, -1):
+        up = part(step).astype(jnp.float32)
+        down = part(count - step).astype(jnp.float32)
+        if first:
+            up = up.at[:rows].add(ahead.astype(jnp.float32))
+            down = down.at[rows:].add(behind.astype(jnp.float32))
+            first = False
+        else:
+            up = up + ahead.astype(jnp.float32)
+            down = down + behind.astype(jnp.float32)
+        ahead = lax.ppermute(up.astype(jnp.bfloat16), axis, rotation(count, 1))
+        behind = lax.ppermute(down.astype(jnp.bfloat16), axis, rotation(count, -1))
+    return part(0).astype(jnp.float32) + ahead.astype(jnp.float32) + behind.astype(jnp.float32)
+
+
+def small_sum(value, axis):
+    count = lax.axis_size(axis)
+    total = value
+    for step in range(1, count):
+        total = total + lax.ppermute(value, axis, rotation(count, step))
+    return total
+
+
+def doubled_sum(value, axis):
+    count = lax.axis_size(axis)
+    for bit in range(bits_of(count)):
+        value = value + lax.ppermute(value, axis, flips(count, bit))
+    return value
+
+
+def halve(value, axis, bit, position):
+    count = lax.axis_size(axis)
+    mine = (lax.axis_index(axis) >> bit) & 1
+    kept = lax.dynamic_index_in_dim(value, mine, position, False)
+    sent = lax.dynamic_index_in_dim(value, 1 - mine, position, False)
+    return kept + lax.ppermute(sent, axis, flips(count, bit))
+
+
+def scatter_rows(value, axis):
+    count = lax.axis_size(axis)
+    bits = bits_of(count)
+    rows, columns = value.shape
+    split = value.reshape((2,) * bits + (rows // count, columns))
+    split = halve(split, axis, 0, bits - 1)
+    parts = []
+    for piece in range(2):
+        half = split[..., piece * (columns // 2) : (piece + 1) * (columns // 2)]
+        left = list(range(bits - 1, 0, -1))
+        order = list(range(1, bits)) if piece == 0 else list(range(bits - 1, 0, -1))
+        for bit in order:
+            half = halve(half, axis, bit, left.index(bit))
+            left.remove(bit)
+        parts.append(half)
+    return jnp.concatenate(parts, axis=1).astype(jnp.float32)
+
+
+def prefix_state(passing, state, axis, reverse):
+    count = lax.axis_size(axis)
+    me = lax.axis_index(axis)
+    total_pass, total_state = passing, state
+    prefix = jnp.zeros_like(state)
+    prefix_pass = jnp.ones_like(passing)
+    for bit in range(bits_of(count)):
+        other_pass = lax.ppermute(total_pass, axis, flips(count, bit))
+        other_state = lax.ppermute(total_state, axis, flips(count, bit))
+        upper = ((me >> bit) & 1) == 1
+        other_first = jnp.logical_not(upper) if reverse else upper
+        prefix = jnp.where(other_first, prefix_pass[:, None, None] * other_state + prefix, prefix)
+        prefix_pass = jnp.where(other_first, prefix_pass * other_pass, prefix_pass)
+        total_state = jnp.where(
+            other_first,
+            total_pass[:, None, None] * other_state + total_state,
+            other_pass[:, None, None] * total_state + other_state,
         )
-
-    return lax.fori_loop(0, ahead, one, state)
+        total_pass = total_pass * other_pass
+    return prefix
+
+
+def gather_small(value, axis):
+    count = lax.axis_size(axis)
+    me = lax.axis_index(axis)
+    whole = jnp.zeros((count,) + value.shape, value.dtype)
+    for step in range(count):
+        piece = value if step == 0 else lax.ppermute(value, axis, rotation(count, -step))
+        whole = lax.dynamic_update_index_in_dim(whole, piece, (me + step) % count, 0)
+    return whole
+
+
+def sum_everywhere(value):
+    count, heads = lax.axis_size("seq"), lax.axis_size("head")
+    bits = bits_of(count)
+    rows, columns = value.shape
+    split = value.reshape((2,) * bits + (rows // count, columns))
+    for bit in range(bits):
+        split = halve(split, "seq", bit, bits - 1 - bit)
+    blocks = split.reshape(heads, rows // count // heads, columns)
+    me = lax.axis_index("head")
+    total = lax.dynamic_index_in_dim(blocks, me, 0, False)
+    for step in range(1, heads):
+        sent = lax.dynamic_index_in_dim(blocks, (me + step) % heads, 0, False)
+        total = total + lax.ppermute(sent, "head", rotation(heads, step))
+    whole = gather_small(total.astype(jnp.bfloat16), "head").reshape(rows // count, columns)
+    place = lax.axis_index("seq")
+    for bit in range(bits - 1, -1, -1):
+        other = lax.ppermute(whole, "seq", flips(count, bit))
+        upper = ((place >> bit) & 1) == 1
+        low = jnp.where(upper, other, whole)
+        high = jnp.where(upper, whole, other)
+        whole = jnp.stack([low, high])
+    order = list(range(bits - 1, -1, -1)) + [bits, bits + 1]
+    return whole.transpose(order).reshape(rows, columns).astype(jnp.float32)
 
 
 def causal_conv(extended, weights, biases, length):
@@ -59,16 +209,16 @@
     linked = (segment[:, :, None] == segment[:, None, :]) & (places[:, None] >= places[None, :])
     spread = cumulative[:, :, :, None] - cumulative[:, :, None, :]
     decays = jnp.exp(jnp.where(linked[:, None], spread, -1e30))
-    scores = jnp.einsum("ktn,ksn->kts", read_blocks, write_blocks, precision=highest)
+    scores = jnp.einsum("ktn,ksn->kts", read_blocks, write_blocks, precision=lax.Precision.DEFAULT)
     mixing = decays * scores[:, None] * step_blocks[:, :, None, :]
-    within = jnp.einsum("khts,kshp->kthp", mixing, signal_blocks, precision=highest)
+    within = jnp.einsum("khts,kshp->kthp", mixing, signal_blocks, precision=lax.Precision.DEFAULT)
     ending = segment == segment[:, -1:]
     toward = (
         jnp.exp(jnp.where(ending[:, None, :], cumulative[:, :, -1:] - cumulative, -1e30))
         * step_blocks
     )
     produced = jnp.einsum(
-        "khs,kshp,ksn->khpn", toward, signal_blocks, write_blocks, precision=highest
+        "khs,kshp,ksn->khpn", toward, signal_blocks, write_blocks, precision=lax.Precision.DEFAULT
     )
     passing = jnp.exp(cumulative[:, :, -1]) * (segment[:, -1] == 0)[:, None]
     entering = jnp.exp(cumulative) * (segment == 0)[:, None, :]
@@ -78,7 +228,7 @@
         entries.append(current)
         current = passing[position][:, None, None] * current + produced[position]
     carried = jnp.einsum(
-        "khq,kqn,khpn->kqhp", entering, read_blocks, jnp.stack(entries), precision=highest
+        "khq,kqn,khpn->kqhp", entering, read_blocks, jnp.stack(entries), precision=lax.Precision.HIGHEST
     )
     return ((within + carried).reshape(length, head_count * HDIM), current)
 
@@ -106,17 +256,6 @@
     step_size = jax.nn.softplus(timestep_in + timing)
     log_decay = -step_size * jnp.exp(damping)
     return (signal, control_out[:, :STATE], control_out[:, STATE:], step_size, log_decay)
-
-
-def combine(earlier, later):
-    return (earlier[0] * later[0], later[0][:, None, None] * earlier[1] + later[1])
-
-
-def embed(piece, whole_shape, axis_number):
-    begin = lax.axis_index("head") * piece.shape[axis_number]
-    return lax.dynamic_update_slice_in_dim(
-        jnp.zeros(whole_shape, jnp.float32), piece, begin, axis_number
-    )
 
 
 def shards(
@@ -140,10 +279,8 @@
 ):
     contract_last = (((1,), (1,)), ((), ()))
     contract_first = (((0,), (0,)), ((), ()))
-    gathered, gain_full = (
-        lax.all_gather(tokens, "head", axis=1, tiled=True),
-        lax.all_gather(prenorm, "head", axis=0, tiled=True),
-    )
+    gain_full = gather_small(prenorm, "head").reshape(-1)
+    gathered = gather_columns(tokens, "head")
     residual = gathered.astype(jnp.float32)
     scale = lax.rsqrt(jnp.mean(residual * residual, axis=1, keepdims=True) + epsilon)
     unit_rows = residual * scale
@@ -185,10 +322,9 @@
         toward,
         signal.reshape(length, head_count, HDIM),
         writers,
-        precision=highest,
-    )
-    identity = (jnp.ones_like(passing), jnp.zeros_like(produced))
-    prefix = prefix_2((passing, produced), "seq", combine, identity, False)
+        precision=lax.Precision.HIGHEST,
+    )
+    prefix = prefix_state(passing, produced, "seq", False)
 
     def scan_local(signal_in, writers_in, readers_in, step_in, decay_in, incoming):
         return spanned_scan(
@@ -196,29 +332,29 @@
         )
 
     scan_out, scan_back = jax.vjp(
-        scan_local, signal, writers, readers, step_size, log_decay, prefix[1]
+        scan_local, signal, writers, readers, step_size, log_decay, prefix
     )
     skip = jnp.repeat(direct, HDIM)
     full = scan_out[0] + skip * signal
     gate = jax.nn.silu(gate_in)
     gated = full * gate
-    squares = lax.psum(jnp.sum(gated * gated, axis=1), "head")
+    squares = small_sum(jnp.sum(gated * gated, axis=1), "head")
     inverse = lax.rsqrt(squares / INNER + epsilon)[:, None]
     unit_gated = gated * inverse
     normalized = (unit_gated * postnorm).astype(jnp.bfloat16)
     partial_rows = lax.dot_general(
         normalized, readout, contract_last, preferred_element_type=jnp.float32
-    )
-    branch = lax.psum_scatter(partial_rows, "head", scatter_dimension=1, tiled=True)
+    ).astype(jnp.bfloat16)
+    branch = scatter_columns(partial_rows, "head")
     mixed = (tokens.astype(jnp.float32) + branch).astype(jnp.bfloat16)
-    upstream = lax.all_gather(cotangent, "head", axis=1, tiled=True)
+    upstream = gather_columns(cotangent, "head")
     norm_cot = jnp.dot(upstream, readout, preferred_element_type=jnp.float32)
     readout_local = lax.dot_general(
         upstream, normalized, contract_first, preferred_element_type=jnp.float32
     )
     postnorm_local = jnp.sum(norm_cot * unit_gated, axis=0)
     scaled_cot = norm_cot * postnorm
-    inner_sum = lax.psum(jnp.sum(scaled_cot * unit_gated, axis=1), "head")
+    inner_sum = small_sum(jnp.sum(scaled_cot * unit_gated, axis=1), "head")
     gated_cot = inverse * (scaled_cot - unit_gated * (inner_sum / INNER)[:, None])
     full_cot = gated_cot * gate
     sigmoid_gate = jax.nn.sigmoid(gate_in)
@@ -230,11 +366,11 @@
         entering,
         full_cot.reshape(length, head_count, HDIM),
         readers,
-        precision=highest,
-    )
-    suffix = prefix_2((passing, pending), "seq", combine, identity, True)
+        precision=lax.Precision.HIGHEST,
+    )
+    suffix = prefix_state(passing, pending, "seq", True)
     signal_cot, writer_cot, reader_cot, step_cot, decay_cot, ignored = scan_back(
-        (full_cot, suffix[1])
+        (full_cot, suffix)
     )
     signal_cot = signal_cot + skip * full_cot
     back = activate_back((signal_cot, writer_cot, reader_cot, step_cot, decay_cot))
@@ -285,53 +421,56 @@
         normed, timestep_low, contract_first, preferred_element_type=jnp.float32
     )
     share = tokens.shape[1]
-    normed_total = lax.psum(normed_cot, "head")
-    scaled_rows = normed_total * gain_full.astype(jnp.float32)
-    row_mean = jnp.mean(scaled_rows * unit_rows, axis=1, keepdims=True)
-    token_full = scale * (scaled_rows - unit_rows * row_mean)
+    heads = lax.axis_size("head")
     begin = lax.axis_index("head") * share
-    token_local = lax.dynamic_slice_in_dim(token_full, begin, share, 1)
-    prenorm_local = lax.dynamic_slice_in_dim(
-        jnp.sum(normed_total * unit_rows, axis=0), begin, share, 0
-    )
-    tokens_gradient = cotangent.astype(jnp.float32) + token_local
-    gating_gradient, values_gradient, timestep_gradient, readout_gradient = (
-        lax.psum_scatter(gating_local, "seq", scatter_dimension=0, tiled=True),
-        lax.psum_scatter(values_local, "seq", scatter_dimension=0, tiled=True),
-        lax.psum_scatter(timestep_local, "seq", scatter_dimension=0, tiled=True),
-        lax.psum_scatter(readout_local, "seq", scatter_dimension=0, tiled=True),
-    )
-    totals = lax.psum(
-        (
-            control_local,
-            filters_local,
-            baseline_local,
-            embed(prenorm_local, (D,), 0),
-            embed(kernel_local, (kernel.shape[0], INNER), 1),
-            embed(offset_local, (INNER,), 0),
-            embed(timing_local, (HEADS,), 0),
-            embed(damping_local, (HEADS,), 0),
-            embed(direct_local, (HEADS,), 0),
-            embed(postnorm_local, (INNER,), 0),
-        ),
-        ("seq", "head"),
-    )
+    unit_gain = gain_full.astype(jnp.float32)
+    cot_units = normed_cot * unit_rows
+    prenorm_local = jnp.sum(cot_units, axis=0)
+    row_mean = small_sum(jnp.sum(cot_units * unit_gain, axis=1), "head") / D
+    own_total = scatter_columns(normed_cot.astype(jnp.bfloat16), "head")
+    own_units = tokens.astype(jnp.float32) * scale
+    tokens_gradient = cotangent.astype(jnp.float32) + scale * (
+        own_total * prenorm.astype(jnp.float32) - own_units * row_mean[:, None]
+    )
+    gating_gradient, values_gradient, readout_gradient = (
+        scatter_rows(gating_local.astype(jnp.bfloat16), "seq"),
+        scatter_rows(values_local.astype(jnp.bfloat16), "seq"),
+        scatter_rows(readout_local.astype(jnp.bfloat16), "seq"),
+    )
+    timestep_gradient = scatter_rows(timestep_local, "seq")
+    control_gradient = sum_everywhere(control_local)
+    everywhere = (filters_local, baseline_local, prenorm_local)
+    split = (kernel_local, offset_local, timing_local, damping_local, direct_local, postnorm_local)
+    flat_every = jnp.concatenate([item.reshape(-1) for item in everywhere])
+    flat_split = jnp.concatenate([item.reshape(-1) for item in split])
+    flat = doubled_sum(jnp.concatenate([flat_every, flat_split]), "seq")
+    blocks = gather_small(flat, "head")
+    summed = jnp.sum(blocks[:, : flat_every.shape[0]], axis=0)
+    totals = []
+    place = 0
+    for item in everywhere:
+        totals.append(summed[place : place + item.size].reshape(item.shape))
+        place += item.size
+    for item in split:
+        piece = blocks[:, place : place + item.size].reshape((heads,) + item.shape)
+        totals.append(jnp.moveaxis(piece, 0, -2).reshape(item.shape[:-1] + (-1,)))
+        place += item.size
     return (
         mixed,
         tokens_gradient,
-        totals[3],
+        totals[2],
         gating_gradient,
         values_gradient,
+        control_gradient,
+        timestep_gradient,
+        totals[3],
+        totals[4],
         totals[0],
-        timestep_gradient,
-        totals[4],
+        totals[1],
         totals[5],
-        totals[1],
-        totals[2],
         totals[6],
         totals[7],
         totals[8],
-        totals[9],
         readout_gradient,
     )
 

time: 1310 us -> 793 us (0.61)
  waiting for transfers between devices: 731 us -> 256 us
  blocking collectives: 90.6 us -> 0 us
  matrix products: 243 us -> 157 us
  starting transfers between devices: 15.6 us -> 101 us
  local copies, waits for them, and re-layouts: 86.9 us -> 126 us
  other arithmetic: 118 us -> 137 us
    psum x2 -> x0, waiting for transfers between devices: 387 us -> none  [the longest x1 246 us: shards(): normed_total = lax.psum(normed_cot, 'head')]
    reduce_scatter x5 -> x0, waiting for transfers between devices: 274 us -> none  [the longest x1 88.6 us: shards(): lax.psum_scatter(partial_rows, 'head', scatter_dimension=1, tiled=True)]
    ppermute x0 -> x74, waiting for transfers between devices: none -> 256 us  [the longest x9 104 us: gather_small(): lax.ppermute(value, axis, rotation(count, -step))]
    ppermute x0 -> x74, starting transfers between devices: none -> 90 us  [the longest x23 20.1 us: halve(): return kept + lax.ppermute(sent, axis, flips(count, bit))]
    psum x3 -> x0, blocking collectives: 69.4 us -> none  [the longest x1 46.4 us: shards(): lax.psum((control_local, filters_local, baseline_local, embed(prenorm_loc...]
    all_gather x4 -> x0, waiting for transfers between devices: 69.1 us -> none  [the longest x1 65.1 us: shards(): lax.all_gather(tokens, 'head', axis=1, tiled=True)]
    dot_general x6, matrix products: 71.9 us -> 30.5 us  [the longest x3 26.6 us: spanned_scan(): jnp.einsum('khts,kshp->kthp', mixing, signal_blocks, precision=lax.Precis...]
    all_gather x2 -> x0, blocking collectives: 21.2 us -> none  [the longest x1 12.2 us: shards(): lax.all_gather(prenorm, 'head', axis=0, tiled=True)]
  transfers between devices with their start and end apart: 15 -> 78, of which waited for: 9 -> 31; matrix products, arithmetic and copies ran while one was open for 28% -> 45% of each run, Pallas kernels for 0% -> 0%
where the time goes in v1:
time: 793 us; the launch traced here: 781 us
  waiting for transfers between devices  256 us (32%)
  matrix products  157 us (20%)
  other arithmetic  137 us (17%)
  local copies, waits for them, and re-layouts  126 us (16%)
  starting transfers between devices  101 us (13%)
    ppermute x9, waiting for transfers between devices, gather_small(): lax.ppermute(value, axis, rotation(count, -step))  104 us
    ppermute x23, waiting for transfers between devices, halve(): return kept + lax.ppermute(sent, axis, flips(count, bit))  45.8 us
    ppermute x2, waiting for transfers between devices, gather_blocks(): left = lax.ppermute(left, axis, rotation(count, 1))  28.6 us
    dot_general x3, matrix products, spanned_scan(): jnp.einsum('khts,kshp->kthp', mixing, signal_blocks, precision=lax.Precis...  26.6 us
    ppermute x3, waiting for transfers between devices, sum_everywhere(): total = total + lax.ppermute(sent, 'head', rotation(heads, step))  22.3 us
    reshape x3, local copies, waits for them, and re-layouts, spanned_scan(): return ((within + carried).reshape(length, head_count * HDIM), current)  21.7 us
    reshape x3, local copies, waits for them, and re-layouts, spanned_scan(): signal_blocks = signal.reshape(blocks, SPAN, head_count, HDIM)  21.5 us
    another operation x12, other arithmetic  20.2 us
  transfers between devices with their start and end apart: 78, of which 31 were waited for; matrix products, arithmetic and copies ran while one was open for 45% of the time, Pallas kernels for 0%

profile of v1, /device:TPU:4, one launch (start us, length us, event | category | flops | bytes accessed | tf_op | source)
XLA Modules:
  0.0 781.4 jit_solution(17256109268106213473)
XLA Ops:
  23.0 28.6 %collective-permute-done.1 = bf16[1024,512]{1,0:T(8,128)(2,1)} collective-permute-done((bf16[1024,512]{1,0:T(8,128)(2,1)}, bf16[1024,512]{1,0:T(8,128)(2,1)}, u32[]{:S(2)}, u32[]{:S(2)}) %collective-permute-start.1) | collective-permute-done | bytes 1048608 | tf_op jit(solution)/shard_map/ppermute | solution.py:43
  63.5 32.1 %collective-permute-done.4 = bf16[512]{0:T(512)(128)(2,1)S(1)} collective-permute-done((bf16[512]{0:T(512)(128)(2,1)}, bf16[512]{0:T(512)(128)(2,1)S(1)}, u32[]{:S(2)}, u32[]{:S(2)}) %collective-permute-start.4) | collective-permute-done | bytes 1056 | tf_op jit(solution)/shard_map/ppermute | solution.py:160
  97.8 19.3 %collective-permute-done.5 = bf16[512]{0:T(512)(128)(2,1)S(1)} collective-permute-done((bf16[512]{0:T(512)(128)(2,1)S(1)}, bf16[512]{0:T(512)(128)(2,1)S(1)}, u32[]{:S(2)}, u32[]{:S(2)}) %collective-permute-start.5) | collective-permute-done | bytes 1056 | tf_op jit(solution)/shard_map/ppermute | solution.py:160
  170.7 9.7 %fusion.39 = (f32[1024,1024]{1,0:T(8,128)}, f32[1024,1024]{1,0:T(8,128)}) fusion(f32[1024,1024]{1,0:T(8,128)} %copy-done.16, f32[1024]{0:T(1024)S(1)} %bitcast.544, f32[3,1024]{1,0:T(4,128)S(1)} %collective-permute-done.7, f32[1024]{0:T(1024)S(1)} %bitcast.546, f32[1024]{0:T(1024)S(1)} %bitcast.542, f32[1024]{0:T(1024)S(1)} %bitcast.540, f32[1024]{0:T(1024)S(1)} %copy-done.135), kind=kLoop, calls=%fused_computation.69 | loop fusion | flops 15728640 | bytes 12615680 | tf_op jit(solution)/shard_map/jvp(jit(silu))/mul | solution.py:250
  199.3 9.2 %collective-permute-done.10 = f32[16]{0:T(128)S(1)} collective-permute-done((f32[16]{0:T(128)S(1)}, f32[16]{0:T(128)S(1)}, u32[]{:S(2)}, u32[]{:S(2)}) %collective-permute-start.10) | collective-permute-done | bytes 96 | tf_op jit(solution)/shard_map/ppermute | solution.py:140
  237.2 8.1 %copy.251 = f32[4,256,16,64]{3,2,1,0:T(8,128)} copy(f32[4,256,16,64]{1,3,2,0:T(8,128)} %fusion.33) | data formatting | bytes 8388608 | tf_op jit(solution)/shard_map/jvp()/reshape | solution.py:233
  253.1 11.4 %multiply_reduce_fusion.12 = (f32[1024]{0:T(1024)S(1)}, f32[1024,1024]{1,0:T(8,128)S(1)}, f32[1024,1024]{1,0:T(8,128)S(1)}) fusion(f32[1024,1024]{1,0:T(8,128)} %reshape.635, f32[1024,1024]{1,0:T(8,128)} %get-tuple-element.134, f32[1024]{0:T(1024)S(1)} %mul.742, bf16[1024,2048]{1,0:T(8,128)(2,1)} %copy-done.9, bf16[2048,1024]{1,0:T(8,128)(2,1)} %param.31), kind=kOutput, calls=%fused_computation.62 | convolution fusion | flops 4308597760 | bytes 25174016 | tf_op jit(solution)/shard_map/dot_general | solution.py:288
  278.1 9.0 %multiply_reduce_fusion.5 = (f32[1024]{0:T(1024)}, f32[1024]{0:T(1024)S(1)}, f32[1024,1024]{1,0:T(8,128)S(1)}) fusion(f32[1024,1024]{1,0:T(8,128)S(1)} %get-tuple-element.126, f32[1024]{0:T(1024)S(1)} %add_rsqrt_fusion, f32[1024]{0:T(1024)S(1)} %copy-done.136, bf16[1024,2048]{1,0:T(8,128)(2,1)} %constant_dynamic-update-slice_fusion, ...), kind=kOutput, calls=%fused_computation.50 | convolution fusion | flops 4301256704 | bytes 16793600 | tf_op jit(solution)/shard_map/dot_general | solution.py:351
  292.1 8.9 %convolution_convert_fusion.3 = bf16[1024,2048]{1,0:T(8,128)(2,1)} fusion(bf16[2048,1024]{1,0:T(8,128)(2,1)} %param.43, f32[1024,1024]{1,0:T(8,128)S(1)} %get-tuple-element.126, f32[1024]{0:T(1024)S(1)} %copy-done.136, f32[1024]{0:T(1024)S(1)} %add_rsqrt_fusion), kind=kOutput, calls=%fused_computation.81 | convolution fusion | flops 4300210176 | bytes 12591104 | tf_op jit(solution)/shard_map/dot_general | solution.py:345
  316.8 9.1 %fusion.170 = f32[1024,2048]{1,0:T(8,128)} fusion(bf16[1024,1024]{1,0:T(8,128)(2,1)S(1)} %get-tuple-element.137, bf16[2048,1024]{1,0:T(8,128)(2,1)} %param.31), kind=kOutput, calls=%fused_computation.386 | convolution fusion | flops 4294967296 | bytes 14680064 | tf_op jit(solution)/shard_map/dot_general | solution.py:399
  350.2 9.0 %fusion.75 = f32[4,256,128]{2,1,0:T(8,128)} fusion(f32[4,256,16,64]{1,0,3,2:T(4,128)S(1)} %copy-done.14, f32[4,256,16]{1,2,0:T(8,128)S(1)} %get-tuple-element.188, f32[1,16,64,128]{3,2,1,0:T(8,128)} %copy-done.59, f32[1,16,64,128]{3,2,1,0:T(8,128)S(1)} %bitcast.491, f32[1,16,64,128]{3,2,1,0:T(8,128)S(1)} %bitcast.493, f32[1,16,64,128]{3,2,1,0:T(8,128)} %bitcast.495), kind=kOutput, calls=%fused_computation.119 | convolution fusion | flops 1613234176 | bytes 6881280 | tf_op jit(solution)/shard_map/transpose(jvp(khq,kqn,khpn->kqhp))/dot_general | solution.py:230
  359.3 14.1 %fusion.9 = (f32[4,16,256]{2,1,0:T(8,128)}, f32[4,16,256]{2,1,0:T(8,128)}, f32[4,16,256]{2,1,0:T(8,128)}, bf16[4,256,256]{2,1,0:T(8,128)(2,1)}) fusion(f32[4,16,256]{2,1,0:T(8,128)S(1)} %bitcast.535, f32[4,256,256]{2,1,0:T(8,128)S(1)} %copy-done.67, f32[4,16,256]{2,1,0:T(8,128)S(1)} %copy-done.79, pred[4,256,256]{2,1,0:T(8,128)(4,1)S(1)} %copy-done.75, ...), kind=kOutput, calls=%fused_computation.13 | convolution fusion | flops 591085568 | bytes 10551296 | tf_op jit(solution)/shard_map/transpose(jvp(khts,kshp->kthp))/dot_general | solution.py:214
  392.6 8.3 %collective-permute-done.29 = f32[16,64,128]{2,1,0:T(8,128)S(1)} collective-permute-done((f32[16,64,128]{2,1,0:T(8,128)S(1)}, f32[16,64,128]{2,1,0:T(8,128)S(1)}, u32[]{:S(2)}, u32[]{:S(2)}) %collective-permute-start.29) | collective-permute-done | bytes 524320 | tf_op jit(solution)/shard_map/ppermute | solution.py:141
  427.3 8.1 %copy.252 = f32[4,256,16,64]{3,2,1,0:T(8,128)} copy(f32[4,256,16,64]{1,3,2,0:T(8,128)} %bitcast_add_fusion) | data formatting | bytes 8388608 | tf_op jit(solution)/shard_map/transpose(jvp())/reshape | solution.py:202
  443.0 14.1 %multiply_reduce_fusion.9 = (f32[1024]{0:T(1024)}, f32[1024]{0:T(1024)}, f32[1024]{0:T(1024)}, f32[1024]{0:T(1024)}, f32[1024]{0:T(1024)}, /*index=5*/f32[1024,1024]{1,0:T(8,128)}) fusion(f32[1024,1024]{1,0:T(8,128)} %copy-done.16, f32[3,1024]{1,0:T(4,128)S(1)} %copy-done.88, f32[1024,1024]{1,0:T(8,128)} %get-tuple-element.134, f32[1024,1024]{1,0:T(8,128)} %reshape.636, ...), kind=kLoop, calls=%fused_computation.54 | loop fusion | flops 24112128 | bytes 21008384 | tf_op jit(solution)/shard_map/transpose(jvp())/reduce_sum | solution.py:193
  488.1 9.9 %reduce-window.49 = f32[4,16,2,128]{3,1,2,0:T(8,128)S(1)} reduce-window(f32[4,16,2,128]{3,1,2,0:T(8,128)S(1)} %bitcast.528, f32[]{:T(128)} %constant.445.clone.1), window={size=1x1x1x128 pad=0_0x0_0x0_0x0_127}, to_apply=%region_20.21 | reduce-window | flops 2080768 | bytes 131076 | tf_op jit(solution)/shard_map/reduce-window.8
  533.1 7.9 %convolution_convert_fusion.1 = bf16[2048,1024]{1,0:T(8,128)(2,1)} fusion(bf16[1024,2048]{1,0:T(8,128)(2,1)S(1)} %copy-done.12, bf16[1024,1024]{1,0:T(8,128)(2,1)} %scatter-add.24), kind=kOutput, calls=%fused_computation.79 | convolution fusion | flops 4297064448 | bytes 10485760 | tf_op jit(solution)/shard_map/dot_general | solution.py:414
  541.0 8.8 %fusion.24 = (f32[2048]{0:T(1024)S(1)}, f32[1024]{0:T(1024)S(1)}, bf16[1024,2048]{1,0:T(8,128)(2,1)S(1)}) fusion(bf16[1024,2048]{1,0:T(8,128)(2,1)} %constant_dynamic-update-slice_fusion.3, f32[1024]{0:T(1024)S(1)} %copy-done.90, f32[2048]{0:T(1024)S(1)} %bitcast.531, f32[1024,2048]{1,0:T(8,128)} %fusion.127, bf16[1024,256]{1,0:T(8,128)(2,1)S(1)} %copy-done.51, ...), kind=kOutput, calls=%fused_computation.33 | convolution fusion | flops 1094710272 | bytes 35151872 | tf_op jit(solution)/shard_map/dot_general | solution.py:405
  612.2 9.2 %collective-permute-done.47 = bf16[2,256,512]{2,1,0:T(8,128)(2,1)S(1)} collective-permute-done((bf16[2,256,512]{2,1,0:T(8,128)(2,1)S(1)}, bf16[2,256,512]{2,1,0:T(8,128)(2,1)S(1)}, u32[]{:S(2)}, u32[]{:S(2)}) %collective-permute-start.47) | collective-permute-done | bytes 524320 | tf_op jit(solution)/shard_map/ppermute | solution.py:112
  630.5 11.3 %collective-permute-done.57 = f32[2,256,256]{2,1,0:T(8,128)S(1)} collective-permute-done((f32[2,256,256]{2,1,0:T(8,128)S(1)}, f32[2,256,256]{2,1,0:T(8,128)S(1)}, u32[]{:S(2)}, u32[]{:S(2)}) %collective-permute-start.57) | collective-permute-done | bytes 524320 | tf_op jit(solution)/shard_map/ppermute | solution.py:112
  655.4 19.1 %collective-permute-done.60 = f32[64,256]{1,0:T(8,128)S(1)} collective-permute-done((f32[64,256]{1,0:T(8,128)S(1)}, f32[64,256]{1,0:T(8,128)S(1)}, u32[]{:S(2)}, u32[]{:S(2)}) %collective-permute-start.60) | collective-permute-done | bytes 65568 | tf_op jit(solution)/shard_map/ppermute | solution.py:177
  678.7 41.4 %collective-permute-done.62 = bf16[64,256]{1,0:T(8,128)(2,1)S(1)} collective-permute-done((bf16[64,256]{1,0:T(8,128)(2,1)S(1)}, bf16[64,256]{1,0:T(8,128)(2,1)S(1)}, u32[]{:S(2)}, u32[]{:S(2)}) %collective-permute-start.62) | collective-permute-done | bytes 32800 | tf_op jit(solution)/shard_map/ppermute | solution.py:160
  742.3 15.2 %collective-permute-done.36 = bf16[1024,512]{1,0:T(8,128)(2,1)S(1)} collective-permute-done((bf16[1024,512]{1,0:T(8,128)(2,1)S(1)}, bf16[1024,512]{1,0:T(8,128)(2,1)S(1)}, u32[]{:S(2)}, u32[]{:S(2)}) %collective-permute-start.36) | collective-permute-done | bytes 1048608 | tf_op jit(solution)/shard_map/ppermute | solution.py:88
  764.0 9.6 %collective-permute-done.54 = bf16[2,256,512]{2,1,0:T(8,128)(2,1)S(1)} collective-permute-done((bf16[2,256,512]{2,1,0:T(8,128)(2,1)S(1)}, bf16[2,256,512]{2,1,0:T(8,128)(2,1)S(1)}, u32[]{:S(2)}, u32[]{:S(2)}) %collective-permute-start.54) | collective-permute-done | bytes 524320 | tf_op jit(solution)/shard_map/ppermute | solution.py:112
  (748 shorter events, 445.9 us)
Async XLA Ops:
  0.7 54.4 %collective-permute-start = (bf16[1024,512]{1,0:T(8,128)(2,1)}, bf16[1024,512]{1,0:T(8,128)(2,1)}, u32[]{:S(2)}, u32[]{:S(2)}) collective-permute-start(bf16[1024,512]{1,0:T(8,128)(2,1)} %param.29), channel_id=1, source_target_pairs={{0,3},{1,0},{2,1},{3,2},{4,7},{5,4},{6,5},{7,6},{8,11},{9,8},{10,9... | collective-permute-start | bytes 3145736 | tf_op jit(solution)/shard_map/ppermute | solution.py:44
  4.3 47.3 %collective-permute-start.1 = (bf16[1024,512]{1,0:T(8,128)(2,1)}, bf16[1024,512]{1,0:T(8,128)(2,1)}, u32[]{:S(2)}, u32[]{:S(2)}) collective-permute-start(bf16[1024,512]{1,0:T(8,128)(2,1)} %param.29), channel_id=1, source_target_pairs={{0,1},{1,2},{2,3},{3,0},{4,5},{5,6},{6,7},{7,4},{8,9},{9,10},{10,1... | collective-permute-start | bytes 3145736 | tf_op jit(solution)/shard_map/ppermute | solution.py:43
  4.3 120.1 %collective-permute-start.21 = (bf16[1024,512]{1,0:T(8,128)(2,1)}, bf16[1024,512]{1,0:T(8,128)(2,1)}, u32[]{:S(2)}, u32[]{:S(2)}) collective-permute-start(bf16[1024,512]{1,0:T(8,128)(2,1)} %param.45), channel_id=1, source_target_pairs={{0,3},{1,0},{2,1},{3,2},{4,7},{5,4},{6,5},{7,6},{8,11},{9,8},{10,9... | collective-permute-start | bytes 3145736 | tf_op jit(solution)/shard_map/ppermute | solution.py:44
  8.2 114.4 %collective-permute-start.22 = (bf16[1024,512]{1,0:T(8,128)(2,1)}, bf16[1024,512]{1,0:T(8,128)(2,1)}, u32[]{:S(2)}, u32[]{:S(2)}) collective-permute-start(bf16[1024,512]{1,0:T(8,128)(2,1)} %param.45), channel_id=1, source_target_pairs={{0,1},{1,2},{2,3},{3,0},{4,5},{5,6},{6,7},{7,4},{8,9},{9,10},{10,1... | collective-permute-start | bytes 3145736 | tf_op jit(solution)/shard_map/ppermute | solution.py:43
  8.2 87.5 %collective-permute-start.4 = (bf16[512]{0:T(512)(128)(2,1)}, bf16[512]{0:T(512)(128)(2,1)S(1)}, u32[]{:S(2)}, u32[]{:S(2)}) collective-permute-start(bf16[512]{0:T(512)(128)(2,1)} %param.30), channel_id=1, source_target_pairs={{0,3},{1,0},{2,1},{3,2},{4,7},{5,4},{6,5},{7,6},{8,11},{9,8},{10,9... | collective-permute-start | bytes 3080 | tf_op jit(solution)/shard_map/ppermute | solution.py:160
  53.5 81.2 %collective-permute-start.2 = (bf16[512,512]{1,0:T(8,128)(2,1)}, bf16[512,512]{1,0:T(8,128)(2,1)S(1)}, u32[]{:S(2)}, u32[]{:S(2)}) collective-permute-start(bf16[512,512]{1,0:T(8,128)(2,1)} %slice.398), channel_id=1, source_target_pairs={{0,1},{1,2},{2,3},{3,0},{4,5},{5,6},{6,7},{7,4},{8,9},{9,10},{10,1... | collective-permute-start | bytes 1572872 | tf_op jit(solution)/shard_map/ppermute | solution.py:47
  56.9 77.8 %collective-permute-start.3 = (bf16[512,512]{1,0:T(8,128)(2,1)}, bf16[512,512]{1,0:T(8,128)(2,1)S(1)}, u32[]{:S(2)}, u32[]{:S(2)}) collective-permute-start(bf16[512,512]{1,0:T(8,128)(2,1)} %slice.399), channel_id=1, source_target_pairs={{0,3},{1,0},{2,1},{3,2},{4,7},{5,4},{6,5},{7,6},{8,11},{9,8},{10,9... | collective-permute-start | bytes 1572872 | tf_op jit(solution)/shard_map/ppermute | solution.py:48
  124.4 69.9 %collective-permute-start.23 = (bf16[512,512]{1,0:T(8,128)(2,1)}, bf16[512,512]{1,0:T(8,128)(2,1)}, u32[]{:S(2)}, u32[]{:S(2)}) collective-permute-start(bf16[512,512]{1,0:T(8,128)(2,1)} %slice.426), channel_id=1, source_target_pairs={{0,1},{1,2},{2,3},{3,0},{4,5},{5,6},{6,7},{7,4},{8,9},{9,10},{10,1... | collective-permute-start | bytes 1572872 | tf_op jit(solution)/shard_map/ppermute | solution.py:47
  126.3 68.1 %collective-permute-start.24 = (bf16[512,512]{1,0:T(8,128)(2,1)}, bf16[512,512]{1,0:T(8,128)(2,1)}, u32[]{:S(2)}, u32[]{:S(2)}) collective-permute-start(bf16[512,512]{1,0:T(8,128)(2,1)} %slice.427), channel_id=1, source_target_pairs={{0,3},{1,0},{2,1},{3,2},{4,7},{5,4},{6,5},{7,6},{8,11},{9,8},{10,9... | collective-permute-start | bytes 1572872 | tf_op jit(solution)/shard_map/ppermute | solution.py:48
  163.0 29.5 %collective-permute-start.9 = (f32[16]{0:T(128)S(1)}, f32[16]{0:T(128)S(1)}, u32[]{:S(2)}, u32[]{:S(2)}) collective-permute-start(f32[16]{0:T(128)S(1)} %exponential_multiply_fusion.3), channel_id=1, source_target_pairs={{0,4},{4,0},{8,12},{12,8},{16,20},{20,16},{24,28},{28,24},{1,5},{5... | collective-permute-start | bytes 200 | tf_op jit(solution)/shard_map/ppermute | solution.py:140
  302.7 284.0 %collective-permute-start.73 = (bf16[2,2,256,1024]{3,2,1,0:T(8,128)(2,1)}, bf16[2,2,256,1024]{3,2,1,0:T(8,128)(2,1)}, u32[]{:S(2)}, u32[]{:S(2)}) collective-permute-start(bf16[2,2,256,1024]{3,2,1,0:T(8,128)(2,1)} %dynamic-slice_bitcast_fusion), channel_id=1, source_target_pairs={{0,4},{4,0},{8,12},{12,8},{16,20},{20,16},{24,28},{28,24},{1,5},{5... | collective-permute-start | bytes 6291464 | tf_op jit(solution)/shard_map/ppermute | solution.py:112
  306.9 94.7 %collective-permute-start.17 = (bf16[512,512]{1,0:T(8,128)(2,1)}, bf16[512,512]{1,0:T(8,128)(2,1)}, u32[]{:S(2)}, u32[]{:S(2)}) collective-permute-start(bf16[512,512]{1,0:T(8,128)(2,1)} %get-tuple-element.147), channel_id=1, source_target_pairs={{0,1},{1,2},{2,3},{3,0},{4,5},{5,6},{6,7},{7,4},{8,9},{9,10},{10,1... | collective-permute-start | bytes 1572872 | tf_op jit(solution)/shard_map/ppermute | solution.py:74
  307.6 96.5 %collective-permute-start.19 = (bf16[512,512]{1,0:T(8,128)(2,1)}, bf16[512,512]{1,0:T(8,128)(2,1)}, u32[]{:S(2)}, u32[]{:S(2)}) collective-permute-start(bf16[512,512]{1,0:T(8,128)(2,1)} %get-tuple-element.148), channel_id=1, source_target_pairs={{0,3},{1,0},{2,1},{3,2},{4,7},{5,4},{6,5},{7,6},{8,11},{9,8},{10,9... | collective-permute-start | bytes 1572872 | tf_op jit(solution)/shard_map/ppermute | solution.py:75
  350.1 35.1 %collective-permute-start.28 = (f32[16,64,128]{2,1,0:T(8,128)}, f32[16,64,128]{2,1,0:T(8,128)}, u32[]{:S(2)}, u32[]{:S(2)}) collective-permute-start(f32[16,64,128]{2,1,0:T(8,128)} %fusion.34), channel_id=1, source_target_pairs={{0,4},{4,0},{8,12},{12,8},{16,20},{20,16},{24,28},{28,24},{1,5},{5... | collective-permute-start | bytes 1572872 | tf_op jit(solution)/shard_map/ppermute | solution.py:141
  377.3 215.9 %collective-permute-start.46 = (bf16[2,2,256,1024]{3,2,1,0:T(8,128)(2,1)}, bf16[2,2,256,1024]{3,2,1,0:T(8,128)(2,1)}, u32[]{:S(2)}, u32[]{:S(2)}) collective-permute-start(bf16[2,2,256,1024]{3,2,1,0:T(8,128)(2,1)} %dynamic-slice_bitcast_fusion.2), channel_id=1, source_target_pairs={{0,4},{4,0},{8,12},{12,8},{16,20},{20,16},{24,28},{28,24},{1,5},{5... | collective-permute-start | bytes 6291464 | tf_op jit(solution)/shard_map/ppermute | solution.py:112
  577.6 45.3 %collective-permute-start.56 = (f32[2,2,256,256]{3,2,1,0:T(8,128)}, f32[2,2,256,256]{3,2,1,0:T(8,128)}, u32[]{:S(2)}, u32[]{:S(2)}) collective-permute-start(f32[2,2,256,256]{3,2,1,0:T(8,128)} %dynamic-slice_bitcast_fusion.3), channel_id=1, source_target_pairs={{0,4},{4,0},{8,12},{12,8},{16,20},{20,16},{24,28},{28,24},{1,5},{5... | collective-permute-start | bytes 3145736 | tf_op jit(solution)/shard_map/ppermute | solution.py:112
  578.8 159.3 %collective-permute-start.51 = (bf16[2,2,256,1024]{3,2,1,0:T(8,128)(2,1)}, bf16[2,2,256,1024]{3,2,1,0:T(8,128)(2,1)}, u32[]{:S(2)}, u32[]{:S(2)}) collective-permute-start(bf16[2,2,256,1024]{3,2,1,0:T(8,128)(2,1)} %dynamic-slice_bitcast_fusion.1), channel_id=1, source_target_pairs={{0,4},{4,0},{8,12},{12,8},{16,20},{20,16},{24,28},{28,24},{1,5},{5... | collective-permute-start | bytes 6291464 | tf_op jit(solution)/shard_map/ppermute | solution.py:112
  622.9 26.2 %collective-permute-start.48 = (bf16[256,512]{1,0:T(8,128)(2,1)S(1)}, bf16[256,512]{1,0:T(8,128)(2,1)S(1)}, u32[]{:S(2)}, u32[]{:S(2)}) collective-permute-start(bf16[256,512]{1,0:T(8,128)(2,1)S(1)} %dynamic-slice_bitcast_fusion.17), channel_id=1, source_target_pairs={{0,16},{4,20},{8,24},{12,28},{16,0},{20,4},{24,8},{28,12},{1,17},{... | collective-permute-start | bytes 786440 | tf_op jit(solution)/shard_map/ppermute | solution.py:112
  629.9 47.9 %collective-permute-start.50 = (bf16[256,512]{1,0:T(8,128)(2,1)S(1)}, bf16[256,512]{1,0:T(8,128)(2,1)S(1)}, u32[]{:S(2)}, u32[]{:S(2)}) collective-permute-start(bf16[256,512]{1,0:T(8,128)(2,1)S(1)} %dynamic-slice_bitcast_fusion.16), channel_id=1, source_target_pairs={{0,8},{4,12},{8,0},{12,4},{16,24},{20,28},{24,16},{28,20},{1,9},{5... | collective-permute-start | bytes 786440 | tf_op jit(solution)/shard_map/ppermute | solution.py:112
  649.1 25.6 %collective-permute-start.61 = (f32[64,256]{1,0:T(8,128)S(1)}, f32[64,256]{1,0:T(8,128)S(1)}, u32[]{:S(2)}, u32[]{:S(2)}) collective-permute-start(f32[64,256]{1,0:T(8,128)S(1)} %get-tuple-element.170), channel_id=1, source_target_pairs={{0,3},{1,0},{2,1},{3,2},{4,7},{5,4},{6,5},{7,6},{8,11},{9,8},{10,9... | collective-permute-start | bytes 196616 | tf_op jit(solution)/shard_map/ppermute | solution.py:177
  655.4 86.3 %collective-permute-start.18 = (bf16[1024,512]{1,0:T(8,128)(2,1)S(1)}, bf16[1024,512]{1,0:T(8,128)(2,1)S(1)}, u32[]{:S(2)}, u32[]{:S(2)}) collective-permute-start(bf16[1024,512]{1,0:T(8,128)(2,1)S(1)} %copy-done.64), channel_id=1, source_target_pairs={{0,1},{1,2},{2,3},{3,0},{4,5},{5,6},{6,7},{7,4},{8,9},{9,10},{10,1... | collective-permute-start | bytes 3145736 | tf_op jit(solution)/shard_map/ppermute | solution.py:87
  674.4 67.9 %collective-permute-start.20 = (bf16[1024,512]{1,0:T(8,128)(2,1)S(1)}, bf16[1024,512]{1,0:T(8,128)(2,1)S(1)}, u32[]{:S(2)}, u32[]{:S(2)}) collective-permute-start(bf16[1024,512]{1,0:T(8,128)(2,1)S(1)} %copy-done.65), channel_id=1, source_target_pairs={{0,3},{1,0},{2,1},{3,2},{4,7},{5,4},{6,5},{7,6},{8,11},{9,8},{10,9... | collective-permute-start | bytes 3145736 | tf_op jit(solution)/shard_map/ppermute | solution.py:88
  674.7 67.6 %collective-permute-start.34 = (bf16[1024,512]{1,0:T(8,128)(2,1)S(1)}, bf16[1024,512]{1,0:T(8,128)(2,1)S(1)}, u32[]{:S(2)}, u32[]{:S(2)}) collective-permute-start(bf16[1024,512]{1,0:T(8,128)(2,1)S(1)} %convert_element_type.186), channel_id=1, source_target_pairs={{0,1},{1,2},{2,3},{3,0},{4,5},{5,6},{6,7},{7,4},{8,9},{9,10},{10,1... | collective-permute-start | bytes 3145736 | tf_op jit(solution)/shard_map/ppermute | solution.py:87
  677.9 42.2 %collective-permute-start.62 = (bf16[64,256]{1,0:T(8,128)(2,1)S(1)}, bf16[64,256]{1,0:T(8,128)(2,1)S(1)}, u32[]{:S(2)}, u32[]{:S(2)}) collective-permute-start(bf16[64,256]{1,0:T(8,128)(2,1)S(1)} %get-tuple-element.111), channel_id=1, source_target_pairs={{0,3},{1,0},{2,1},{3,2},{4,7},{5,4},{6,5},{7,6},{8,11},{9,8},{10,9... | collective-permute-start | bytes 98312 | tf_op jit(solution)/shard_map/ppermute | solution.py:160
  (220 other events, 4246.3 us)

commit v2 on v1

v2 whole, which is shorter than its diff:
```python
import jax
import jax.numpy as jnp
from jax import lax
from jax.experimental import pallas as pl
from jax.experimental.pallas import tpu as pltpu
from jax.sharding import PartitionSpec as P

HDIM = 64
STATE = 128
SPAN = 128
BLOCK = 256


epsilon = 1e-05


def shifted(value, axis, steps):
    count = lax.axis_size(axis)
    leading, last = (max(0, -steps), min(count, count - steps))
    return lax.ppermute(value, axis, [(source, source + steps) for source in range(leading, last)])


def rotation(count, steps):
    return [(source, (source + steps) % count) for source in range(count)]


def flips(count, bit):
    return [(source, source ^ (1 << bit)) for source in range(count)]


def bits_of(count):
    return count.bit_length() - 1


def gather_blocks(block, axis):
    count = lax.axis_size(axis)
    half = count // 2
    rows = block.shape[0] // 2
    found = [None] * count
    found[0] = block
    left = right = block
    for step in range(1, half):
        left = lax.ppermute(left, axis, rotation(count, 1))
        right = lax.ppermute(right, axis, rotation(count, -1))
        found[count - step] = left
        found[step] = right
    far_low = lax.ppermute(left[:rows], axis, rotation(count, 1))
    far_high = lax.ppermute(right[rows:], axis, rotation(count, -1))
    found[half] = jnp.concatenate([far_low, far_high], axis=0)
    return found


def gather_columns(block, axis):
    count = lax.axis_size(axis)
    me = lax.axis_index(axis)
    width = block.shape[1]
    whole = jnp.zeros((block.shape[0], count * width), block.dtype)
    for step, piece in enumerate(gather_blocks(block, axis)):
        whole = lax.dynamic_update_slice_in_dim(whole, piece, (me + step) % count * width, 1)
    return whole


def scatter_columns(whole, axis):
    count = lax.axis_size(axis)
    me = lax.axis_index(axis)
    half = count // 2
    width = whole.shape[1] // count
    rows = whole.shape[0] // 2

    def part(step):
        return lax.dynamic_slice_in_dim(whole, (me + step) % count * width, width, 1)

    far = part(half)
    ahead = lax.ppermute(far[:rows].astype(jnp.bfloat16), axis, rotation(count, 1))
    behind = lax.ppermute(far[rows:].astype(jnp.bfloat16), axis, rotation(count, -1))
    first = True
    for step in range(half - 1, 0, -1):
        up = part(step).astype(jnp.float32)
        down = part(count - step).astype(jnp.float32)
        if first:
            up = up.at[:rows].add(ahead.astype(jnp.float32))
            down = down.at[rows:].add(behind.astype(jnp.float32))
            first = False
        else:
            up = up + ahead.astype(jnp.float32)
            down = down + behind.astype(jnp.float32)
        ahead = lax.ppermute(up.astype(jnp.bfloat16), axis, rotation(count, 1))
        behind = lax.ppermute(down.astype(jnp.bfloat16), axis, rotation(count, -1))
    return part(0).astype(jnp.float32) + ahead.astype(jnp.float32) + behind.astype(jnp.float32)


def small_sum(value, axis):
    count = lax.axis_size(axis)
    total = value
    for step in range(1, count):
        total = total + lax.ppermute(value, axis, rotation(count, step))
    return total


def doubled_sum(value, axis):
    count = lax.axis_size(axis)
    for bit in range(bits_of(count)):
        value = value + lax.ppermute(value, axis, flips(count, bit))
    return value


def halve(value, axis, bit, position):
    count = lax.axis_size(axis)
    mine = (lax.axis_index(axis) >> bit) & 1
    kept = lax.dynamic_index_in_dim(value, mine, position, False)
    sent = lax.dynamic_index_in_dim(value, 1 - mine, position, False)
    return kept + lax.ppermute(sent, axis, flips(count, bit))


def scatter_rows(value, axis):
    count = lax.axis_size(axis)
    bits = bits_of(count)
    rows, columns = value.shape
    split = value.reshape((2,) * bits + (rows // count, columns))
    split = halve(split, axis, 0, bits - 1)
    parts = []
    for piece in range(2):
        half = split[..., piece * (columns // 2) : (piece + 1) * (columns // 2)]
        left = list(range(bits - 1, 0, -1))
        order = list(range(1, bits)) if piece == 0 else list(range(bits - 1, 0, -1))
        for bit in order:
            half = halve(half, axis, bit, left.index(bit))
            left.remove(bit)
        parts.append(half)
    return jnp.concatenate(parts, axis=1).astype(jnp.float32)


def prefix_state(passing, state, axis, reverse):
    count = lax.axis_size(axis)
    me = lax.axis_index(axis)
    depth = state.shape[0]
    total = jnp.concatenate([state, jnp.broadcast_to(passing, (8, state.shape[1]))], axis=0)
    prefix = jnp.zeros_like(state)
    prefix_pass = jnp.ones_like(passing)
    for bit in range(bits_of(count)):
        other = lax.ppermute(total, axis, flips(count, bit))
        upper = ((me >> bit) & 1) == 1
        other_first = jnp.logical_not(upper) if reverse else upper
        other_state, other_pass = other[:depth], other[depth : depth + 1]
        total_state, total_pass = total[:depth], total[depth : depth + 1]
        prefix = jnp.where(other_first, prefix_pass * other_state + prefix, prefix)
        prefix_pass = jnp.where(other_first, prefix_pass * other_pass, prefix_pass)
        if bit < bits_of(count) - 1:
            joined = jnp.where(other_first, total_pass * other_state + total_state, other_pass * total_state + other_state)
            total = jnp.concatenate([joined, jnp.broadcast_to(total_pass * other_pass, (8, state.shape[1]))], axis=0)
    return prefix


def gather_small(value, axis):
    count = lax.axis_size(axis)
    me = lax.axis_index(axis)
    whole = jnp.zeros((count,) + value.shape, value.dtype)
    for step in range(count):
        piece = value if step == 0 else lax.ppermute(value, axis, rotation(count, -step))
        whole = lax.dynamic_update_index_in_dim(whole, piece, (me + step) % count, 0)
    return whole


def sum_everywhere(value):
    count, heads = lax.axis_size("seq"), lax.axis_size("head")
    bits = bits_of(count)
    rows, columns = value.shape
    split = value.reshape((2,) * bits + (rows // count, columns))
    for bit in range(bits):
        split = halve(split, "seq", bit, bits - 1 - bit)
    blocks = split.reshape(heads, rows // count // heads, columns)
    me = lax.axis_index("head")
    total = lax.dynamic_index_in_dim(blocks, me, 0, False)
    for step in range(1, heads):
        sent = lax.dynamic_index_in_dim(blocks, (me + step) % heads, 0, False)
        total = total + lax.ppermute(sent, "head", rotation(heads, step))
    whole = gather_small(total.astype(jnp.bfloat16), "head").reshape(rows // count, columns)
    place = lax.axis_index("seq")
    for bit in range(bits - 1, -1, -1):
        other = lax.ppermute(whole, "seq", flips(count, bit))
        upper = ((place >> bit) & 1) == 1
        low = jnp.where(upper, other, whole)
        high = jnp.where(upper, whole, other)
        whole = jnp.stack([low, high])
    order = list(range(bits - 1, -1, -1)) + [bits, bits + 1]
    return whole.transpose(order).reshape(rows, columns).astype(jnp.float32)


def dot(a, b, dims=(((1,), (0,)), ((), ()))):
    return lax.dot_general(a, b, dims, preferred_element_type=jnp.float32)


LAST = (((1,), (1,)), ((), ()))
FIRST = (((0,), (0,)), ((), ()))


def halves(value):
    high = value.astype(jnp.bfloat16)
    return high, (value - high.astype(jnp.float32)).astype(jnp.bfloat16)


def spread_heads(value, expand):
    high, rest = halves(value)
    return dot(high, expand) + dot(rest, expand)


def sum_heads(value, expand):
    high, rest = halves(value)
    return dot(high, expand, LAST) + dot(rest, expand, LAST)


def two_part(state):
    return jnp.concatenate(halves(state), axis=0)


def twice(value):
    value = value.astype(jnp.bfloat16)
    return jnp.concatenate([value, value], axis=1)


def triangle(size, upper):
    row = lax.broadcasted_iota(jnp.int32, (size, size), 0)
    column = lax.broadcasted_iota(jnp.int32, (size, size), 1)
    keep = column >= row if upper else row >= column
    return jnp.where(keep, 1.0, 0.0).astype(jnp.float32)


def exact_dot(a, b):
    return lax.dot_general(
        a, b, (((1,), (0,)), ((), ())), precision=lax.Precision.HIGHEST, preferred_element_type=jnp.float32
    )


def pair_blocks(value):
    lane = lax.broadcasted_iota(jnp.int32, value.shape, 1)
    zero = jnp.zeros_like(value)
    return jnp.concatenate(
        [jnp.where(lane < HDIM, value, zero), jnp.where(lane >= HDIM, value, zero)], axis=0
    )


def conv_rows(extended, taps, bias, rows):
    count = taps.shape[0]
    total = bias
    for tap in range(count):
        begin = 8 - (count - 1) + tap
        total = total + taps[tap : tap + 1] * extended[begin : begin + rows, :]
    return total


def head_terms(dt, timing, damping, seg_column, seg_row):
    value = dt + timing
    step = jnp.maximum(value, 0.0) + jnp.log1p(jnp.exp(-jnp.abs(value)))
    rate = jnp.exp(damping)
    log_decay = -step * rate
    rows = dt.shape[0]
    running = exact_dot(triangle(rows, False), log_decay)
    last = running[rows - 1 : rows]
    seg_last = seg_row[:, rows - 1 : rows]
    entering = jnp.where(seg_column == 0.0, jnp.exp(running), 0.0)
    toward = jnp.where(seg_column == seg_last, jnp.exp(last - running), 0.0)
    return value, step, rate, log_decay, running, entering, toward


def forward_kernel(
    proj, shared, dt, seg_col, seg_row, edge_v, edge_s, taps, offset, filters, baseline, timing, damping, skip, expand,
    full, readers_out, run_out, entry_out, states_out, final_out,
    ext_v, ext_s, state, carried,
):
    rows = dt.shape[0]
    heads = dt.shape[1]

    @pl.when(pl.program_id(0) == 0)
    def start():
        ext_v[0:8, :] = edge_v[...]
        ext_s[0:8, :] = edge_s[...]
        state[...] = jnp.zeros_like(state)
        carried[...] = jnp.ones_like(carried)

    ext_v[8 : 8 + rows, :] = proj[...]
    ext_s[8 : 8 + rows, :] = shared[...]
    pre = conv_rows(ext_v, taps[...], offset[...], rows)
    signal = pre * jax.nn.sigmoid(pre)
    pre_c = conv_rows(ext_s, filters[...], baseline[...], rows)
    control = pre_c * jax.nn.sigmoid(pre_c)
    ext_v[0:8, :] = ext_v[rows : rows + 8, :]
    ext_s[0:8, :] = ext_s[rows : rows + 8, :]
    writers = control[:, :STATE].astype(jnp.bfloat16)
    readers = control[:, STATE:].astype(jnp.bfloat16)
    readers_out[...] = readers
    seg_c, seg_r = seg_col[...], seg_row[0]
    value, step, rate, log_decay, running, entering, toward = head_terms(dt[...], timing[...], damping[...], seg_c, seg_r)
    across = running.T
    row = lax.broadcasted_iota(jnp.int32, (rows, rows), 0)
    column = lax.broadcasted_iota(jnp.int32, (rows, rows), 1)
    bias = jnp.where((seg_c == seg_r) & (row >= column), 0.0, -1e30)
    scores = dot(readers, writers, LAST)
    bias = jnp.concatenate([bias, bias], axis=1)
    scores = jnp.concatenate([scores, scores], axis=1)
    spread = spread_heads(jnp.concatenate([step, entering, toward, entering * carried[...]], axis=0), expand[...])
    step_e, enter_e, toward_e = spread[:rows], spread[rows : 2 * rows], spread[2 * rows : 3 * rows]
    run_out[...] = entering * carried[...]
    weighted = signal * step_e
    low = weighted.astype(jnp.bfloat16)
    old = state[...]
    states_out[0] = old
    carry = dot(twice(readers), two_part(old)) * enter_e + skip[...] * signal
    for pair in range(heads // 2):
        a, b = 2 * pair, 2 * pair + 1
        lanes = slice(pair * 2 * HDIM, (pair + 1) * 2 * HDIM)
        ahead = jnp.concatenate(
            [running[:, a : a + 1] - across[a : a + 1], running[:, b : b + 1] - across[b : b + 1]], axis=1
        )
        mixing = (jnp.exp(ahead + bias) * scores).astype(jnp.bfloat16)
        full[:, lanes] = dot(mixing, pair_blocks(low[:, lanes])) + carry[:, lanes]
    passing = enter_e[rows - 1 : rows]
    new = passing * old + dot(writers, (weighted * toward_e).astype(jnp.bfloat16), FIRST)
    state[...] = new
    final_out[...] = new
    entry_out[0] = carried[...]
    carried[...] = carried[...] * entering[rows - 1 : rows]


def vmem(limit=56):
    return pltpu.CompilerParams(vmem_limit_bytes=limit * 1024 * 1024, dimension_semantics=("arbitrary",))


def whole_spec(array):
    return pl.BlockSpec(array.shape, lambda *index: (0,) * array.ndim)


def forward_scan(proj, shared, dt, seg_col, seg_row, edge_v, edge_s, taps, offset, filters, baseline, timing, damping, skip, expand):
    length, inner = proj.shape
    heads = dt.shape[1]
    blocks = length // SPAN
    rows2 = lambda width: pl.BlockSpec((SPAN, width), lambda c: (c, 0))
    fixed = (edge_v, edge_s, taps, offset, filters, baseline, timing, damping, skip, expand)
    return pl.pallas_call(
        forward_kernel,
        grid=(blocks,),
        in_specs=[rows2(inner), rows2(2 * STATE), rows2(heads), rows2(1), pl.BlockSpec((1, 1, SPAN), lambda c: (c, 0, 0))]
        + [whole_spec(a) for a in fixed],
        out_specs=[
            rows2(inner), rows2(STATE), rows2(heads),
            pl.BlockSpec((1, 1, heads), lambda c: (c, 0, 0)),
            pl.BlockSpec((1, STATE, inner), lambda c: (c, 0, 0)),
            pl.BlockSpec((STATE, inner), lambda c: (0, 0)),
        ],
        out_shape=[
            jax.ShapeDtypeStruct((length, inner), jnp.float32),
            jax.ShapeDtypeStruct((length, STATE), jnp.bfloat16),
            jax.ShapeDtypeStruct((length, heads), jnp.float32),
            jax.ShapeDtypeStruct((blocks, 1, heads), jnp.float32),
            jax.ShapeDtypeStruct((blocks, STATE, inner), jnp.float32),
            jax.ShapeDtypeStruct((STATE, inner), jnp.float32),
        ],
        scratch_shapes=[
            pltpu.VMEM((SPAN + 8, inner), jnp.float32),
            pltpu.VMEM((SPAN + 8, 2 * STATE), jnp.float32),
            pltpu.VMEM((STATE, inner), jnp.float32),
            pltpu.VMEM((1, heads), jnp.float32),
        ],
        compiler_params=vmem(),
    )(proj, shared, dt, seg_col, seg_row, *fixed)


def join_kernel(local, readers, run, gate_in, incoming, expand, full, squares):
    run_e = spread_heads(run[...], expand[...])
    value = local[...] + run_e * dot(twice(readers[...]), two_part(incoming[...]))
    full[...] = value
    gate = gate_in[...]
    gated = value * gate * jax.nn.sigmoid(gate)
    squares[...] = jnp.sum(gated * gated, axis=1, keepdims=True)


def join_incoming(local, readers, run, gate_in, incoming, expand):
    length, inner = local.shape
    heads = run.shape[1]
    rows2 = lambda width: pl.BlockSpec((BLOCK, width), lambda c: (c, 0))
    return pl.pallas_call(
        join_kernel,
        grid=(length // BLOCK,),
        in_specs=[rows2(inner), rows2(STATE), rows2(heads), rows2(inner), whole_spec(incoming), whole_spec(expand)],
        out_specs=[rows2(inner), rows2(1)],
        out_shape=[jax.ShapeDtypeStruct((length, inner), jnp.float32), jax.ShapeDtypeStruct((length, 1), jnp.float32)],
        compiler_params=vmem(),
    )(local, readers, run, gate_in, incoming, expand)


def norm_cot_kernel(upstream, readout, full, gate_in, inverse, postnorm, norm_cot, inner_sum, gain_sum):
    @pl.when(pl.program_id(0) == 0)
    def start():
        gain_sum[...] = jnp.zeros_like(gain_sum)

    cot = dot(upstream[...], readout[...])
    norm_cot[...] = cot
    gate = gate_in[...]
    product = cot * (full[...] * gate * jax.nn.sigmoid(gate) * inverse[...])
    gain_sum[...] += jnp.sum(product.reshape(-1, 8, product.shape[1]), axis=0)
    inner_sum[...] = jnp.sum(product * postnorm[...], axis=1, keepdims=True)


def norm_cotangent(upstream, readout, full, gate_in, inverse, postnorm):
    length, inner = full.shape
    rows2 = lambda width: pl.BlockSpec((BLOCK, width), lambda c: (c, 0))
    return pl.pallas_call(
        norm_cot_kernel,
        grid=(length // BLOCK,),
        in_specs=[rows2(upstream.shape[1]), whole_spec(readout), rows2(inner), rows2(inner), rows2(1), whole_spec(postnorm)],
        out_specs=[rows2(inner), rows2(1), pl.BlockSpec((8, inner), lambda c: (0, 0))],
        out_shape=[
            jax.ShapeDtypeStruct((length, inner), jnp.float32),
            jax.ShapeDtypeStruct((length, 1), jnp.float32),
            jax.ShapeDtypeStruct((8, inner), jnp.float32),
        ],
        compiler_params=vmem(),
    )(upstream, readout, full, gate_in, inverse, postnorm)


def gate_kernel(norm_cot, full_in, gate_in, inverse, mean, postnorm, run, readers, expand, full_cot, gate_low, pending):
    @pl.when(pl.program_id(0) == 0)
    def start():
        pending[...] = jnp.zeros_like(pending)

    gate, full = gate_in[...], full_in[...]
    sigmoid = jax.nn.sigmoid(gate)
    active = gate * sigmoid
    scaled = inverse[...]
    unit = full * active * scaled
    gated_cot = scaled * (norm_cot[...] * postnorm[...] - unit * mean[...])
    cot = gated_cot * active
    full_cot[...] = cot
    gate_low[...] = (gated_cot * full * sigmoid * (1.0 + gate * (1.0 - sigmoid))).astype(jnp.bfloat16)
    run_e = spread_heads(run[...], expand[...])
    high, rest = halves(cot * run_e)
    pending[...] += dot(readers[...], high, FIRST)


def gate_cotangent(norm_cot, full, gate_in, inverse, mean, postnorm, run, readers, expand):
    length, inner = full.shape
    heads = run.shape[1]
    rows2 = lambda width: pl.BlockSpec((BLOCK, width), lambda c: (c, 0))
    return pl.pallas_call(
        gate_kernel,
        grid=(length // BLOCK,),
        in_specs=[rows2(inner), rows2(inner), rows2(inner), rows2(1), rows2(1), whole_spec(postnorm), rows2(heads), rows2(STATE), whole_spec(expand)],
        out_specs=[rows2(inner), rows2(inner), pl.BlockSpec((STATE, inner), lambda c: (0, 0))],
        out_shape=[
            jax.ShapeDtypeStruct((length, inner), jnp.float32),
            jax.ShapeDtypeStruct((length, inner), jnp.bfloat16),
            jax.ShapeDtypeStruct((STATE, inner), jnp.float32),
        ],
        compiler_params=vmem(),
    )(norm_cot, full, gate_in, inverse, mean, postnorm, run, readers, expand)


def silu_slope(pre, sigmoid):
    return sigmoid * (1.0 + pre * (1.0 - sigmoid))


def fold(value):
    return jnp.sum(value.reshape(-1, 8, value.shape[1]), axis=0)


def taps_back(pre_cot, taps, following, rows):
    count = taps.shape[0]
    total = taps[count - 1 : count] * pre_cot
    for tap in range(count - 1):
        later = count - 1 - tap
        total = total + taps[tap : tap + 1] * following[later : later + rows, :]
    return total


def backward_kernel(
    proj, shared, before_v, before_s, dt, seg_col, seg_row, full_cot, states, entry,
    edge_v, edge_s, taps, offset, filters, baseline, timing, damping, skip, expand, incoming, leaving, after_v, after_s,
    values_low, shared_low, dt_low, tap_sum, offset_sum, filter_sum, base_sum, timing_sum, damping_sum, direct_sum,
    tail_v, tail_s, head_v, head_s,
    ext_v, ext_s, later_v, later_s, lam,
):
    rows, heads = dt.shape
    step_index = pl.program_id(0)
    blocks = pl.num_programs(0)

    @pl.when(step_index == 0)
    def start():
        lam[...] = leaving[...]
        later_v[rows : rows + 8, :] = after_v[...]
        later_s[rows : rows + 8, :] = after_s[...]
        for item in (tap_sum, offset_sum, filter_sum, base_sum, timing_sum, damping_sum, direct_sum):
            item[...] = jnp.zeros_like(item)

    @pl.when(step_index == blocks - 1)
    def first_block():
        ext_v[0:8, :] = edge_v[...]
        ext_s[0:8, :] = edge_s[...]

    @pl.when(step_index < blocks - 1)
    def other_block():
        ext_v[0:8, :] = before_v[...]
        ext_s[0:8, :] = before_s[...]

    ext_v[8 : 8 + rows, :] = proj[...]
    ext_s[8 : 8 + rows, :] = shared[...]
    pre = conv_rows(ext_v, taps[...], offset[...], rows)
    sigmoid = jax.nn.sigmoid(pre)
    signal = pre * sigmoid
    pre_c = conv_rows(ext_s, filters[...], baseline[...], rows)
    sigmoid_c = jax.nn.sigmoid(pre_c)
    control = pre_c * sigmoid_c
    writers = control[:, :STATE].astype(jnp.bfloat16)
    readers = control[:, STATE:].astype(jnp.bfloat16)
    seg_c, seg_r = seg_col[...], seg_row[0]
    value, step, rate, log_decay, running, entering, toward = head_terms(dt[...], timing[...], damping[...], seg_c, seg_r)
    across = running.T
    row = lax.broadcasted_iota(jnp.int32, (rows, rows), 0)
    column = lax.broadcasted_iota(jnp.int32, (rows, rows), 1)
    bias = jnp.where((seg_c == seg_r) & (column >= row), 0.0, -1e30)
    scores = dot(writers, readers, LAST)
    bias = jnp.concatenate([bias, bias], axis=1)
    scores = jnp.concatenate([scores, scores], axis=1)
    one_hot = expand[...]
    spread = spread_heads(jnp.concatenate([step, entering, toward], axis=0), one_hot)
    step_e, enter_e, toward_e = spread[:rows], spread[rows : 2 * rows], spread[2 * rows : 3 * rows]
    cot = full_cot[...]
    cot_low = cot.astype(jnp.bfloat16)
    weighted = signal * step_e
    low = weighted.astype(jnp.bfloat16)
    after = lam[...]
    after_parts = two_part(after)
    from_state = dot(twice(writers), after_parts) * toward_e
    entry_e = spread_heads(jnp.broadcast_to(entry[0], (8, heads)), one_hot)
    old = states[0] + entry_e[0:1] * incoming[...]
    old_parts = two_part(old)
    cot_entering = cot * enter_e
    cot_entering_low = cot_entering.astype(jnp.bfloat16)
    score_cot = jnp.zeros((rows, rows), jnp.float32)
    row_sums = jnp.zeros((rows, heads), jnp.float32)
    column_sums = []
    ones = jnp.ones((8, rows), jnp.bfloat16)
    place = lax.broadcasted_iota(jnp.int32, (2 * rows, heads), 0) // rows
    head_place = lax.broadcasted_iota(jnp.int32, (2 * rows, heads), 1)
    direct_part = []
    step_part = []
    for pair in range(heads // 2):
        a, b = 2 * pair, 2 * pair + 1
        lanes = slice(pair * 2 * HDIM, (pair + 1) * 2 * HDIM)
        ahead = jnp.concatenate(
            [across[a : a + 1] - running[:, a : a + 1], across[b : b + 1] - running[:, b : b + 1]], axis=1
        )
        decays = jnp.exp(ahead + bias)
        mixing = decays * scores
        blocked = pair_blocks(cot_low[:, lanes])
        weighted_cot = dot(mixing.astype(jnp.bfloat16), blocked) + from_state[:, lanes]
        step_part.append(weighted_cot * signal[:, lanes])
        later_v[0:rows, lanes] = weighted_cot * step_e[:, lanes] + skip[:, lanes] * cot[:, lanes]
        inner = dot(low[:, lanes], blocked, LAST)
        linked = inner * decays
        score_cot = score_cot + linked[:, :rows] + linked[:, rows:]
        energy = (inner * mixing).astype(jnp.bfloat16)
        chosen = jnp.where(head_place == place + a, 1.0, 0.0).astype(jnp.bfloat16)
        row_sums = row_sums + dot(energy, chosen)
        column_sums.append(dot(ones, energy))
    step_cot = sum_heads(jnp.concatenate(step_part, axis=1), one_hot)
    sums_across = jnp.concatenate(
        [piece for pair in column_sums for piece in (pair[0:1, :rows], pair[0:1, rows:])], axis=0
    )
    state_term = weighted * from_state
    enter_term = cot_entering * dot(twice(readers), old_parts)
    passing = enter_e[rows - 1 : rows]
    last_term = fold(state_term) + fold(after * old * passing)
    running_cot = sums_across.T - row_sums + sum_heads(enter_term - state_term, one_hot)
    last_cot = jnp.sum(sum_heads(last_term, one_hot), axis=0, keepdims=True)
    decay_cot = exact_dot(triangle(rows, True), running_cot) + last_cot
    step_cot = step_cot - decay_cot * rate
    dt_cot = step_cot * jax.nn.sigmoid(value)
    dt_low[...] = dt_cot.astype(jnp.bfloat16)
    timing_sum[...] += fold(dt_cot)
    damping_sum[...] += fold(decay_cot * log_decay)
    direct_sum[...] += fold(cot * signal)
    score_low = score_cot.astype(jnp.bfloat16)
    reader_cot = dot(score_low, writers, FIRST) + dot(
        jnp.concatenate([cot_entering_low, cot_entering_low], axis=1), jnp.concatenate(halves(old), axis=1), LAST
    )
    push = (weighted * toward_e).astype(jnp.bfloat16)
    writer_cot = dot(score_low, readers) + dot(
        jnp.concatenate([push, push], axis=1), jnp.concatenate(halves(after), axis=1), LAST
    )
    lam[...] = passing * after + dot(readers, cot_entering_low, FIRST)

    pre_cot = later_v[0:rows, :] * silu_slope(pre, sigmoid)
    later_v[0:rows, :] = pre_cot
    pre_cot_c = jnp.concatenate([writer_cot, reader_cot], axis=1) * silu_slope(pre_c, sigmoid_c)
    later_s[0:rows, :] = pre_cot_c
    values_cot = taps_back(pre_cot, taps[...], later_v, rows)
    shared_cot = taps_back(pre_cot_c, filters[...], later_s, rows)
    values_low[...] = values_cot.astype(jnp.bfloat16)
    shared_low[...] = shared_cot.astype(jnp.bfloat16)
    count = taps.shape[0]
    for tap in range(count):
        begin = 8 - (count - 1) + tap
        tap_sum[tap] += fold(pre_cot * ext_v[begin : begin + rows, :])
        filter_sum[tap] += fold(pre_cot_c * ext_s[begin : begin + rows, :])
    offset_sum[...] += fold(pre_cot)
    base_sum[...] += fold(pre_cot_c)
    later_v[rows : rows + 8, :] = later_v[0:8, :]
    later_s[rows : rows + 8, :] = later_s[0:8, :]

    @pl.when(step_index == 0)
    def tail():
        tail_v[...] = values_cot[rows - 8 :, :]
        tail_s[...] = shared_cot[rows - 8 :, :]

    @pl.when(step_index == blocks - 1)
    def head():
        head_v[...] = pre_cot[0:8, :]
        head_s[...] = pre_cot_c[0:8, :]


def backward_scan(
    proj, shared, dt, seg_col, seg_row, full_cot, states, entry,
    edge_v, edge_s, taps, offset, filters, baseline, timing, damping, skip, expand, incoming, leaving, after_v, after_s,
):
    length, inner = proj.shape
    heads = dt.shape[1]
    blocks = length // SPAN
    count = taps.shape[0]
    back = lambda c: blocks - 1 - c
    rows2 = lambda width: pl.BlockSpec((SPAN, width), lambda c: (back(c), 0))
    before = lambda width: pl.BlockSpec((8, width), lambda c: (jnp.maximum(back(c) * (SPAN // 8) - 1, 0), 0))
    lead = lambda *shape: pl.BlockSpec((1,) + shape, lambda c: (back(c), 0, 0))
    fixed = (edge_v, edge_s, taps, offset, filters, baseline, timing, damping, skip, expand, incoming, leaving, after_v, after_s)
    f32 = lambda *shape: jax.ShapeDtypeStruct(shape, jnp.float32)
    sums = [f32(count, 8, inner), f32(8, inner), f32(count, 8, 2 * STATE), f32(8, 2 * STATE), f32(8, heads), f32(8, heads), f32(8, inner), f32(8, inner), f32(8, 2 * STATE), f32(8, inner), f32(8, 2 * STATE)]
    low = lambda width: jax.ShapeDtypeStruct((length, width), jnp.bfloat16)
    return pl.pallas_call(
        backward_kernel,
        grid=(blocks,),
        in_specs=[rows2(inner), rows2(2 * STATE), before(inner), before(2 * STATE), rows2(heads), rows2(1), lead(1, SPAN), rows2(inner), lead(STATE, inner), lead(1, heads)]
        + [whole_spec(a) for a in fixed],
        out_specs=[rows2(inner), rows2(2 * STATE), rows2(heads)] + [whole_spec(a) for a in sums],
        out_shape=[low(inner), low(2 * STATE), low(heads)] + sums,
        scratch_shapes=[
            pltpu.VMEM((SPAN + 8, inner), jnp.float32),
            pltpu.VMEM((SPAN + 8, 2 * STATE), jnp.float32),
            pltpu.VMEM((SPAN + 8, inner), jnp.float32),
            pltpu.VMEM((SPAN + 8, 2 * STATE), jnp.float32),
            pltpu.VMEM((STATE, inner), jnp.float32),
        ],
        compiler_params=vmem(),
    )(proj, shared, proj, shared, dt, seg_col, seg_row, full_cot, states, entry, *fixed)


def normed_cot_kernel(gate_low, values_low, shared_low, dt_low, gating, values, control, timestep, tokens, scale, gain, low, row_sum, gain_sum):
    @pl.when(pl.program_id(0) == 0)
    def start():
        gain_sum[...] = jnp.zeros_like(gain_sum)

    total = dot(gate_low[...], gating[...], LAST) + dot(values_low[...], values[...], LAST)
    total = total + dot(shared_low[...], control[...], LAST) + dot(dt_low[...], timestep[...], LAST)
    low[...] = total.astype(jnp.bfloat16)
    product = total * (tokens[...].astype(jnp.float32) * scale[...])
    gain_sum[...] += fold(product)
    row_sum[...] = jnp.sum(product * gain[...], axis=1, keepdims=True)


def normed_cotangent(gate_low, values_low, shared_low, dt_low, gating, values, control, timestep, tokens, scale, gain):
    length = gate_low.shape[0]
    width = gating.shape[0]
    rows2 = lambda size: pl.BlockSpec((BLOCK, size), lambda c: (c, 0))
    parts = (gate_low, values_low, shared_low, dt_low)
    weights = (gating, values, control, timestep)
    return pl.pallas_call(
        normed_cot_kernel,
        grid=(length // BLOCK,),
        in_specs=[rows2(a.shape[1]) for a in parts] + [whole_spec(a) for a in weights] + [rows2(width), rows2(1), whole_spec(gain)],
        out_specs=[rows2(width), rows2(1), pl.BlockSpec((8, width), lambda c: (0, 0))],
        out_shape=[
            jax.ShapeDtypeStruct((length, width), jnp.bfloat16),
            jax.ShapeDtypeStruct((length, 1), jnp.float32),
            jax.ShapeDtypeStruct((8, width), jnp.float32),
        ],
        compiler_params=vmem(),
    )(*parts, *weights, tokens, scale, gain)


def shards(
    tokens,
    prenorm,
    gating,
    values,
    control,
    timestep,
    kernel,
    offset,
    filters,
    baseline,
    timing,
    damping,
    direct,
    postnorm,
    readout,
    doc_starts,
    cotangent,
):
    length, share = tokens.shape
    inner = kernel.shape[1]
    heads = timing.shape[0]
    ranks = lax.axis_size("head")
    features = share * ranks
    channels = inner * ranks
    blocks = length // SPAN
    f32, bf16 = jnp.float32, jnp.bfloat16

    starts = doc_starts.reshape(blocks, SPAN).astype(bf16)
    place = jnp.arange(SPAN)
    counted = jnp.dot(starts, (place[:, None] <= place[None, :]).astype(bf16), preferred_element_type=f32)
    seg_row, seg_col = counted.reshape(blocks, 1, SPAN), counted.reshape(length, 1)
    expand = (jnp.arange(heads)[:, None] == jnp.arange(inner)[None, :] // HDIM).astype(bf16)
    skip = jnp.repeat(direct, HDIM)[None]
    offset_row, baseline_row, postnorm_row = offset[None], baseline[None], postnorm[None]
    timing_row, damping_row = timing[None], damping[None]

    gain = gather_small(prenorm, "head").reshape(1, features).astype(f32)
    gathered = gather_columns(tokens, "head")
    wide = gathered.astype(f32)
    scale = lax.rsqrt(jnp.mean(wide * wide, axis=1, keepdims=True) + epsilon)
    normed = (wide * scale * gain).astype(bf16)
    gate_in = jnp.dot(normed, gating, preferred_element_type=f32)
    projected = jnp.dot(normed, values, preferred_element_type=f32)
    shared = jnp.dot(normed, control, preferred_element_type=f32)
    timestep_in = jnp.dot(normed, timestep, preferred_element_type=f32)

    edge = shifted(jnp.concatenate([projected[length - 8 :], shared[length - 8 :]], axis=1), "seq", 1)
    edge_v, edge_s = edge[:, :inner], edge[:, inner:]
    local, readers, run, entry, states, final = forward_scan(
        projected, shared, timestep_in, seg_col, seg_row, edge_v, edge_s, kernel, offset_row, filters, baseline_row,
        timing_row, damping_row, skip, expand,
    )
    passing = jnp.repeat(run[length - 1 :], HDIM, axis=1)
    incoming = prefix_state(passing, final, "seq", False)
    full, squares = join_incoming(local, readers, run, gate_in, incoming, expand)
    squares = small_sum(squares.reshape(length), "head")
    inverse = lax.rsqrt(squares / channels + epsilon)[:, None]
    normalized = (full * jax.nn.silu(gate_in) * inverse * postnorm_row).astype(bf16)
    partial_rows = lax.dot_general(normalized, readout, LAST, preferred_element_type=f32).astype(bf16)
    branch = scatter_columns(partial_rows, "head")
    mixed = (tokens.astype(f32) + branch).astype(bf16)

    upstream = gather_columns(cotangent, "head")
    norm_cot, inner_sum, postnorm_sum = norm_cotangent(upstream, readout, full, gate_in, inverse, postnorm_row)
    mean = small_sum(inner_sum.reshape(length), "head")[:, None] / channels
    full_cot, gate_low, pending = gate_cotangent(
        norm_cot, full, gate_in, inverse, mean, postnorm_row, run, readers, expand
    )
    leaving = prefix_state(passing, pending, "seq", True)
    readout_local = lax.dot_general(upstream, normalized, FIRST, preferred_element_type=f32)
    gating_local = lax.dot_general(normed, gate_low, FIRST, preferred_element_type=f32)
    zeros_v, zeros_s = jnp.zeros((8, inner), f32), jnp.zeros((8, 2 * STATE), f32)
    (
        values_low, shared_low, timestep_low, tap_sum, offset_sum, filter_sum, base_sum, timing_sum, damping_sum, direct_sum,
        tail_v, tail_s, head_v, head_s,
    ) = backward_scan(
        projected, shared, timestep_in, seg_col, seg_row, full_cot, states, entry,
        edge_v, edge_s, kernel, offset_row, filters, baseline_row, timing_row, damping_row, skip, expand,
        incoming, leaving, zeros_v, zeros_s,
    )
    ahead = shifted(jnp.concatenate([head_v, head_s], axis=1), "seq", -1)
    ahead = jnp.concatenate([jnp.zeros_like(ahead), ahead], axis=0)
    taps = kernel.shape[0]
    for tap in range(taps):
        begin = taps - 1 - tap
        tail_v = tail_v + kernel[tap] * ahead[begin : begin + 8, :inner]
        tail_s = tail_s + filters[tap] * ahead[begin : begin + 8, inner:]
    values_low = values_low.at[length - 8 :].set(tail_v.astype(bf16))
    shared_low = shared_low.at[length - 8 :].set(tail_s.astype(bf16))

    normed_low, row_sum, prenorm_sum = normed_cotangent(
        gate_low, values_low, shared_low, timestep_low, gating, values, control, timestep, gathered, scale, gain
    )
    row_mean = small_sum(row_sum.reshape(length), "head")[:, None] / features
    own_total = scatter_columns(normed_low, "head")
    own_units = tokens.astype(f32) * scale
    tokens_gradient = cotangent.astype(f32) + scale * (own_total * prenorm.astype(f32) - own_units * row_mean)
    values_local = lax.dot_general(normed, values_low, FIRST, preferred_element_type=f32)
    control_local = lax.dot_general(normed, shared_low, FIRST, preferred_element_type=f32)
    timestep_local = lax.dot_general(normed, timestep_low, FIRST, preferred_element_type=f32)

    gating_gradient, values_gradient, readout_gradient = (
        scatter_rows(gating_local.astype(bf16), "seq"),
        scatter_rows(values_local.astype(bf16), "seq"),
        scatter_rows(readout_local.astype(bf16), "seq"),
    )
    timestep_gradient = scatter_rows(timestep_local, "seq")
    control_gradient = sum_everywhere(control_local)
    everywhere = (filter_sum.sum(1), base_sum.sum(0), prenorm_sum.sum(0))
    split = (
        tap_sum.sum(1), offset_sum.sum(0), timing_sum.sum(0), damping_sum.sum(0),
        direct_sum.sum(0).reshape(heads, HDIM).sum(1), postnorm_sum.sum(0),
    )
    flat_every = jnp.concatenate([item.reshape(-1) for item in everywhere])
    flat_split = jnp.concatenate([item.reshape(-1) for item in split])
    flat = doubled_sum(jnp.concatenate([flat_every, flat_split]), "seq")
    pieces = gather_small(flat, "head")
    summed = jnp.sum(pieces[:, : flat_every.shape[0]], axis=0)
    totals = []
    begin = 0
    for item in everywhere:
        totals.append(summed[begin : begin + item.size].reshape(item.shape))
        begin += item.size
    for item in split:
        piece = pieces[:, begin : begin + item.size].reshape((ranks,) + item.shape)
        totals.append(jnp.moveaxis(piece, 0, -2).reshape(item.shape[:-1] + (-1,)))
        begin += item.size
    return (
        mixed,
        tokens_gradient,
        totals[2],
        gating_gradient,
        values_gradient,
        control_gradient,
        timestep_gradient,
        totals[3],
        totals[4],
        totals[0],
        totals[1],
        totals[5],
        totals[6],
        totals[7],
        totals[8],
        readout_gradient,
    )


def solution(mesh):
    return jax.shard_map(
        shards,
        mesh=mesh,
        in_specs=(
            P("seq", "head"),
            P("head"),
            P(None, "head"),
            P(None, "head"),
            P(),
            P(None, "head"),
            P(None, "head"),
            P("head"),
            P(),
            P(),
            P("head"),
            P("head"),
            P("head"),
            P("head"),
            P(None, "head"),
            P("seq"),
            P("seq", "head"),
        ),
        out_specs=(
            P("seq", "head"),
            P("seq", "head"),
            P(),
            P("seq", "head"),
            P("seq", "head"),
            P(),
            P("seq", "head"),
            P(),
            P(),
            P(),
            P(),
            P(),
            P(),
            P(),
            P(),
            P("seq", "head"),
        ),
        check_vma=False,
    )
```

time: 793 us -> 625 us (0.79)
  matrix products: 157 us -> 45.5 us
  Pallas kernels: 0 us -> 104 us
  local copies, waits for them, and re-layouts: 126 us -> 48.3 us
  other arithmetic: 137 us -> 64.2 us
  starting transfers between devices: 101 us -> 79.8 us
  waiting for transfers between devices: 256 us -> 269 us
    dot_general x29 -> x11, matrix products: 157 us -> 45.5 us  [the longest x1 8.31 us: shards(): lax.dot_general(upstream, normalized, FIRST, preferred_element_type=f32)]
    pallas_call x0 -> x6, Pallas kernels: none -> 104 us  [the longest x1 39.2 us: backward_scan(): pl.pallas_call(backward_kernel, grid=(blocks,), in_specs=[rows2(inner), r...]
    ppermute x9, waiting for transfers between devices: 104 us -> 48.8 us  [gather_small(): lax.ppermute(value, axis, rotation(count, -step))]
    reshape x10 -> x2, local copies, waits for them, and re-layouts: 46.1 us -> 1.09 us  [the longest x1 1.02 us: shards(): counted.reshape(length, 1)]
    reduce_sum x10 -> x12, other arithmetic: 33.2 us -> 3.41 us  [the longest x1 3.07 us: shards(): scale = lax.rsqrt(jnp.mean(wide * wide, axis=1, keepdims=True) + epsilon)]
    ppermute x2, waiting for transfers between devices: 28.6 us -> 58.1 us  [gather_blocks(): left = lax.ppermute(left, axis, rotation(count, 1))]
    another operation x13 -> x0, other arithmetic: 21.7 us -> none
    mul x11 -> x0, other arithmetic: 21.2 us -> none  [the longest x1 9.72 us: activate(): jax.nn.silu(causal_conv(jnp.concatenate([edge_values, projected], axis=0)...]
  transfers between devices with their start and end apart: 78 -> 74, of which waited for: 31 -> 33; matrix products, arithmetic and copies ran while one was open for 45% -> 20% of each run, Pallas kernels for 0% -> 9%
where the time goes in v2:
time: 625 us; the launch traced here: 614 us
  waiting for transfers between devices  269 us (43%)
  Pallas kernels  104 us (17%)
  starting transfers between devices  79.8 us (13%)
  other arithmetic  64.2 us (10%)
  local copies, waits for them, and re-layouts  48.3 us (8%)
  matrix products  45.5 us (7%)
    ppermute x2, waiting for transfers between devices, gather_blocks(): left = lax.ppermute(left, axis, rotation(count, 1))  58.1 us
    ppermute x9, waiting for transfers between devices, gather_small(): lax.ppermute(value, axis, rotation(count, -step))  48.8 us
    ppermute x23, waiting for transfers between devices, halve(): return kept + lax.ppermute(sent, axis, flips(count, bit))  48.3 us
    pallas_call x1, Pallas kernels, backward_scan(): pl.pallas_call(backward_kernel, grid=(blocks,), in_specs=[rows2(inner), r...  39.2 us
    ppermute x3, waiting for transfers between devices, sum_everywhere(): total = total + lax.ppermute(sent, 'head', rotation(heads, step))  22.3 us
    ppermute x2, waiting for transfers between devices, gather_blocks(): right = lax.ppermute(right, axis, rotation(count, -1))  20.4 us
    pallas_call x1, Pallas kernels, normed_cotangent(): pl.pallas_call(normed_cot_kernel, grid=(length // BLOCK,), in_specs=[rows...  18.4 us
    pallas_call x1, Pallas kernels, forward_scan(): pl.pallas_call(forward_kernel, grid=(blocks,), in_specs=[rows2(inner), ro...  18.3 us
  transfers between devices with their start and end apart: 74, of which 33 were waited for; matrix products, arithmetic and copies ran while one was open for 20% of the time, Pallas kernels for 9%

profile of v2, /device:TPU:4, one launch (start us, length us, event | category | flops | bytes accessed | tf_op | source)
XLA Modules:
  0.0 614.0 jit_solution(15464476502198529266)
XLA Ops:
  8.0 20.8 %collective-permute-done.1 = bf16[1024,512]{1,0:T(8,128)(2,1)S(1)} collective-permute-done((bf16[1024,512]{1,0:T(8,128)(2,1)}, bf16[1024,512]{1,0:T(8,128)(2,1)S(1)}, u32[]{:S(2)}, u32[]{:S(2)}) %collective-permute-start.1) | collective-permute-done | bytes 1048608 | tf_op jit(solution)/shard_map/ppermute | solution.py:43
  29.6 20.4 %collective-permute-done = bf16[1024,512]{1,0:T(8,128)(2,1)S(1)} collective-permute-done((bf16[1024,512]{1,0:T(8,128)(2,1)}, bf16[1024,512]{1,0:T(8,128)(2,1)S(1)}, u32[]{:S(2)}, u32[]{:S(2)}) %collective-permute-start) | collective-permute-done | bytes 1048608 | tf_op jit(solution)/shard_map/ppermute | solution.py:44
  65.1 7.8 %collective-permute-done.3 = bf16[512,512]{1,0:T(8,128)(2,1)} collective-permute-done((bf16[512,512]{1,0:T(8,128)(2,1)}, bf16[512,512]{1,0:T(8,128)(2,1)}, u32[]{:S(2)}, u32[]{:S(2)}) %collective-permute-start.3) | collective-permute-done | bytes 524320 | tf_op jit(solution)/shard_map/ppermute | solution.py:48
  96.0 18.3 %shard_map.288 = (f32[1024,1024]{1,0:T(8,128)}, bf16[1024,128]{1,0:T(8,128)(2,1)}, f32[1024,16]{1,0:T(8,128)}, f32[8,1,16]{2,1,0:T(1,128)}, f32[8,128,1024]{2,1,0:T(8,128)}, /*index=5*/f32[128,1024]{1,0:T(8,128)}) custom-call(f32[1024,1024]{1,0:T(8,128)} %copy-done, f32[1024,256]{1,0:T(8,128)} %copy-done.6, f32[1024,16]{1,0:T(8,128)} %fusion.56.dt, ...), custom_call_target="tpu_custom_call" | custom-call | tf_op jit(solution)/shard_map/pallas_call | solution.py:338
  127.9 37.2 %collective-permute-done.19 = bf16[1024,512]{1,0:T(8,128)(2,1)S(1)} collective-permute-done((bf16[1024,512]{1,0:T(8,128)(2,1)S(1)}, bf16[1024,512]{1,0:T(8,128)(2,1)S(1)}, u32[]{:S(2)}, u32[]{:S(2)}) %collective-permute-start.19) | collective-permute-done | bytes 1048608 | tf_op jit(solution)/shard_map/ppermute | solution.py:43
  173.6 6.1 fusion.57.gate_in
  181.9 9.9 %collective-permute-done.21 = bf16[512,512]{1,0:T(8,128)(2,1)S(1)} collective-permute-done((bf16[512,512]{1,0:T(8,128)(2,1)S(1)}, bf16[512,512]{1,0:T(8,128)(2,1)S(1)}, u32[]{:S(2)}, u32[]{:S(2)}) %collective-permute-start.21) | collective-permute-done | bytes 524320 | tf_op jit(solution)/shard_map/ppermute | solution.py:48
  194.9 7.4 %shard_map.289 = (f32[1024,1024]{1,0:T(8,128)}, f32[1024,1]{1,0:T(8,128)}) custom-call(f32[1024,1024]{1,0:T(8,128)} %get-tuple-element.119.local, bf16[1024,128]{1,0:T(8,128)(2,1)} %get-tuple-element.120.readers, f32[1024,16]{1,0:T(8,128)} %get-tuple-element.121.run, f32[1024,1024]{1,0:T(8,128)} %fusion.57.gate_in, f32[128,1024]{1,0:T(8,128)} %add_select_fusion.2.incoming, ...), custom_call_target="tpu_custom_call" | custom-call | tf_op jit(solution)/shard_map/pallas_call | solution.py:380
  214.9 11.0 %shard_map.290 = (f32[1024,1024]{1,0:T(8,128)}, f32[1024,1]{1,0:T(8,128)}, f32[8,1024]{1,0:T(8,128)}) custom-call(bf16[1024,2048]{1,0:T(8,128)(2,1)} %constant_dynamic-update-slice_fusion.2.upstream, bf16[2048,1024]{1,0:T(8,128)(2,1)} %readout.1, f32[1024,1024]{1,0:T(8,128)} %get-tuple-element.123.full.full_in, f32[1024,1024]{1,0:T(8,128)} %fusion.57.gate_in, ...), custom_call_target="tpu_custom_call" | custom-call | tf_op jit(solution)/shard_map/pallas_call | solution.py:406
  232.2 8.3 %convolution_convert_fusion = bf16[2048,1024]{1,0:T(8,128)(2,1)} fusion(bf16[1024,2048]{1,0:T(8,128)(2,1)} %constant_dynamic-update-slice_fusion.2.upstream, bf16[1024,1024]{1,0:T(8,128)(2,1)S(1)} %multiply_convert_fusion), kind=kOutput, calls=%fused_computation.6 | convolution fusion | flops 4297064448 | bytes 10485760 | tf_op jit(solution)/shard_map/dot_general | solution.py:757
  241.6 9.8 %shard_map.291 = (f32[1024,1024]{1,0:T(8,128)}, bf16[1024,1024]{1,0:T(8,128)(2,1)}, f32[128,1024]{1,0:T(8,128)}) custom-call(f32[1024,1024]{1,0:T(8,128)} %get-tuple-element.125.norm_cot, f32[1024,1024]{1,0:T(8,128)} %get-tuple-element.123.full.full_in, f32[1024,1024]{1,0:T(8,128)} %fusion.57.gate_in, f32[1024,1]{1,0:T(8,128)} %copy.63.inverse, ...), custom_call_target="tpu_custom_call" | custom-call | tf_op jit(solution)/shard_map/pallas_call | solution.py:443
  277.6 7.3 %collective-permute-done.26 = f32[136,1024]{1,0:T(8,128)S(1)} collective-permute-done((f32[136,1024]{1,0:T(8,128)S(1)}, f32[136,1024]{1,0:T(8,128)S(1)}, u32[]{:S(2)}, u32[]{:S(2)}) %collective-permute-start.26) | collective-permute-done | bytes 557088 | tf_op jit(solution)/shard_map/ppermute | solution.py:141
  290.9 8.8 %collective-permute-done.27 = f32[136,1024]{1,0:T(8,128)S(1)} collective-permute-done((f32[136,1024]{1,0:T(8,128)S(1)}, f32[136,1024]{1,0:T(8,128)S(1)}, u32[]{:S(2)}, u32[]{:S(2)}) %collective-permute-start.27) | collective-permute-done | bytes 557088 | tf_op jit(solution)/shard_map/ppermute | solution.py:141
  302.9 39.2 %shard_map.292 = (bf16[1024,1024]{1,0:T(8,128)(2,1)}, bf16[1024,256]{1,0:T(8,128)(2,1)}, bf16[1024,16]{1,0:T(8,128)(2,1)}, f32[4,8,1024]{2,1,0:T(8,128)}, f32[8,...) custom-call(f32[1024,1024]{1,0:T(8,128)} %copy-done, ...), custom_call_target="tpu_custom_call" | custom-call | tf_op jit(solution)/shard_map/pallas_call | solution.py:636
  352.8 6.2 %convolution_convert_fusion.1 = bf16[2048,1024]{1,0:T(8,128)(2,1)} fusion(bf16[1024,2048]{1,0:T(8,128)(2,1)S(1)} %copy-done.4, bf16[1024,1024]{1,0:T(8,128)(2,1)S(1)} %constant_dynamic-update-slice_fusion.1.values_low), kind=kOutput, calls=%fused_computation.7 | convolution fusion | flops 4297064448 | bytes 10485760 | tf_op jit(solution)/shard_map/dot_general | solution.py:785
  359.0 18.4 %shard_map.293 = (bf16[1024,2048]{1,0:T(8,128)(2,1)}, f32[1024,1]{1,0:T(8,128)}, f32[8,2048]{1,0:T(8,128)}) custom-call(bf16[1024,1024]{1,0:T(8,128)(2,1)} %get-tuple-element.127.gate_low, bf16[1024,1024]{1,0:T(8,128)(2,1)} %copy-done.21, bf16[1024,256]{1,0:T(8,128)(2,1)} %copy-done.28, bf16[1024,16]{1,0:T(8,128)(2,1)} %get-tuple-element.138.dt_low, ...), custom_call_target="tpu_custom_call" | custom-call | tf_op jit(solution)/shard_map/pallas_call | solution.py:673
  432.4 7.4 %collective-permute-done.31 = bf16[512,512]{1,0:T(8,128)(2,1)S(1)} collective-permute-done((bf16[512,512]{1,0:T(8,128)(2,1)}, bf16[512,512]{1,0:T(8,128)(2,1)S(1)}, u32[]{:S(2)}, u32[]{:S(2)}) %collective-permute-start.31) | collective-permute-done | bytes 524320 | tf_op jit(solution)/shard_map/ppermute | solution.py:75
  443.7 10.0 %collective-permute-done.43 = bf16[2,256,512]{2,1,0:T(8,128)(2,1)S(1)} collective-permute-done((bf16[2,256,512]{2,1,0:T(8,128)(2,1)S(1)}, bf16[2,256,512]{2,1,0:T(8,128)(2,1)S(1)}, u32[]{:S(2)}, u32[]{:S(2)}) %collective-permute-start.43) | collective-permute-done | bytes 524320 | tf_op jit(solution)/shard_map/ppermute | solution.py:112
  462.8 11.3 %collective-permute-done.53 = f32[2,256,256]{2,1,0:T(8,128)S(1)} collective-permute-done((f32[2,256,256]{2,1,0:T(8,128)S(1)}, f32[2,256,256]{2,1,0:T(8,128)S(1)}, u32[]{:S(2)}, u32[]{:S(2)}) %collective-permute-start.53) | collective-permute-done | bytes 524320 | tf_op jit(solution)/shard_map/ppermute | solution.py:112
  487.6 19.1 %collective-permute-done.56 = f32[64,256]{1,0:T(8,128)S(1)} collective-permute-done((f32[64,256]{1,0:T(8,128)S(1)}, f32[64,256]{1,0:T(8,128)S(1)}, u32[]{:S(2)}, u32[]{:S(2)}) %collective-permute-start.56) | collective-permute-done | bytes 65568 | tf_op jit(solution)/shard_map/ppermute | solution.py:176
  510.9 41.4 %collective-permute-done.58 = bf16[64,256]{1,0:T(8,128)(2,1)S(1)} collective-permute-done((bf16[64,256]{1,0:T(8,128)(2,1)S(1)}, bf16[64,256]{1,0:T(8,128)(2,1)S(1)}, u32[]{:S(2)}, u32[]{:S(2)}) %collective-permute-start.58) | collective-permute-done | bytes 32800 | tf_op jit(solution)/shard_map/ppermute | solution.py:159
  559.0 5.6 collective-permute-done.60
  574.6 15.2 %collective-permute-done.32 = bf16[1024,512]{1,0:T(8,128)(2,1)S(1)} collective-permute-done((bf16[1024,512]{1,0:T(8,128)(2,1)S(1)}, bf16[1024,512]{1,0:T(8,128)(2,1)S(1)}, u32[]{:S(2)}, u32[]{:S(2)}) %collective-permute-start.32) | collective-permute-done | bytes 1048608 | tf_op jit(solution)/shard_map/ppermute | solution.py:88
  596.3 9.6 %collective-permute-done.50 = bf16[2,256,512]{2,1,0:T(8,128)(2,1)S(1)} collective-permute-done((bf16[2,256,512]{2,1,0:T(8,128)(2,1)S(1)}, bf16[2,256,512]{2,1,0:T(8,128)(2,1)S(1)}, u32[]{:S(2)}, u32[]{:S(2)}) %collective-permute-start.50) | collective-permute-done | bytes 524320 | tf_op jit(solution)/shard_map/ppermute | solution.py:112
  (440 shorter events, 255.0 us)
Async XLA Ops:
  0.7 28.1 %collective-permute-start.1 = (bf16[1024,512]{1,0:T(8,128)(2,1)}, bf16[1024,512]{1,0:T(8,128)(2,1)S(1)}, u32[]{:S(2)}, u32[]{:S(2)}) collective-permute-start(bf16[1024,512]{1,0:T(8,128)(2,1)} %param.29), channel_id=1, source_target_pairs={{0,1},{1,2},{2,3},{3,0},{4,5},{5,6},{6,7},{7,4},{8,9},{9,10},{10,1... | collective-permute-start | bytes 3145736 | tf_op jit(solution)/shard_map/ppermute | solution.py:43
  2.3 47.7 %collective-permute-start = (bf16[1024,512]{1,0:T(8,128)(2,1)}, bf16[1024,512]{1,0:T(8,128)(2,1)S(1)}, u32[]{:S(2)}, u32[]{:S(2)}) collective-permute-start(bf16[1024,512]{1,0:T(8,128)(2,1)} %param.29), channel_id=1, source_target_pairs={{0,3},{1,0},{2,1},{3,2},{4,7},{5,4},{6,5},{7,6},{8,11},{9,8},{10,9... | collective-permute-start | bytes 3145736 | tf_op jit(solution)/shard_map/ppermute | solution.py:44
  4.5 55.3 %collective-permute-start.4 = (bf16[512]{0:T(512)(128)(2,1)}, bf16[512]{0:T(512)(128)(2,1)S(1)}, u32[]{:S(2)}, u32[]{:S(2)}) collective-permute-start(bf16[512]{0:T(512)(128)(2,1)} %param.30), channel_id=1, source_target_pairs={{0,3},{1,0},{2,1},{3,2},{4,7},{5,4},{6,5},{7,6},{8,11},{9,8},{10,9... | collective-permute-start | bytes 3080 | tf_op jit(solution)/shard_map/ppermute | solution.py:159
  6.3 53.6 %collective-permute-start.5 = (bf16[512]{0:T(512)(128)(2,1)}, bf16[512]{0:T(512)(128)(2,1)S(1)}, u32[]{:S(2)}, u32[]{:S(2)}) collective-permute-start(bf16[512]{0:T(512)(128)(2,1)} %param.30), channel_id=1, source_target_pairs={{0,2},{1,3},{2,0},{3,1},{4,6},{5,7},{6,4},{7,5},{8,10},{9,11},{10,... | collective-permute-start | bytes 3080 | tf_op jit(solution)/shard_map/ppermute | solution.py:159
  6.3 53.7 %collective-permute-start.6 = (bf16[512]{0:T(512)(128)(2,1)}, bf16[512]{0:T(512)(128)(2,1)S(1)}, u32[]{:S(2)}, u32[]{:S(2)}) collective-permute-start(bf16[512]{0:T(512)(128)(2,1)} %param.30), channel_id=1, source_target_pairs={{0,1},{1,2},{2,3},{3,0},{4,5},{5,6},{6,7},{7,4},{8,9},{9,10},{10,1... | collective-permute-start | bytes 3080 | tf_op jit(solution)/shard_map/ppermute | solution.py:159
  29.6 35.5 %collective-permute-start.2 = (bf16[512,512]{1,0:T(8,128)(2,1)}, bf16[512,512]{1,0:T(8,128)(2,1)}, u32[]{:S(2)}, u32[]{:S(2)}) collective-permute-start(bf16[512,512]{1,0:T(8,128)(2,1)} %slice.352), channel_id=1, source_target_pairs={{0,1},{1,2},{2,3},{3,0},{4,5},{5,6},{6,7},{7,4},{8,9},{9,10},{10,1... | collective-permute-start | bytes 1572872 | tf_op jit(solution)/shard_map/ppermute | solution.py:47
  117.1 49.9 %collective-permute-start.18 = (bf16[1024,512]{1,0:T(8,128)(2,1)S(1)}, bf16[1024,512]{1,0:T(8,128)(2,1)}, u32[]{:S(2)}, u32[]{:S(2)}) collective-permute-start(bf16[1024,512]{1,0:T(8,128)(2,1)S(1)} %copy-done.17), channel_id=1, source_target_pairs={{0,3},{1,0},{2,1},{3,2},{4,7},{5,4},{6,5},{7,6},{8,11},{9,8},{10,9... | collective-permute-start | bytes 3145736 | tf_op jit(solution)/shard_map/ppermute | solution.py:44
  118.8 46.4 %collective-permute-start.19 = (bf16[1024,512]{1,0:T(8,128)(2,1)S(1)}, bf16[1024,512]{1,0:T(8,128)(2,1)S(1)}, u32[]{:S(2)}, u32[]{:S(2)}) collective-permute-start(bf16[1024,512]{1,0:T(8,128)(2,1)S(1)} %copy-done.17), channel_id=1, source_target_pairs={{0,1},{1,2},{2,3},{3,0},{4,5},{5,6},{6,7},{7,4},{8,9},{9,10},{10,1... | collective-permute-start | bytes 3145736 | tf_op jit(solution)/shard_map/ppermute | solution.py:43
  126.6 45.9 %collective-permute-start.9 = (f32[136,1024]{1,0:T(8,128)S(1)}, f32[136,1024]{1,0:T(8,128)S(1)}, u32[]{:S(2)}, u32[]{:S(2)}) collective-permute-start(f32[136,1024]{1,0:T(8,128)S(1)} %pad_maximum_fusion.2), channel_id=1, source_target_pairs={{0,8},{4,12},{8,0},{12,4},{16,24},{20,28},{24,16},{28,20},{1,9},{5... | collective-permute-start | bytes 1671176 | tf_op jit(solution)/shard_map/ppermute | solution.py:141
  259.9 159.0 %collective-permute-start.69 = (bf16[2,2,256,1024]{3,2,1,0:T(8,128)(2,1)}, bf16[2,2,256,1024]{3,2,1,0:T(8,128)(2,1)}, u32[]{:S(2)}, u32[]{:S(2)}) collective-permute-start(bf16[2,2,256,1024]{3,2,1,0:T(8,128)(2,1)} %dynamic-slice_bitcast_fusion), channel_id=1, source_target_pairs={{0,4},{4,0},{8,12},{12,8},{16,20},{20,16},{24,28},{28,24},{1,5},{5... | collective-permute-start | bytes 6291464 | tf_op jit(solution)/shard_map/ppermute | solution.py:112
  261.8 24.2 %collective-permute-start.14 = (bf16[512,512]{1,0:T(8,128)(2,1)}, bf16[512,512]{1,0:T(8,128)(2,1)}, u32[]{:S(2)}, u32[]{:S(2)}) collective-permute-start(bf16[512,512]{1,0:T(8,128)(2,1)} %get-tuple-element.160), channel_id=1, source_target_pairs={{0,1},{1,2},{2,3},{3,0},{4,5},{5,6},{6,7},{7,4},{8,9},{9,10},{10,1... | collective-permute-start | bytes 1572872 | tf_op jit(solution)/shard_map/ppermute | solution.py:74
  262.7 25.8 %collective-permute-start.16 = (bf16[512,512]{1,0:T(8,128)(2,1)}, bf16[512,512]{1,0:T(8,128)(2,1)}, u32[]{:S(2)}, u32[]{:S(2)}) collective-permute-start(bf16[512,512]{1,0:T(8,128)(2,1)} %get-tuple-element.161), channel_id=1, source_target_pairs={{0,3},{1,0},{2,1},{3,2},{4,7},{5,4},{6,5},{7,6},{8,11},{9,8},{10,9... | collective-permute-start | bytes 1572872 | tf_op jit(solution)/shard_map/ppermute | solution.py:75
  277.6 148.0 %collective-permute-start.42 = (bf16[2,2,256,1024]{3,2,1,0:T(8,128)(2,1)}, bf16[2,2,256,1024]{3,2,1,0:T(8,128)(2,1)}, u32[]{:S(2)}, u32[]{:S(2)}) collective-permute-start(bf16[2,2,256,1024]{3,2,1,0:T(8,128)(2,1)} %dynamic-slice_bitcast_fusion.2), channel_id=1, source_target_pairs={{0,4},{4,0},{8,12},{12,8},{16,20},{20,16},{24,28},{28,24},{1,5},{5... | collective-permute-start | bytes 6291464 | tf_op jit(solution)/shard_map/ppermute | solution.py:112
  409.9 44.4 %collective-permute-start.52 = (f32[2,2,256,256]{3,2,1,0:T(8,128)}, f32[2,2,256,256]{3,2,1,0:T(8,128)}, u32[]{:S(2)}, u32[]{:S(2)}) collective-permute-start(f32[2,2,256,256]{3,2,1,0:T(8,128)} %dynamic-slice_bitcast_fusion.3), channel_id=1, source_target_pairs={{0,4},{4,0},{8,12},{12,8},{16,20},{20,16},{24,28},{28,24},{1,5},{5... | collective-permute-start | bytes 3145736 | tf_op jit(solution)/shard_map/ppermute | solution.py:112
  411.1 159.3 %collective-permute-start.47 = (bf16[2,2,256,1024]{3,2,1,0:T(8,128)(2,1)}, bf16[2,2,256,1024]{3,2,1,0:T(8,128)(2,1)}, u32[]{:S(2)}, u32[]{:S(2)}) collective-permute-start(bf16[2,2,256,1024]{3,2,1,0:T(8,128)(2,1)} %dynamic-slice_bitcast_fusion.1), channel_id=1, source_target_pairs={{0,4},{4,0},{8,12},{12,8},{16,20},{20,16},{24,28},{28,24},{1,5},{5... | collective-permute-start | bytes 6291464 | tf_op jit(solution)/shard_map/ppermute | solution.py:112
  454.3 27.0 %collective-permute-start.44 = (bf16[256,512]{1,0:T(8,128)(2,1)S(1)}, bf16[256,512]{1,0:T(8,128)(2,1)S(1)}, u32[]{:S(2)}, u32[]{:S(2)}) collective-permute-start(bf16[256,512]{1,0:T(8,128)(2,1)S(1)} %dynamic-slice_bitcast_fusion.17), channel_id=1, source_target_pairs={{0,16},{4,20},{8,24},{12,28},{16,0},{20,4},{24,8},{28,12},{1,17},{... | collective-permute-start | bytes 786440 | tf_op jit(solution)/shard_map/ppermute | solution.py:112
  461.3 48.8 %collective-permute-start.46 = (bf16[256,512]{1,0:T(8,128)(2,1)S(1)}, bf16[256,512]{1,0:T(8,128)(2,1)S(1)}, u32[]{:S(2)}, u32[]{:S(2)}) collective-permute-start(bf16[256,512]{1,0:T(8,128)(2,1)S(1)} %dynamic-slice_bitcast_fusion.16), channel_id=1, source_target_pairs={{0,8},{4,12},{8,0},{12,4},{16,24},{20,28},{24,16},{28,20},{1,9},{5... | collective-permute-start | bytes 786440 | tf_op jit(solution)/shard_map/ppermute | solution.py:112
  481.4 25.3 %collective-permute-start.56 = (f32[64,256]{1,0:T(8,128)S(1)}, f32[64,256]{1,0:T(8,128)S(1)}, u32[]{:S(2)}, u32[]{:S(2)}) collective-permute-start(f32[64,256]{1,0:T(8,128)S(1)} %get-tuple-element.188), channel_id=1, source_target_pairs={{0,2},{1,3},{2,0},{3,1},{4,6},{5,7},{6,4},{7,5},{8,10},{9,11},{10,... | collective-permute-start | bytes 196616 | tf_op jit(solution)/shard_map/ppermute | solution.py:176
  481.4 25.6 %collective-permute-start.57 = (f32[64,256]{1,0:T(8,128)S(1)}, f32[64,256]{1,0:T(8,128)S(1)}, u32[]{:S(2)}, u32[]{:S(2)}) collective-permute-start(f32[64,256]{1,0:T(8,128)S(1)} %get-tuple-element.187), channel_id=1, source_target_pairs={{0,3},{1,0},{2,1},{3,2},{4,7},{5,4},{6,5},{7,6},{8,11},{9,8},{10,9... | collective-permute-start | bytes 196616 | tf_op jit(solution)/shard_map/ppermute | solution.py:176
  487.6 85.4 %collective-permute-start.15 = (bf16[1024,512]{1,0:T(8,128)(2,1)S(1)}, bf16[1024,512]{1,0:T(8,128)(2,1)S(1)}, u32[]{:S(2)}, u32[]{:S(2)}) collective-permute-start(bf16[1024,512]{1,0:T(8,128)(2,1)S(1)} %copy-done.25), channel_id=1, source_target_pairs={{0,1},{1,2},{2,3},{3,0},{4,5},{5,6},{6,7},{7,4},{8,9},{9,10},{10,1... | collective-permute-start | bytes 3145736 | tf_op jit(solution)/shard_map/ppermute | solution.py:87
  506.7 67.9 %collective-permute-start.17 = (bf16[1024,512]{1,0:T(8,128)(2,1)S(1)}, bf16[1024,512]{1,0:T(8,128)(2,1)S(1)}, u32[]{:S(2)}, u32[]{:S(2)}) collective-permute-start(bf16[1024,512]{1,0:T(8,128)(2,1)S(1)} %copy-done.26), channel_id=1, source_target_pairs={{0,3},{1,0},{2,1},{3,2},{4,7},{5,4},{6,5},{7,6},{8,11},{9,8},{10,9... | collective-permute-start | bytes 3145736 | tf_op jit(solution)/shard_map/ppermute | solution.py:88
  507.0 67.6 %collective-permute-start.30 = (bf16[1024,512]{1,0:T(8,128)(2,1)S(1)}, bf16[1024,512]{1,0:T(8,128)(2,1)S(1)}, u32[]{:S(2)}, u32[]{:S(2)}) collective-permute-start(bf16[1024,512]{1,0:T(8,128)(2,1)S(1)} %convert_element_type.168), channel_id=1, source_target_pairs={{0,1},{1,2},{2,3},{3,0},{4,5},{5,6},{6,7},{7,4},{8,9},{9,10},{10,1... | collective-permute-start | bytes 3145736 | tf_op jit(solution)/shard_map/ppermute | solution.py:87
  510.1 42.2 %collective-permute-start.58 = (bf16[64,256]{1,0:T(8,128)(2,1)S(1)}, bf16[64,256]{1,0:T(8,128)(2,1)S(1)}, u32[]{:S(2)}, u32[]{:S(2)}) collective-permute-start(bf16[64,256]{1,0:T(8,128)(2,1)S(1)} %get-tuple-element.151), channel_id=1, source_target_pairs={{0,3},{1,0},{2,1},{3,2},{4,7},{5,4},{6,5},{7,6},{8,11},{9,8},{10,9... | collective-permute-start | bytes 98312 | tf_op jit(solution)/shard_map/ppermute | solution.py:159
  570.4 24.1 %collective-permute-start.62 = (bf16[2,256,256]{2,1,0:T(8,128)(2,1)S(1)}, bf16[2,256,256]{2,1,0:T(8,128)(2,1)S(1)}, u32[]{:S(2)}, u32[]{:S(2)}) collective-permute-start(bf16[2,256,256]{2,1,0:T(8,128)(2,1)S(1)} %pad_maximum_fusion.7), channel_id=1, source_target_pairs={{0,8},{4,12},{8,0},{12,4},{16,24},{20,28},{24,16},{28,20},{1,9},{5... | collective-permute-start | bytes 786440 | tf_op jit(solution)/shard_map/ppermute | solution.py:180
  (97 other events, 1218.2 us)

commit v3 on v2

--- a/solution.py
+++ b/solution.py
@@ -1,3 +1,5 @@
+import functools
+
 import jax
 import jax.numpy as jnp
 from jax import lax
@@ -14,12 +16,6 @@
 epsilon = 1e-05
 
 
-def shifted(value, axis, steps):
-    count = lax.axis_size(axis)
-    leading, last = (max(0, -steps), min(count, count - steps))
-    return lax.ppermute(value, axis, [(source, source + steps) for source in range(leading, last)])
-
-
 def rotation(count, steps):
     return [(source, (source + steps) % count) for source in range(count)]
 
@@ -32,7 +28,42 @@
     return count.bit_length() - 1
 
 
-def gather_blocks(block, axis):
+class Chain:
+    def __init__(self, gen):
+        self.gen = gen
+        self.result = None
+        self.sends = None
+        self.step(None)
+
+    def step(self, moved):
+        try:
+            self.sends = self.gen.send(moved)
+        except StopIteration as stop:
+            self.sends, self.result = None, stop.value
+
+
+def phase(chains, work=None, *inputs):
+    chains = [chain for chain in chains if chain.sends is not None]
+    values = [[send[0] for send in chain.sends] for chain in chains]
+    values, inputs = lax.optimization_barrier((values, inputs))
+    moved = [
+        [lax.ppermute(value, send[1], send[2]) for value, send in zip(group, chain.sends)]
+        for group, chain in zip(values, chains)
+    ]
+    outs = work(*inputs) if work is not None else ()
+    moved, outs = lax.optimization_barrier((moved, outs))
+    for chain, group in zip(chains, moved):
+        chain.step(group)
+    return outs
+
+
+def finish(*chains):
+    while any(chain.sends is not None for chain in chains):
+        phase(chains)
+    return [chain.result for chain in chains]
+
+
+def gather_chain(block, axis):
     count = lax.axis_size(axis)
     half = count // 2
     rows = block.shape[0] // 2
@@ -40,27 +71,25 @@
     found[0] = block
     left = right = block
     for step in range(1, half):
-        left = lax.ppermute(left, axis, rotation(count, 1))
-        right = lax.ppermute(right, axis, rotation(count, -1))
+        left, right = yield [(left, axis, rotation(count, 1)), (right, axis, rotation(count, -1))]
         found[count - step] = left
         found[step] = right
-    far_low = lax.ppermute(left[:rows], axis, rotation(count, 1))
-    far_high = lax.ppermute(right[rows:], axis, rotation(count, -1))
-    found[half] = jnp.concatenate([far_low, far_high], axis=0)
+    low, high = yield [(left[:rows], axis, rotation(count, 1)), (right[rows:], axis, rotation(count, -1))]
+    found[half] = jnp.concatenate([low, high], axis=0)
     return found
 
 
-def gather_columns(block, axis):
-    count = lax.axis_size(axis)
+def place_columns(found, axis):
+    count = len(found)
     me = lax.axis_index(axis)
-    width = block.shape[1]
-    whole = jnp.zeros((block.shape[0], count * width), block.dtype)
-    for step, piece in enumerate(gather_blocks(block, axis)):
+    width = found[0].shape[1]
+    whole = jnp.zeros((found[0].shape[0], count * width), found[0].dtype)
+    for step, piece in enumerate(found):
         whole = lax.dynamic_update_slice_in_dim(whole, piece, (me + step) % count * width, 1)
     return whole
 
 
-def scatter_columns(whole, axis):
+def scatter_chain(whole, axis, pieces=1):
     count = lax.axis_size(axis)
     me = lax.axis_index(axis)
     half = count // 2
@@ -71,119 +100,149 @@
         return lax.dynamic_slice_in_dim(whole, (me + step) % count * width, width, 1)
 
     far = part(half)
-    ahead = lax.ppermute(far[:rows].astype(jnp.bfloat16), axis, rotation(count, 1))
-    behind = lax.ppermute(far[rows:].astype(jnp.bfloat16), axis, rotation(count, -1))
-    first = True
+    ahead, behind = yield [(far[:rows], axis, rotation(count, 1)), (far[rows:], axis, rotation(count, -1))]
     for step in range(half - 1, 0, -1):
         up = part(step).astype(jnp.float32)
         down = part(count - step).astype(jnp.float32)
-        if first:
+        if step == half - 1:
             up = up.at[:rows].add(ahead.astype(jnp.float32))
             down = down.at[rows:].add(behind.astype(jnp.float32))
-            first = False
         else:
             up = up + ahead.astype(jnp.float32)
             down = down + behind.astype(jnp.float32)
-        ahead = lax.ppermute(up.astype(jnp.bfloat16), axis, rotation(count, 1))
-        behind = lax.ppermute(down.astype(jnp.bfloat16), axis, rotation(count, -1))
+        arrived = []
+        cuts = [2 * rows * cut // (16 * pieces) * 16 for cut in range(pieces + 1)]
+        for begin, end in zip(cuts, cuts[1:]):
+            arrived.append(
+                (yield [
+                    (up[begin:end].astype(jnp.bfloat16), axis, rotation(count, 1)),
+                    (down[begin:end].astype(jnp.bfloat16), axis, rotation(count, -1)),
+                ])
+            )
+        ahead, behind = [jnp.concatenate(side, axis=0) if pieces > 1 else side[0] for side in zip(*arrived)]
     return part(0).astype(jnp.float32) + ahead.astype(jnp.float32) + behind.astype(jnp.float32)
 
 
-def small_sum(value, axis):
+def sum_chain(value, axis):
     count = lax.axis_size(axis)
-    total = value
-    for step in range(1, count):
-        total = total + lax.ppermute(value, axis, rotation(count, step))
-    return total
-
-
-def doubled_sum(value, axis):
-    count = lax.axis_size(axis)
-    for bit in range(bits_of(count)):
-        value = value + lax.ppermute(value, axis, flips(count, bit))
+    moved = yield [(value, axis, rotation(count, step)) for step in range(1, count)]
+    for other in moved:
+        value = value + other
     return value
 
 
-def halve(value, axis, bit, position):
-    count = lax.axis_size(axis)
+def split_half(value, axis, bit, position):
     mine = (lax.axis_index(axis) >> bit) & 1
     kept = lax.dynamic_index_in_dim(value, mine, position, False)
     sent = lax.dynamic_index_in_dim(value, 1 - mine, position, False)
-    return kept + lax.ppermute(sent, axis, flips(count, bit))
-
-
-def scatter_rows(value, axis):
+    return kept, (sent, axis, flips(lax.axis_size(axis), bit))
+
+
+def rows_chain(value, axis):
     count = lax.axis_size(axis)
     bits = bits_of(count)
     rows, columns = value.shape
     split = value.reshape((2,) * bits + (rows // count, columns))
-    split = halve(split, axis, 0, bits - 1)
-    parts = []
-    for piece in range(2):
-        half = split[..., piece * (columns // 2) : (piece + 1) * (columns // 2)]
-        left = list(range(bits - 1, 0, -1))
-        order = list(range(1, bits)) if piece == 0 else list(range(bits - 1, 0, -1))
-        for bit in order:
-            half = halve(half, axis, bit, left.index(bit))
-            left.remove(bit)
-        parts.append(half)
+    kept, send = split_half(split, axis, 0, bits - 1)
+    (moved,) = yield [send]
+    split = kept + moved
+    parts = [split[..., : columns // 2], split[..., columns // 2 :]]
+    orders = [list(range(1, bits)), list(range(bits - 1, 0, -1))]
+    left = [list(range(bits - 1, 0, -1)) for _ in parts]
+    for turn in range(bits - 1):
+        keeps, sends = [], []
+        for piece in range(2):
+            bit = orders[piece][turn]
+            kept, send = split_half(parts[piece], axis, bit, left[piece].index(bit))
+            left[piece].remove(bit)
+            keeps.append(kept)
+            sends.append(send)
+        moved = yield sends
+        parts = [kept + other for kept, other in zip(keeps, moved)]
     return jnp.concatenate(parts, axis=1).astype(jnp.float32)
 
 
-def prefix_state(passing, state, axis, reverse):
+def state_chain(total, reverse):
+    count = lax.axis_size("seq")
+    me = lax.axis_index("seq")
+    chips = count // 2
+    chip, core = me // 2, me % 2
+    (neighbour,) = yield [(total, "seq", flips(count, 0))]
+    half = chip_state(total, neighbour, core, reverse)
+    parts = yield [
+        (half, "seq", [(source, source ^ (2 * step)) for source in range(count)]) for step in range(1, chips)
+    ]
+    entering = entering_state(chip, chips, reverse, parts)
+    (other,) = yield [(entering, "seq", flips(count, 0))]
+    return core_state(entering, other, neighbour, core, reverse)
+
+
+def all_chain(value, axis):
     count = lax.axis_size(axis)
     me = lax.axis_index(axis)
-    depth = state.shape[0]
-    total = jnp.concatenate([state, jnp.broadcast_to(passing, (8, state.shape[1]))], axis=0)
-    prefix = jnp.zeros_like(state)
-    prefix_pass = jnp.ones_like(passing)
-    for bit in range(bits_of(count)):
-        other = lax.ppermute(total, axis, flips(count, bit))
-        upper = ((me >> bit) & 1) == 1
-        other_first = jnp.logical_not(upper) if reverse else upper
-        other_state, other_pass = other[:depth], other[depth : depth + 1]
-        total_state, total_pass = total[:depth], total[depth : depth + 1]
-        prefix = jnp.where(other_first, prefix_pass * other_state + prefix, prefix)
-        prefix_pass = jnp.where(other_first, prefix_pass * other_pass, prefix_pass)
-        if bit < bits_of(count) - 1:
-            joined = jnp.where(other_first, total_pass * other_state + total_state, other_pass * total_state + other_state)
-            total = jnp.concatenate([joined, jnp.broadcast_to(total_pass * other_pass, (8, state.shape[1]))], axis=0)
-    return prefix
-
-
-def gather_small(value, axis):
-    count = lax.axis_size(axis)
-    me = lax.axis_index(axis)
+    moved = yield [(value, axis, rotation(count, -step)) for step in range(1, count)]
     whole = jnp.zeros((count,) + value.shape, value.dtype)
-    for step in range(count):
-        piece = value if step == 0 else lax.ppermute(value, axis, rotation(count, -step))
+    for step, piece in enumerate([value] + list(moved)):
         whole = lax.dynamic_update_index_in_dim(whole, piece, (me + step) % count, 0)
     return whole
 
 
-def sum_everywhere(value):
-    count, heads = lax.axis_size("seq"), lax.axis_size("head")
-    bits = bits_of(count)
+def parts_of(value):
+    high = lax.reduce_precision(value, 8, 7)
+    return high.astype(jnp.bfloat16), (value - high).astype(jnp.bfloat16)
+
+
+def shared_chain(value, flat, holder):
+    count = lax.axis_size("seq")
+    me = lax.axis_index("seq")
     rows, columns = value.shape
-    split = value.reshape((2,) * bits + (rows // count, columns))
-    for bit in range(bits):
-        split = halve(split, "seq", bit, bits - 1 - bit)
-    blocks = split.reshape(heads, rows // count // heads, columns)
-    me = lax.axis_index("head")
-    total = lax.dynamic_index_in_dim(blocks, me, 0, False)
-    for step in range(1, heads):
-        sent = lax.dynamic_index_in_dim(blocks, (me + step) % heads, 0, False)
-        total = total + lax.ppermute(sent, "head", rotation(heads, step))
-    whole = gather_small(total.astype(jnp.bfloat16), "head").reshape(rows // count, columns)
-    place = lax.axis_index("seq")
-    for bit in range(bits - 1, -1, -1):
-        other = lax.ppermute(whole, "seq", flips(count, bit))
-        upper = ((place >> bit) & 1) == 1
-        low = jnp.where(upper, other, whole)
-        high = jnp.where(upper, whole, other)
-        whole = jnp.stack([low, high])
-    order = list(range(bits - 1, -1, -1)) + [bits, bits + 1]
-    return whole.transpose(order).reshape(rows, columns).astype(jnp.float32)
+    chips = count // 2
+    block = rows // count
+    chip, core = me // 2, me % 2
+    kept, send = split_half(value.reshape(chips, 2, block, columns), "seq", 0, 1)
+    moved, flat_moved = yield [send, (flat, "seq", flips(count, 0))]
+    own = kept + moved
+    flat = flat + flat_moved
+    flat_parts = parts_of(flat)
+    depth = flat.shape[0]
+
+    def chip_pairs(step):
+        return [(source, source ^ (2 * step)) for source in range(count)]
+
+    steps = range(1, chips)
+    outgoing = [
+        jnp.concatenate([lax.dynamic_index_in_dim(own, chip ^ step, 0, False).astype(jnp.bfloat16), *flat_parts], axis=0)
+        for step in steps
+    ]
+    moved = yield [(part, "seq", chip_pairs(step)) for part, step in zip(outgoing, steps)]
+    own = lax.dynamic_index_in_dim(own, chip, 0, False)
+    held = jnp.zeros((chips, 2 * depth, columns), jnp.bfloat16)
+    held = lax.dynamic_update_index_in_dim(held, jnp.concatenate(flat_parts, axis=0), chip, 0)
+    for step, other in zip(steps, moved):
+        own = own + other[:block].astype(jnp.float32)
+        held = lax.dynamic_update_index_in_dim(held, other[block:], chip ^ step, 0)
+    held = held.astype(jnp.float32)
+    flat = jnp.sum(held[:, :depth] + held[:, depth:], axis=0)
+    pieces = yield from all_chain(jnp.concatenate([own.astype(jnp.bfloat16), *parts_of(flat)], axis=0), "head")
+    mine = jnp.sum(pieces[:, :block].astype(jnp.float32), axis=0).astype(jnp.bfloat16)
+    copies = pieces[:, block:].astype(jnp.float32)
+    copies = copies[:, :depth] + copies[:, depth:]
+    holder.append(copies)
+    moved = yield [(mine, "seq", chip_pairs(step)) for step in steps]
+    found = jnp.zeros((chips,) + mine.shape, mine.dtype)
+    for step, piece in zip(range(chips), [mine] + list(moved)):
+        found = lax.dynamic_update_index_in_dim(found, piece, chip ^ step, 0)
+    (moved,) = yield [(found, "seq", flips(count, 0))]
+    low = jnp.where(core == 0, found, moved)
+    high = jnp.where(core == 0, moved, found)
+    return jnp.stack([low, high], axis=1).astype(jnp.float32).reshape(rows, columns)
+
+
+def shift_chain(value, axis, steps):
+    count = lax.axis_size(axis)
+    leading, last = (max(0, -steps), min(count, count - steps))
+    (moved,) = yield [(value, axis, [(source, source + steps) for source in range(leading, last)])]
+    return moved
 
 
 def dot(a, b, dims=(((1,), (0,)), ((), ()))):
@@ -316,9 +375,14 @@
     passing = enter_e[rows - 1 : rows]
     new = passing * old + dot(writers, (weighted * toward_e).astype(jnp.bfloat16), FIRST)
     state[...] = new
-    final_out[...] = new
     entry_out[0] = carried[...]
-    carried[...] = carried[...] * entering[rows - 1 : rows]
+    through = carried[...] * entering[rows - 1 : rows]
+    carried[...] = through
+
+    @pl.when(pl.program_id(0) == pl.num_programs(0) - 1)
+    def last():
+        final_out[0:STATE, :] = new
+        final_out[STATE : STATE + 8, :] = spread_heads(jnp.broadcast_to(through, (8, heads)), expand[...])
 
 
 def vmem(limit=56):
@@ -344,7 +408,7 @@
             rows2(inner), rows2(STATE), rows2(heads),
             pl.BlockSpec((1, 1, heads), lambda c: (c, 0, 0)),
             pl.BlockSpec((1, STATE, inner), lambda c: (c, 0, 0)),
-            pl.BlockSpec((STATE, inner), lambda c: (0, 0)),
+            pl.BlockSpec((STATE + 8, inner), lambda c: (0, 0)),
         ],
         out_shape=[
             jax.ShapeDtypeStruct((length, inner), jnp.float32),
@@ -352,7 +416,7 @@
             jax.ShapeDtypeStruct((length, heads), jnp.float32),
             jax.ShapeDtypeStruct((blocks, 1, heads), jnp.float32),
             jax.ShapeDtypeStruct((blocks, STATE, inner), jnp.float32),
-            jax.ShapeDtypeStruct((STATE, inner), jnp.float32),
+            jax.ShapeDtypeStruct((STATE + 8, inner), jnp.float32),
         ],
         scratch_shapes=[
             pltpu.VMEM((SPAN + 8, inner), jnp.float32),
@@ -387,7 +451,7 @@
     )(local, readers, run, gate_in, incoming, expand)
 
 
-def norm_cot_kernel(upstream, readout, full, gate_in, inverse, postnorm, norm_cot, inner_sum, gain_sum):
+def norm_cot_kernel(upstream, readout, full, gate_in, inverse, postnorm, norm_cot, normalized, inner_sum, gain_sum):
     @pl.when(pl.program_id(0) == 0)
     def start():
         gain_sum[...] = jnp.zeros_like(gain_sum)
@@ -395,7 +459,9 @@
     cot = dot(upstream[...], readout[...])
     norm_cot[...] = cot
     gate = gate_in[...]
-    product = cot * (full[...] * gate * jax.nn.sigmoid(gate) * inverse[...])
+    unit = full[...] * gate * jax.nn.sigmoid(gate) * inverse[...]
+    normalized[...] = (unit * postnorm[...]).astype(jnp.bfloat16)
+    product = cot * unit
     gain_sum[...] += jnp.sum(product.reshape(-1, 8, product.shape[1]), axis=0)
     inner_sum[...] = jnp.sum(product * postnorm[...], axis=1, keepdims=True)
 
@@ -407,9 +473,10 @@
         norm_cot_kernel,
         grid=(length // BLOCK,),
         in_specs=[rows2(upstream.shape[1]), whole_spec(readout), rows2(inner), rows2(inner), rows2(1), whole_spec(postnorm)],
-        out_specs=[rows2(inner), rows2(1), pl.BlockSpec((8, inner), lambda c: (0, 0))],
+        out_specs=[rows2(inner), rows2(inner), rows2(1), pl.BlockSpec((8, inner), lambda c: (0, 0))],
         out_shape=[
             jax.ShapeDtypeStruct((length, inner), jnp.float32),
+            jax.ShapeDtypeStruct((length, inner), jnp.bfloat16),
             jax.ShapeDtypeStruct((length, 1), jnp.float32),
             jax.ShapeDtypeStruct((8, inner), jnp.float32),
         ],
@@ -417,10 +484,11 @@
     )(upstream, readout, full, gate_in, inverse, postnorm)
 
 
-def gate_kernel(norm_cot, full_in, gate_in, inverse, mean, postnorm, run, readers, expand, full_cot, gate_low, pending):
+def gate_kernel(norm_cot, full_in, gate_in, inverse, mean, postnorm, run, readers, expand, final, full_cot, gate_low, pending):
     @pl.when(pl.program_id(0) == 0)
     def start():
-        pending[...] = jnp.zeros_like(pending)
+        pending[0:STATE, :] = jnp.zeros((STATE, pending.shape[1]), jnp.float32)
+        pending[STATE : STATE + 8, :] = final[STATE : STATE + 8, :]
 
     gate, full = gate_in[...], full_in[...]
     sigmoid = jax.nn.sigmoid(gate)
@@ -432,26 +500,25 @@
     full_cot[...] = cot
     gate_low[...] = (gated_cot * full * sigmoid * (1.0 + gate * (1.0 - sigmoid))).astype(jnp.bfloat16)
     run_e = spread_heads(run[...], expand[...])
-    high, rest = halves(cot * run_e)
-    pending[...] += dot(readers[...], high, FIRST)
-
-
-def gate_cotangent(norm_cot, full, gate_in, inverse, mean, postnorm, run, readers, expand):
+    pending[0:STATE, :] += dot(readers[...], (cot * run_e).astype(jnp.bfloat16), FIRST)
+
+
+def gate_cotangent(norm_cot, full, gate_in, inverse, mean, postnorm, run, readers, expand, final):
     length, inner = full.shape
     heads = run.shape[1]
     rows2 = lambda width: pl.BlockSpec((BLOCK, width), lambda c: (c, 0))
     return pl.pallas_call(
         gate_kernel,
         grid=(length // BLOCK,),
-        in_specs=[rows2(inner), rows2(inner), rows2(inner), rows2(1), rows2(1), whole_spec(postnorm), rows2(heads), rows2(STATE), whole_spec(expand)],
-        out_specs=[rows2(inner), rows2(inner), pl.BlockSpec((STATE, inner), lambda c: (0, 0))],
+        in_specs=[rows2(inner), rows2(inner), rows2(inner), rows2(1), rows2(1), whole_spec(postnorm), rows2(heads), rows2(STATE), whole_spec(expand), whole_spec(final)],
+        out_specs=[rows2(inner), rows2(inner), pl.BlockSpec((STATE + 8, inner), lambda c: (0, 0))],
         out_shape=[
             jax.ShapeDtypeStruct((length, inner), jnp.float32),
             jax.ShapeDtypeStruct((length, inner), jnp.bfloat16),
-            jax.ShapeDtypeStruct((STATE, inner), jnp.float32),
+            jax.ShapeDtypeStruct((STATE + 8, inner), jnp.float32),
         ],
         compiler_params=vmem(),
-    )(norm_cot, full, gate_in, inverse, mean, postnorm, run, readers, expand)
+    )(norm_cot, full, gate_in, inverse, mean, postnorm, run, readers, expand, final)
 
 
 def silu_slope(pre, sigmoid):
@@ -472,11 +539,11 @@
 
 
 def backward_kernel(
+    opening,
     proj, shared, before_v, before_s, dt, seg_col, seg_row, full_cot, states, entry,
-    edge_v, edge_s, taps, offset, filters, baseline, timing, damping, skip, expand, incoming, leaving, after_v, after_s,
-    values_low, shared_low, dt_low, tap_sum, offset_sum, filter_sum, base_sum, timing_sum, damping_sum, direct_sum,
-    tail_v, tail_s, head_v, head_s,
-    ext_v, ext_s, later_v, later_s, lam,
+    edge_v, edge_s, taps, offset, filters, baseline, timing, damping, skip, expand, incoming, leaving, after_v, after_s, sums_in,
+    values_low, shared_low, dt_low, sums_out, head_v, head_s, lam_out,
+    ext_v, ext_s, later_v, later_s, lam, tap_sum, offset_sum, filter_sum, base_sum, timing_sum, damping_sum, direct_sum,
 ):
     rows, heads = dt.shape
     step_index = pl.program_id(0)
@@ -490,15 +557,14 @@
         for item in (tap_sum, offset_sum, filter_sum, base_sum, timing_sum, damping_sum, direct_sum):
             item[...] = jnp.zeros_like(item)
 
-    @pl.when(step_index == blocks - 1)
-    def first_block():
-        ext_v[0:8, :] = edge_v[...]
-        ext_s[0:8, :] = edge_s[...]
-
-    @pl.when(step_index < blocks - 1)
-    def other_block():
-        ext_v[0:8, :] = before_v[...]
-        ext_s[0:8, :] = before_s[...]
+    ext_v[0:8, :] = before_v[...]
+    ext_s[0:8, :] = before_s[...]
+    if opening:
+
+        @pl.when(step_index == blocks - 1)
+        def first_block():
+            ext_v[0:8, :] = edge_v[...]
+            ext_s[0:8, :] = edge_s[...]
 
     ext_v[8 : 8 + rows, :] = proj[...]
     ext_s[8 : 8 + rows, :] = shared[...]
@@ -606,75 +672,95 @@
     later_v[rows : rows + 8, :] = later_v[0:8, :]
     later_s[rows : rows + 8, :] = later_s[0:8, :]
 
-    @pl.when(step_index == 0)
-    def tail():
-        tail_v[...] = values_cot[rows - 8 :, :]
-        tail_s[...] = shared_cot[rows - 8 :, :]
-
     @pl.when(step_index == blocks - 1)
     def head():
         head_v[...] = pre_cot[0:8, :]
         head_s[...] = pre_cot_c[0:8, :]
+        lam_out[...] = lam[...]
+        sums_out[...] = sums_in[...]
+        total = lambda value: jnp.sum(value, axis=0, keepdims=True)
+        for tap in range(count):
+            sums_out[tap : tap + 1, :] += total(tap_sum[tap])
+            sums_out[count + 2 + tap : count + 3 + tap, : 2 * STATE] += total(filter_sum[tap])
+        sums_out[count : count + 1, :] += total(offset_sum[...])
+        sums_out[count + 1 : count + 2, :] += total(direct_sum[...])
+        sums_out[2 * count + 2 : 2 * count + 3, : 2 * STATE] += total(base_sum[...])
+        sums_out[2 * count + 3 : 2 * count + 4, :heads] += total(timing_sum[...])
+        sums_out[2 * count + 4 : 2 * count + 5, :heads] += total(damping_sum[...])
 
 
 def backward_scan(
     proj, shared, dt, seg_col, seg_row, full_cot, states, entry,
-    edge_v, edge_s, taps, offset, filters, baseline, timing, damping, skip, expand, incoming, leaving, after_v, after_s,
+    edge_v, edge_s, taps, offset, filters, baseline, timing, damping, skip, expand, incoming, leaving, after_v, after_s, sums, base, blocks,
 ):
-    length, inner = proj.shape
+    inner = proj.shape[1]
+    length = blocks * SPAN
     heads = dt.shape[1]
-    blocks = length // SPAN
     count = taps.shape[0]
-    back = lambda c: blocks - 1 - c
+    back = lambda c: base + blocks - 1 - c
+    own = lambda width: pl.BlockSpec((SPAN, width), lambda c: (blocks - 1 - c, 0))
     rows2 = lambda width: pl.BlockSpec((SPAN, width), lambda c: (back(c), 0))
     before = lambda width: pl.BlockSpec((8, width), lambda c: (jnp.maximum(back(c) * (SPAN // 8) - 1, 0), 0))
     lead = lambda *shape: pl.BlockSpec((1,) + shape, lambda c: (back(c), 0, 0))
-    fixed = (edge_v, edge_s, taps, offset, filters, baseline, timing, damping, skip, expand, incoming, leaving, after_v, after_s)
+    fixed = (edge_v, edge_s, taps, offset, filters, baseline, timing, damping, skip, expand, incoming, leaving, after_v, after_s, sums)
     f32 = lambda *shape: jax.ShapeDtypeStruct(shape, jnp.float32)
-    sums = [f32(count, 8, inner), f32(8, inner), f32(count, 8, 2 * STATE), f32(8, 2 * STATE), f32(8, heads), f32(8, heads), f32(8, inner), f32(8, inner), f32(8, 2 * STATE), f32(8, inner), f32(8, 2 * STATE)]
+    carried = [f32(*sums.shape), f32(8, inner), f32(8, 2 * STATE), f32(STATE, inner)]
     low = lambda width: jax.ShapeDtypeStruct((length, width), jnp.bfloat16)
     return pl.pallas_call(
-        backward_kernel,
+        functools.partial(backward_kernel, base == 0),
         grid=(blocks,),
         in_specs=[rows2(inner), rows2(2 * STATE), before(inner), before(2 * STATE), rows2(heads), rows2(1), lead(1, SPAN), rows2(inner), lead(STATE, inner), lead(1, heads)]
         + [whole_spec(a) for a in fixed],
-        out_specs=[rows2(inner), rows2(2 * STATE), rows2(heads)] + [whole_spec(a) for a in sums],
-        out_shape=[low(inner), low(2 * STATE), low(heads)] + sums,
+        out_specs=[own(inner), own(2 * STATE), own(heads)] + [whole_spec(a) for a in carried],
+        out_shape=[low(inner), low(2 * STATE), low(heads)] + carried,
         scratch_shapes=[
             pltpu.VMEM((SPAN + 8, inner), jnp.float32),
             pltpu.VMEM((SPAN + 8, 2 * STATE), jnp.float32),
             pltpu.VMEM((SPAN + 8, inner), jnp.float32),
             pltpu.VMEM((SPAN + 8, 2 * STATE), jnp.float32),
             pltpu.VMEM((STATE, inner), jnp.float32),
+            pltpu.VMEM((count, 8, inner), jnp.float32),
+            pltpu.VMEM((8, inner), jnp.float32),
+            pltpu.VMEM((count, 8, 2 * STATE), jnp.float32),
+            pltpu.VMEM((8, 2 * STATE), jnp.float32),
+            pltpu.VMEM((8, heads), jnp.float32),
+            pltpu.VMEM((8, heads), jnp.float32),
+            pltpu.VMEM((8, inner), jnp.float32),
         ],
         compiler_params=vmem(),
     )(proj, shared, proj, shared, dt, seg_col, seg_row, full_cot, states, entry, *fixed)
 
 
 def normed_cot_kernel(gate_low, values_low, shared_low, dt_low, gating, values, control, timestep, tokens, scale, gain, low, row_sum, gain_sum):
+    total = dot(gate_low[...], gating[...]) + dot(values_low[...], values[...])
+    total = total + dot(shared_low[...], control[...]) + dot(dt_low[...], timestep[...])
+    low[...] = total.astype(jnp.bfloat16)
+    product = total * (tokens[...].astype(jnp.float32) * scale[...])
+    gain_sum[...] = fold(product)
+
     @pl.when(pl.program_id(0) == 0)
     def start():
-        gain_sum[...] = jnp.zeros_like(gain_sum)
-
-    total = dot(gate_low[...], gating[...], LAST) + dot(values_low[...], values[...], LAST)
-    total = total + dot(shared_low[...], control[...], LAST) + dot(dt_low[...], timestep[...], LAST)
-    low[...] = total.astype(jnp.bfloat16)
-    product = total * (tokens[...].astype(jnp.float32) * scale[...])
-    gain_sum[...] += fold(product)
-    row_sum[...] = jnp.sum(product * gain[...], axis=1, keepdims=True)
-
-
-def normed_cotangent(gate_low, values_low, shared_low, dt_low, gating, values, control, timestep, tokens, scale, gain):
-    length = gate_low.shape[0]
-    width = gating.shape[0]
-    rows2 = lambda size: pl.BlockSpec((BLOCK, size), lambda c: (c, 0))
+        row_sum[...] = jnp.zeros_like(row_sum)
+
+    row_sum[...] += jnp.sum(product * gain[...], axis=1, keepdims=True)
+
+
+def normed_cotangent(gate_low, values_low, shared_low, dt_low, gating, values, control, timestep, tokens, scale, gain, base):
+    length = values_low.shape[0]
+    width = gating.shape[1]
+    tile = 512
+    here = base // length
+    fixed = lambda array: pl.BlockSpec((length, array.shape[1]), lambda c: (0, 0))
+    late = lambda size: pl.BlockSpec((length, size), lambda c: (here, 0))
+    columns = lambda rows: pl.BlockSpec((rows, tile), lambda c: (0, c))
     parts = (gate_low, values_low, shared_low, dt_low)
     weights = (gating, values, control, timestep)
     return pl.pallas_call(
         normed_cot_kernel,
-        grid=(length // BLOCK,),
-        in_specs=[rows2(a.shape[1]) for a in parts] + [whole_spec(a) for a in weights] + [rows2(width), rows2(1), whole_spec(gain)],
-        out_specs=[rows2(width), rows2(1), pl.BlockSpec((8, width), lambda c: (0, 0))],
+        grid=(width // tile,),
+        in_specs=[late(gate_low.shape[1])] + [fixed(a) for a in parts[1:]] + [columns(a.shape[0]) for a in weights]
+        + [pl.BlockSpec((length, tile), lambda c: (here, c)), late(1), columns(1)],
+        out_specs=[columns(length), pl.BlockSpec((length, 1), lambda c: (0, 0)), columns(8)],
         out_shape=[
             jax.ShapeDtypeStruct((length, width), jnp.bfloat16),
             jax.ShapeDtypeStruct((length, 1), jnp.float32),
@@ -682,6 +768,67 @@
         ],
         compiler_params=vmem(),
     )(*parts, *weights, tokens, scale, gain)
+
+
+def small_call(kernel, shape, scratch, place, *arrays):
+    return pl.pallas_call(
+        kernel,
+        in_specs=[pl.BlockSpec(memory_space=pltpu.SMEM)] + [pl.BlockSpec(memory_space=pltpu.VMEM)] * len(arrays),
+        out_specs=pl.BlockSpec(memory_space=pltpu.VMEM),
+        out_shape=jax.ShapeDtypeStruct(shape, jnp.float32),
+        scratch_shapes=scratch,
+        compiler_params=pltpu.CompilerParams(vmem_limit_bytes=32 * 1024 * 1024),
+    )(place.reshape(1), *arrays)
+
+
+def chip_state(mine, other, core, reverse):
+    half = mine.shape[1] // 2
+
+    def kernel(core, mine, other, out):
+        index = core[0]
+        first = (index == 1) if reverse else (index == 0)
+        lanes = pl.ds(pl.multiple_of(index * half, 128), half)
+        a, b = mine[:, lanes], other[:, lanes]
+        early, late = jnp.where(first, a, b), jnp.where(first, b, a)
+        out[0:STATE, :] = late[STATE : STATE + 1] * early[0:STATE] + late[0:STATE]
+        out[STATE : STATE + 8, :] = late[STATE : STATE + 8] * early[STATE : STATE + 8]
+
+    return small_call(kernel, (STATE + 8, half), [], core, mine, other)
+
+
+def entering_state(chip, chips, reverse, parts):
+    shape = parts[0].shape
+
+    def kernel(chip, *refs):
+        ins, out, held = refs[: len(parts)], refs[len(parts)], refs[len(parts) + 1]
+        for step, ref in enumerate(ins):
+            held[step + 1] = ref[...]
+        here = chip[0]
+        out[...] = jnp.zeros_like(out)
+
+        def add(turn, carry):
+            source = chips - 1 - turn if reverse else turn
+            step = source ^ here
+            out[...] = held[step, STATE : STATE + 1, :] * out[...] + held[step, 0:STATE, :]
+            return carry
+
+        lax.fori_loop(0, chips - 1 - here if reverse else here, add, 0)
+
+    return small_call(kernel, (STATE, shape[1]), [pltpu.VMEM((chips,) + shape, jnp.float32)], chip, *parts)
+
+
+def core_state(mine, other, neighbour, core, reverse):
+    half = mine.shape[1]
+
+    def kernel(core, mine, other, neighbour, out):
+        low = core[0] == 0
+        after = low if reverse else jnp.logical_not(low)
+        for side, value in enumerate((jnp.where(low, mine[...], other[...]), jnp.where(low, other[...], mine[...]))):
+            lanes = slice(side * half, (side + 1) * half)
+            passed = neighbour[STATE : STATE + 1, lanes] * value + neighbour[0:STATE, lanes]
+            out[:, lanes] = jnp.where(after, passed, value)
+
+    return small_call(kernel, (STATE, 2 * half), [], core, mine, other, neighbour)
 
 
 def shards(
@@ -710,6 +857,7 @@
     features = share * ranks
     channels = inner * ranks
     blocks = length // SPAN
+    half = length // 2
     f32, bf16 = jnp.float32, jnp.bfloat16
 
     starts = doc_starts.reshape(blocks, SPAN).astype(bf16)
@@ -721,114 +869,207 @@
     offset_row, baseline_row, postnorm_row = offset[None], baseline[None], postnorm[None]
     timing_row, damping_row = timing[None], damping[None]
 
-    gain = gather_small(prenorm, "head").reshape(1, features).astype(f32)
-    gathered = gather_columns(tokens, "head")
-    wide = gathered.astype(f32)
-    scale = lax.rsqrt(jnp.mean(wide * wide, axis=1, keepdims=True) + epsilon)
-    normed = (wide * scale * gain).astype(bf16)
-    gate_in = jnp.dot(normed, gating, preferred_element_type=f32)
-    projected = jnp.dot(normed, values, preferred_element_type=f32)
-    shared = jnp.dot(normed, control, preferred_element_type=f32)
-    timestep_in = jnp.dot(normed, timestep, preferred_element_type=f32)
-
-    edge = shifted(jnp.concatenate([projected[length - 8 :], shared[length - 8 :]], axis=1), "seq", 1)
-    edge_v, edge_s = edge[:, :inner], edge[:, inner:]
-    local, readers, run, entry, states, final = forward_scan(
-        projected, shared, timestep_in, seg_col, seg_row, edge_v, edge_s, kernel, offset_row, filters, baseline_row,
-        timing_row, damping_row, skip, expand,
-    )
-    passing = jnp.repeat(run[length - 1 :], HDIM, axis=1)
-    incoming = prefix_state(passing, final, "seq", False)
+    gains = Chain(all_chain(prenorm, "head"))
+    tokens_in = Chain(gather_chain(tokens, "head"))
+    weights_back = phase([tokens_in, gains], lambda *a: tuple(w.T for w in a), gating, values, control, timestep, readout)
+    readout_t = weights_back[4]
+    finish(tokens_in, gains)
+    cot_ready, found, gain_blocks = lax.optimization_barrier((cotangent, tokens_in.result, gains.result))
+    upstream = lax.all_gather(cot_ready, "head", axis=1, tiled=True)
+    gain = gain_blocks.reshape(1, features).astype(f32)
+
+    def project(*found):
+        gathered = place_columns(found, "head")
+        wide = gathered.astype(f32)
+        scale = lax.rsqrt(jnp.mean(wide * wide, axis=1, keepdims=True) + epsilon)
+        normed = (wide * scale * gain).astype(bf16)
+        projected = jnp.dot(normed, values, preferred_element_type=f32)
+        shared = jnp.dot(normed, control, preferred_element_type=f32)
+        timestep_in = jnp.dot(normed, timestep, preferred_element_type=f32)
+        return gathered, scale, normed, projected, shared, timestep_in
+
+    gathered, scale, normed, projected, shared, timestep_in = phase([], project, *found)
+    edges = Chain(shift_chain(
+        jnp.concatenate([projected[length - 8 :], shared[length - 8 :], gathered[length - 8 :].astype(f32)], axis=1), "seq", 1
+    ))
+    gate_in = phase([edges], lambda n: jnp.dot(n, gating, preferred_element_type=f32), normed)
+    edge_v, edge_s = edges.result[:, :inner], edges.result[:, inner : inner + 2 * STATE]
+    before = edges.result[:, inner + 2 * STATE :]
+    before = jnp.pad(before, ((0, 8), (0, 0)))
+    before_scale = lax.rsqrt(jnp.mean(before * before, axis=1, keepdims=True) + epsilon)
+    normed_more = jnp.concatenate([normed, (before * before_scale * gain).astype(bf16)], axis=0)
+    params = (kernel, offset_row, filters, baseline_row, timing_row, damping_row, skip, expand)
+    local, readers, run, entry, states, final = phase(
+        [], lambda *a: forward_scan(*a, *params), projected, shared, timestep_in, seg_col, seg_row, edge_v, edge_s
+    )
+    prefix = Chain(state_chain(final, False))
+    finish(prefix)
+    incoming = prefix.result
     full, squares = join_incoming(local, readers, run, gate_in, incoming, expand)
-    squares = small_sum(squares.reshape(length), "head")
-    inverse = lax.rsqrt(squares / channels + epsilon)[:, None]
-    normalized = (full * jax.nn.silu(gate_in) * inverse * postnorm_row).astype(bf16)
-    partial_rows = lax.dot_general(normalized, readout, LAST, preferred_element_type=f32).astype(bf16)
-    branch = scatter_columns(partial_rows, "head")
-    mixed = (tokens.astype(f32) + branch).astype(bf16)
-
-    upstream = gather_columns(cotangent, "head")
-    norm_cot, inner_sum, postnorm_sum = norm_cotangent(upstream, readout, full, gate_in, inverse, postnorm_row)
-    mean = small_sum(inner_sum.reshape(length), "head")[:, None] / channels
+    squared = Chain(sum_chain(squares.reshape(length), "head"))
+    finish(squared)
+    inverse = lax.rsqrt(squared.result / channels + epsilon)[:, None]
+    norm_cot, normalized, inner_sum, postnorm_sum = norm_cotangent(
+        upstream, readout, full, gate_in, inverse, postnorm_row
+    )
+    means = Chain(sum_chain(inner_sum.reshape(length), "head"))
+    partial_rows = phase(
+        [means], lambda n: jnp.dot(n, readout_t, preferred_element_type=f32).astype(bf16), normalized
+    )
+    branch = lax.psum_scatter(partial_rows, "head", scatter_dimension=1, tiled=True)
+    mean = means.result[:, None] / channels
     full_cot, gate_low, pending = gate_cotangent(
-        norm_cot, full, gate_in, inverse, mean, postnorm_row, run, readers, expand
-    )
-    leaving = prefix_state(passing, pending, "seq", True)
-    readout_local = lax.dot_general(upstream, normalized, FIRST, preferred_element_type=f32)
-    gating_local = lax.dot_general(normed, gate_low, FIRST, preferred_element_type=f32)
+        norm_cot, full, gate_in, inverse, mean, postnorm_row, run, readers, expand, final
+    )
+    suffix = Chain(state_chain(pending, True))
+    phase([suffix])
+    readout_local, gating_local = phase(
+        [suffix],
+        lambda u, n, m, g: (
+            lax.dot_general(u, n, FIRST, preferred_element_type=f32).astype(bf16),
+            lax.dot_general(m, g, FIRST, preferred_element_type=f32).astype(bf16),
+        ),
+        upstream, normalized, normed, gate_low,
+    )
+    readout_sum = lax.psum_scatter(readout_local, "seq", scatter_dimension=0, tiled=True)
+    gating_sum = lax.psum_scatter(gating_local, "seq", scatter_dimension=0, tiled=True)
+    finish(suffix)
+    leaving = suffix.result
+
+    def backward(base, size, leaving, after_v, after_s, sums):
+        return backward_scan(
+            projected, shared, timestep_in, seg_col, seg_row, full_cot, states, entry,
+            edge_v, edge_s, *params, incoming, leaving, after_v, after_s, sums, base, size,
+        )
+
+    def normed_back(base, *lows):
+        return normed_cotangent(gate_low, *lows, *weights_back[:4], gathered, scale, gain, base)
+
     zeros_v, zeros_s = jnp.zeros((8, inner), f32), jnp.zeros((8, 2 * STATE), f32)
+    taps = kernel.shape[0]
+    sums = jnp.zeros((2 * taps + 5, inner), f32)
+    late = backward(blocks // 2, blocks // 2, leaving, zeros_v, zeros_s, sums)
+    normed_late = normed_back(half, *late[:3])
+    total_late = Chain(scatter_chain(normed_late[0], "head"))
+    middle = phase(
+        [total_late], lambda *a: backward(blocks // 4, blocks // 4, *a), late[6], late[4], late[5], late[3]
+    )
+    branch, middle = lax.optimization_barrier((branch, middle))
+    normed_middle, early = phase(
+        [total_late],
+        lambda lam, head_v, head_s, sums, *lows: (
+            normed_back(half // 2, *lows), backward(0, blocks // 4, lam, head_v, head_s, sums)
+        ),
+        middle[6], middle[4], middle[5], middle[3], *middle[:3],
+    )
+
+    def share_before(head, taps_of):
+        following = jnp.concatenate([jnp.zeros_like(head), head], axis=0)
+        return sum(taps_of[tap][None] * following[taps - 1 - tap : taps + 7 - tap] for tap in range(taps))
+
+    more_v, more_s = share_before(early[4], kernel), share_before(early[5], filters)
+
+    more_v, more_s = [jnp.pad(more.astype(bf16), ((0, 8), (0, 0))) for more in (more_v, more_s)]
+    more_dt = jnp.zeros((16, heads), bf16)
+    shared_low = jnp.concatenate([early[1], middle[1], late[1], more_s], axis=0)
+    control_local = lax.dot_general(normed_more, shared_low, FIRST, preferred_element_type=f32)
+    first = length // 4
+    normed_early = normed_cotangent(
+        jnp.concatenate([gate_low[:first], jnp.zeros((16, inner), bf16)], axis=0),
+        jnp.concatenate([early[0], more_v], axis=0),
+        jnp.concatenate([early[1], more_s], axis=0),
+        jnp.concatenate([early[2], more_dt], axis=0),
+        *weights_back[:4],
+        jnp.concatenate([gathered[:first], before.astype(bf16)], axis=0),
+        jnp.concatenate([scale[:first], before_scale], axis=0), gain, 0,
+    )
+    finish(total_late)
+    total_early = Chain(
+        scatter_chain(jnp.concatenate([normed_early[0], normed_middle[0]], axis=0), "head", 2)
+    )
+    prenorm_sum = (normed_early[2] + normed_middle[2] + normed_late[2]).sum(0).reshape(-1, inner)
+    flat = jnp.concatenate([early[3], postnorm_sum.sum(0)[None], prenorm_sum], axis=0)
+    flat_rows = flat.shape[0]
+    flat = jnp.pad(flat, ((0, -flat_rows % 32), (0, 0))).reshape(-1, 2 * STATE)
+    holder = []
+    shared_sum = Chain(shared_chain(control_local, flat, holder))
+    row_sum = jnp.concatenate(
+        [normed_early[1][:first], normed_middle[1], normed_late[1], normed_early[1][first : first + 8]], axis=0
+    ).reshape(length + 8)
+    rows_of = Chain(sum_chain(row_sum, "head"))
+
+    def weights_of(*lows):
+        lows = [jnp.concatenate(group, axis=0) for group in (lows[:4], lows[4:])]
+        low = jnp.concatenate([lows[0], jnp.pad(lows[1], ((0, 0), (0, 128 - heads)))], axis=1)
+        return lax.dot_general(normed_more, low, FIRST, preferred_element_type=f32).astype(bf16)
+
+    values_local = phase(
+        [shared_sum, total_early],
+        weights_of, early[0], middle[0], late[0], more_v, early[2], middle[2], late[2], more_dt,
+    )
+    values_sum = lax.psum_scatter(values_local, "seq", scatter_dimension=0, tiled=True)
+    mixed = phase(
+        [shared_sum, total_early], lambda t, s: (t.astype(f32) + s.astype(f32)).astype(bf16), tokens, branch
+    )
+    phase([shared_sum, rows_of])
+    readout_sum, gating_sum = phase([shared_sum, total_early], lambda *a: a, readout_sum, gating_sum)
+    finish(total_early, rows_of, total_late)
+    (copies,) = holder
+    scattered = total_early.result
+    extra = jnp.concatenate([scattered[first : first + 8], jnp.broadcast_to(rows_of.result[length:, None], (8, share))], axis=0)
+    from_next = Chain(shift_chain(extra, "seq", -1))
+
+    def closing(row_sum, early_total, late_total, copies):
+        own_total = jnp.concatenate([early_total[:first], early_total[first + 16 :], late_total], axis=0)
+        own_units = tokens.astype(f32) * scale
+        tokens_gradient = cotangent.astype(f32) + scale * (
+            own_total * prenorm.astype(f32) - own_units * (row_sum[:length, None] / features)
+        )
+        by_head = copies.reshape(ranks, -1, inner)[:, :flat_rows].transpose(1, 0, 2)
+        rows = by_head.reshape(flat_rows, channels)
+        alike = by_head[:, 0]
+        for rank in range(1, ranks):
+            alike = alike + by_head[:, rank]
+        return (
+            tokens_gradient,
+            rows[:taps],
+            rows[taps],
+            alike[taps + 2 : 2 * taps + 2, : 2 * STATE],
+            alike[2 * taps + 2, : 2 * STATE],
+            by_head[2 * taps + 3, :, :heads].reshape(-1),
+            by_head[2 * taps + 4, :, :heads].reshape(-1),
+            rows[taps + 1].reshape(ranks * heads, HDIM).sum(1),
+            rows[2 * taps + 5],
+            alike[2 * taps + 6 :].reshape(-1),
+        )
+
     (
-        values_low, shared_low, timestep_low, tap_sum, offset_sum, filter_sum, base_sum, timing_sum, damping_sum, direct_sum,
-        tail_v, tail_s, head_v, head_s,
-    ) = backward_scan(
-        projected, shared, timestep_in, seg_col, seg_row, full_cot, states, entry,
-        edge_v, edge_s, kernel, offset_row, filters, baseline_row, timing_row, damping_row, skip, expand,
-        incoming, leaving, zeros_v, zeros_s,
-    )
-    ahead = shifted(jnp.concatenate([head_v, head_s], axis=1), "seq", -1)
-    ahead = jnp.concatenate([jnp.zeros_like(ahead), ahead], axis=0)
-    taps = kernel.shape[0]
-    for tap in range(taps):
-        begin = taps - 1 - tap
-        tail_v = tail_v + kernel[tap] * ahead[begin : begin + 8, :inner]
-        tail_s = tail_s + filters[tap] * ahead[begin : begin + 8, inner:]
-    values_low = values_low.at[length - 8 :].set(tail_v.astype(bf16))
-    shared_low = shared_low.at[length - 8 :].set(tail_s.astype(bf16))
-
-    normed_low, row_sum, prenorm_sum = normed_cotangent(
-        gate_low, values_low, shared_low, timestep_low, gating, values, control, timestep, gathered, scale, gain
-    )
-    row_mean = small_sum(row_sum.reshape(length), "head")[:, None] / features
-    own_total = scatter_columns(normed_low, "head")
-    own_units = tokens.astype(f32) * scale
-    tokens_gradient = cotangent.astype(f32) + scale * (own_total * prenorm.astype(f32) - own_units * row_mean)
-    values_local = lax.dot_general(normed, values_low, FIRST, preferred_element_type=f32)
-    control_local = lax.dot_general(normed, shared_low, FIRST, preferred_element_type=f32)
-    timestep_local = lax.dot_general(normed, timestep_low, FIRST, preferred_element_type=f32)
-
-    gating_gradient, values_gradient, readout_gradient = (
-        scatter_rows(gating_local.astype(bf16), "seq"),
-        scatter_rows(values_local.astype(bf16), "seq"),
-        scatter_rows(readout_local.astype(bf16), "seq"),
-    )
-    timestep_gradient = scatter_rows(timestep_local, "seq")
-    control_gradient = sum_everywhere(control_local)
-    everywhere = (filter_sum.sum(1), base_sum.sum(0), prenorm_sum.sum(0))
-    split = (
-        tap_sum.sum(1), offset_sum.sum(0), timing_sum.sum(0), damping_sum.sum(0),
-        direct_sum.sum(0).reshape(heads, HDIM).sum(1), postnorm_sum.sum(0),
-    )
-    flat_every = jnp.concatenate([item.reshape(-1) for item in everywhere])
-    flat_split = jnp.concatenate([item.reshape(-1) for item in split])
-    flat = doubled_sum(jnp.concatenate([flat_every, flat_split]), "seq")
-    pieces = gather_small(flat, "head")
-    summed = jnp.sum(pieces[:, : flat_every.shape[0]], axis=0)
-    totals = []
-    begin = 0
-    for item in everywhere:
-        totals.append(summed[begin : begin + item.size].reshape(item.shape))
-        begin += item.size
-    for item in split:
-        piece = pieces[:, begin : begin + item.size].reshape((ranks,) + item.shape)
-        totals.append(jnp.moveaxis(piece, 0, -2).reshape(item.shape[:-1] + (-1,)))
-        begin += item.size
+        tokens_gradient, kernel_gradient, offset_gradient, filters_gradient, baseline_gradient, timing_gradient,
+        damping_gradient, direct_gradient, postnorm_gradient, prenorm_gradient,
+    ) = phase([shared_sum, from_next], closing, rows_of.result, scattered, total_late.result, copies)
+    finish(shared_sum, from_next)
+    more_rows, more_sums = from_next.result[:8], from_next.result[8:, :1] / features
+    last = scale[length - 8 :] * (
+        more_rows * prenorm.astype(f32) - tokens[length - 8 :].astype(f32) * scale[length - 8 :] * more_sums
+    )
+    tokens_gradient = tokens_gradient.at[length - 8 :].add(last)
     return (
         mixed,
         tokens_gradient,
-        totals[2],
-        gating_gradient,
-        values_gradient,
-        control_gradient,
-        timestep_gradient,
-        totals[3],
-        totals[4],
-        totals[0],
-        totals[1],
-        totals[5],
-        totals[6],
-        totals[7],
-        totals[8],
-        readout_gradient,
+        prenorm_gradient,
+        gating_sum.astype(f32),
+        values_sum[:, :inner].astype(f32),
+        shared_sum.result,
+        values_sum[:, inner : inner + heads].astype(f32),
+        kernel_gradient,
+        offset_gradient,
+        filters_gradient,
+        baseline_gradient,
+        timing_gradient,
+        damping_gradient,
+        direct_gradient,
+        postnorm_gradient,
+        readout_sum.astype(f32),
     )
 
 

time: 625 us -> 490 us (0.78)
  waiting for transfers between devices: 269 us -> 93.6 us
  local copies, waits for them, and re-layouts: 48.3 us -> 77.2 us
  Pallas kernels: 104 us -> 122 us
  other arithmetic: 64.2 us -> 49.7 us
  between operations: 2.49 us -> 15.4 us
  starting transfers between devices: 79.8 us -> 70.2 us
  matrix products: 45.5 us -> 52.3 us
    ppermute x74 -> x50, waiting for transfers between devices: 269 us -> 93.5 us  [phase(): lax.ppermute(value, send[1], send[2])]
    optimization_barrier x0 -> x11, local copies, waits for them, and re-layouts: none -> 21.2 us  [the longest x8 18.2 us: phase(): values, inputs = lax.optimization_barrier((values, inputs))]
    pallas_call x2 -> x12, Pallas kernels: 57.6 us -> 73.6 us  [the longest x3 46 us: backward_scan(): pl.pallas_call(functools.partial(backward_kernel, base == 0), grid=(block...]
    ppermute x74 -> x50, starting transfers between devices: 79.8 us -> 69.5 us  [phase(): lax.ppermute(value, send[1], send[2])]
    select_n x8 -> x0, other arithmetic: 8.5 us -> none  [the longest x2 3.99 us: prefix_state(): prefix = jnp.where(other_first, prefix_pass * other_state + prefix, prefix)]
    unnamed x102 -> x116, local copies, waits for them, and re-layouts: 4.97 us -> 13.1 us
    dot_general x10 -> x9, matrix products: 44.7 us -> 52.1 us  [the longest x1 10.8 us: weights_of(): lax.dot_general(normed_more, low, FIRST, preferred_element_type=f32)]
    slice x19 -> x25, local copies, waits for them, and re-layouts: 10.6 us -> 13.9 us  [the longest x2 2.6 us: scatter_chain(): up[begin:end].astype(jnp.bfloat16)]
  transfers between devices with their start and end apart: 74 -> 55, of which waited for: 33 -> 20; matrix products, arithmetic and copies ran while one was open for 20% -> 34% of each run, Pallas kernels for 9% -> 23%
where the time goes in v3:
time: 490 us; the launch traced here: 480 us
  Pallas kernels  122 us (25%)
  waiting for transfers between devices  93.6 us (19%)
  local copies, waits for them, and re-layouts  77.2 us (16%)
  starting transfers between devices  70.2 us (14%)
  matrix products  52.3 us (11%)
  other arithmetic  49.7 us (10%)
  between operations  15.4 us (3%)
    ppermute x50, waiting for transfers between devices, phase(): lax.ppermute(value, send[1], send[2])  93.5 us
    ppermute x50, starting transfers between devices, phase(): lax.ppermute(value, send[1], send[2])  69.5 us
    pallas_call x3, Pallas kernels, backward_scan(): pl.pallas_call(functools.partial(backward_kernel, base == 0), grid=(block...  46 us
    pallas_call x3, Pallas kernels, normed_cotangent(): pl.pallas_call(normed_cot_kernel, grid=(width // tile,), in_specs=[late(g...  27.2 us
    pallas_call x1, Pallas kernels, forward_scan(): pl.pallas_call(forward_kernel, grid=(blocks,), in_specs=[rows2(inner), ro...  18.6 us
    optimization_barrier x8, local copies, waits for them, and re-layouts, phase(): values, inputs = lax.optimization_barrier((values, inputs))  18.2 us
    unnamed x116, local copies, waits for them, and re-layouts  13.1 us
    pallas_call x1, Pallas kernels, norm_cotangent(): pl.pallas_call(norm_cot_kernel, grid=(length // BLOCK,), in_specs=[rows2(...  11.7 us
  transfers between devices with their start and end apart: 55, of which 20 were waited for; matrix products, arithmetic and copies ran while one was open for 34% of the time, Pallas kernels for 23%

profile of v3, /device:TPU:4, one launch (start us, length us, event | category | flops | bytes accessed | tf_op | source)
XLA Modules:
  0.0 480.2 jit_solution(9202079290518644494)
XLA Ops:
  14.6 6.5 %copy.67 = bf16[2048,1024]{0,1:T(8,128)(2,1)} copy(bf16[2048,1024]{1,0:T(8,128)(2,1)} %param.29) | data formatting | bytes 8388608 | tf_op jit(solution)/shard_map/optimization_barrier | solution.py:48
  21.1 6.6 %copy.68 = bf16[2048,1024]{0,1:T(8,128)(2,1)} copy(bf16[2048,1024]{1,0:T(8,128)(2,1)} %param.30) | data formatting | bytes 8388608 | tf_op jit(solution)/shard_map/optimization_barrier | solution.py:48
  29.9 26.3 %collective-permute-done.2 = bf16[512]{0:T(512)(128)(2,1)S(1)} collective-permute-done((bf16[512]{0:T(512)(128)(2,1)}, bf16[512]{0:T(512)(128)(2,1)S(1)}, u32[]{:S(2)}, u32[]{:S(2)}) %collective-permute-start.2) | collective-permute-done | bytes 1056 | tf_op jit(solution)/shard_map/ppermute | solution.py:50
  61.7 12.0 %collective-permute-done.5 = bf16[512,512]{1,0:T(8,128)(2,1)} collective-permute-done((bf16[512,512]{1,0:T(8,128)(2,1)S(1)}, bf16[512,512]{1,0:T(8,128)(2,1)}, u32[]{:S(2)}, u32[]{:S(2)}) %collective-permute-start.5) | collective-permute-done | bytes 524320 | tf_op jit(solution)/shard_map/ppermute | solution.py:50
  73.7 8.7 %collective-permute-done.6 = bf16[512,512]{1,0:T(8,128)(2,1)} collective-permute-done((bf16[512,512]{1,0:T(8,128)(2,1)S(1)}, bf16[512,512]{1,0:T(8,128)(2,1)}, u32[]{:S(2)}, u32[]{:S(2)}) %collective-permute-start.6) | collective-permute-done | bytes 524320 | tf_op jit(solution)/shard_map/ppermute | solution.py:50
  92.2 4.5 fusion.75.proj.before_v
  99.0 6.1 %fusion.78.gate_in = f32[1024,1024]{1,0:T(8,128)} fusion(bf16[1024,2048]{1,0:T(8,128)(2,1)S(1)} %fusion.2, bf16[2048,1024]{1,0:T(8,128)(2,1)S(1)} %copy-done.14), kind=kOutput, calls=%fused_computation.199 | convolution fusion | flops 4294967296 | bytes 12582912 | tf_op jit(solution)/shard_map/dot_general | solution.py:895
  108.3 18.6 %shard_map.288 = (f32[1024,1024]{1,0:T(8,128)}, bf16[1024,128]{1,0:T(8,128)(2,1)}, f32[1024,16]{1,0:T(8,128)}, f32[8,1,16]{2,1,0:T(1,128)}, f32[8,128,1024]{2,1,0:T(8,128)}, /*index=5*/f32[136,1024]{1,0:T(8,128)}) custom-call(f32[1024,1024]{1,0:T(8,128)} %copy-done.4, f32[1024,256]{1,0:T(8,128)} %copy-done.6, f32[1024,16]{1,0:T(8,128)} %copy.70.dt, ...), custom_call_target="tpu_custom_call" | custom-call | tf_op jit(solution)/shard_map/pallas_call | solution.py:402
  135.1 11.4 %collective-permute-done.10.refs_1_ = f32[136,512]{1,0:T(8,128)S(1)} collective-permute-done((f32[136,512]{1,0:T(8,128)S(1)}, f32[136,512]{1,0:T(8,128)S(1)}, u32[]{:S(2)}, u32[]{:S(2)}) %collective-permute-start.10) | collective-permute-done | bytes 278560 | tf_op jit(solution)/shard_map/ppermute | solution.py:50
  150.3 7.3 %shard_map.292 = (f32[1024,1024]{1,0:T(8,128)}, f32[1024,1]{1,0:T(8,128)}) custom-call(f32[1024,1024]{1,0:T(8,128)} %get-tuple-element.364.local, bf16[1024,128]{1,0:T(8,128)(2,1)} %get-tuple-element.365.readers, f32[1024,16]{1,0:T(8,128)} %get-tuple-element.366.run, f32[1024,1024]{1,0:T(8,128)} %fusion.78.gate_in, f32[128,1024]{1,0:T(8,128)} %copy-done, ...), custom_call_target="tpu_custom_call" | custom-call | tf_op jit(solution)/shard_map/pallas_call | solution.py:444
  166.4 11.7 %shard_map.293 = (f32[1024,1024]{1,0:T(8,128)}, bf16[1024,1024]{1,0:T(8,128)(2,1)}, f32[1024,1]{1,0:T(8,128)}, f32[8,1024]{1,0:T(8,128)}) custom-call(bf16[1024,2048]{1,0:T(8,128)(2,1)} %all-gather.2.cloned.1.call-done.upstream, bf16[2048,1024]{1,0:T(8,128)(2,1)} %readout.1, f32[1024,1024]{1,0:T(8,128)} %get-tuple-element.375.full.full_in, ...), custom_call_target="tpu_custom_call" | custom-call | tf_op jit(solution)/shard_map/pallas_call | solution.py:472
  184.0 9.3 %convolution_convert_fusion.3 = bf16[1024,2048]{1,0:T(8,128)(2,1)} fusion(bf16[1024,1024]{1,0:T(8,128)(2,1)} %get-tuple-element.403, bf16[1024,2048]{0,1:T(8,128)(2,1)} %bitcast.135), kind=kOutput, calls=%fused_computation.11 | convolution fusion | flops 4297064448 | bytes 10485760 | tf_op jit(solution)/shard_map/dot_general | solution.py:917
  194.9 10.4 %shard_map.294 = (f32[1024,1024]{1,0:T(8,128)}, bf16[1024,1024]{1,0:T(8,128)(2,1)}, f32[136,1024]{1,0:T(8,128)}) custom-call(f32[1024,1024]{1,0:T(8,128)} %get-tuple-element.383.norm_cot, f32[1024,1024]{1,0:T(8,128)} %get-tuple-element.375.full.full_in, f32[1024,1024]{1,0:T(8,128)} %fusion.78.gate_in, f32[1024,1]{1,0:T(8,128)} %copy.72.inverse, ...), custom_call_target="tpu_custom_call" | custom-call | tf_op jit(solution)/shard_map/pallas_call | solution.py:510
  212.3 7.8 %convolution_convert_fusion.1 = bf16[2048,1024]{1,0:T(8,128)(2,1)} fusion(bf16[1024,2048]{1,0:T(8,128)(2,1)S(1)} %copy-done.8, bf16[1024,1024]{1,0:T(8,128)(2,1)} %get-tuple-element.405.gate_low), kind=kOutput, calls=%fused_computation.9 | convolution fusion | flops 4297064448 | bytes 10485760 | tf_op jit(solution)/shard_map/dot_general | solution.py:930
  220.1 9.5 %convolution_convert_fusion.2 = bf16[2048,1024]{1,0:T(8,128)(2,1)} fusion(bf16[1024,2048]{1,0:T(8,128)(2,1)} %all-gather.2.cloned.1.call-done.upstream, bf16[1024,1024]{1,0:T(8,128)(2,1)} %get-tuple-element.403), kind=kOutput, calls=%fused_computation.10 | convolution fusion | flops 4297064448 | bytes 10485760 | tf_op jit(solution)/shard_map/dot_general | solution.py:929
  242.1 21.2 %shard_map.298 = (bf16[512,1024]{1,0:T(8,128)(2,1)}, bf16[512,256]{1,0:T(8,128)(2,1)}, bf16[512,16]{1,0:T(8,128)(2,1)}, f32[13,1024]{1,0:T(8,128)}, f32[8,1024]{...) custom-call(f32[1024,1024]{1,0:T(8,128)} %copy-done.4, f32[1024,256]{1,0:T(8,128)} %copy-done.6, ...), custom_call_target="tpu_custom_call" | custom-call | tf_op jit(solution)/shard_map/pallas_call | solution.py:709
  263.3 10.8 %shard_map.299 = (bf16[512,2048]{1,0:T(8,128)(2,1)}, f32[512,1]{1,0:T(8,128)}, f32[8,2048]{1,0:T(8,128)}) custom-call(bf16[1024,1024]{1,0:T(8,128)(2,1)} %get-tuple-element.405.gate_low, bf16[512,1024]{1,0:T(8,128)(2,1)} %get-tuple-element.488.values_low, bf16[512,256]{1,0:T(8,128)(2,1)} %get-tuple-element.410.shared_low, ...), custom_call_target="tpu_custom_call" | custom-call | tf_op jit(solution)/shard_map/pallas_call | solution.py:758
  279.0 12.5 %shard_map.300 = (bf16[256,1024]{1,0:T(8,128)(2,1)}, bf16[256,256]{1,0:T(8,128)(2,1)}, bf16[256,16]{1,0:T(8,128)(2,1)}, f32[13,1024]{1,0:T(8,128)}, f32[8,1024]{...) custom-call(f32[1024,1024]{1,0:T(8,128)} %copy-done.4, f32[1024,256]{1,0:T(8,128)} %copy-done.6, ...), custom_call_target="tpu_custom_call" | custom-call | tf_op jit(solution)/shard_map/pallas_call | solution.py:709
  301.6 8.0 %shard_map.301 = (bf16[256,2048]{1,0:T(8,128)(2,1)}, f32[256,1]{1,0:T(8,128)}, f32[8,2048]{1,0:T(8,128)}) custom-call(bf16[1024,1024]{1,0:T(8,128)(2,1)} %get-tuple-element.405.gate_low, bf16[256,1024]{1,0:T(8,128)(2,1)} %get-tuple-element.487.values_low, bf16[256,256]{1,0:T(8,128)(2,1)} %get-tuple-element.455.shared_low, ...), custom_call_target="tpu_custom_call" | custom-call | tf_op jit(solution)/shard_map/pallas_call | solution.py:758
  309.6 12.3 %shard_map.302 = (bf16[256,1024]{1,0:T(8,128)(2,1)}, bf16[256,256]{1,0:T(8,128)(2,1)}, bf16[256,16]{1,0:T(8,128)(2,1)}, f32[13,1024]{1,0:T(8,128)}, f32[8,1024]{...) custom-call(f32[1024,1024]{1,0:T(8,128)} %copy-done.4, f32[1024,256]{1,0:T(8,128)} %copy-done.6, ...), custom_call_target="tpu_custom_call" | custom-call | tf_op jit(solution)/shard_map/pallas_call | solution.py:709
  328.6 8.4 %shard_map.303 = (bf16[272,2048]{1,0:T(8,128)(2,1)}, f32[272,1]{1,0:T(8,128)}, f32[8,2048]{1,0:T(8,128)}) custom-call(bf16[272,1024]{1,0:T(8,128)(2,1)} %slice_select_fusion.gate_low, bf16[272,1024]{1,0:T(8,128)(2,1)} %pad_maximum_fusion.6.values_low, bf16[272,256]{1,0:T(8,128)(2,1)} %pad_maximum_fusion.14.shared_low, bf16[272,16]{1,0:T(8,128)(2,1)} %concatenate.100.dt_low, ...), custom_call_target="tpu_custom_call" | custom-call | tf_op jit(solution)/shard_map/pallas_call | solution.py:758
  349.9 4.0 collective-permute-start.31
  354.0 10.8 %convolution_convert_fusion = bf16[2048,1152]{1,0:T(8,128)(2,1)} fusion(bf16[16,2048]{1,0:T(8,128)(2,1)} %fusion.36, bf16[1024,2048]{1,0:T(8,128)(2,1)} %copy-done.7, bf16[1040,16]{1,0:T(8,128)(2,1)} %copy.87, bf16[16,1024]{1,0:T(8,128)(2,1)} %copy-done.42, bf16[512,1024]{1,0:T(8,128)(2,1)} %get-tuple-element.488.values_low, ...), kind=kOutput, calls=%fused_computation.5 | convolution fusion | flops 4932591616 | bytes 11141632 | tf_op jit(solution)/shard_map/dot_general | solution.py:1004
  412.4 8.8 %collective-permute-done.40 = f32[1032]{0:T(1024)S(1)} collective-permute-done((f32[1032]{0:T(1024)S(1)}, f32[1032]{0:T(1024)S(1)}, u32[]{:S(2)}, u32[]{:S(2)}) %collective-permute-start.40) | collective-permute-done | bytes 4160 | tf_op jit(solution)/shard_map/ppermute | solution.py:50
  (396 shorter events, 211.1 us)
Async XLA Ops:
  7.2 159.2 %all-gather.2.cloned.1.call-start = ((), (), s32[]{:S(2)}) async-start(), calls=%async_computation.4 | async-start | bytes 5242880 | tf_op jit(solution)/shard_map/all_gather | solution.py:878
  7.2 49.6 %collective-permute-start = (bf16[1024,512]{1,0:T(8,128)(2,1)}, bf16[1024,512]{1,0:T(8,128)(2,1)S(1)}, u32[]{:S(2)}, u32[]{:S(2)}) collective-permute-start(bf16[1024,512]{1,0:T(8,128)(2,1)} %param.27), channel_id=1, source_target_pairs={{0,1},{1,2},{2,3},{3,0},{4,5},{5,6},{6,7},{7,4},{8,9},{9,10},{10,1... | collective-permute-start | bytes 3145736 | tf_op jit(solution)/shard_map/ppermute | solution.py:50
  8.9 48.0 %collective-permute-start.1 = (bf16[1024,512]{1,0:T(8,128)(2,1)}, bf16[1024,512]{1,0:T(8,128)(2,1)S(1)}, u32[]{:S(2)}, u32[]{:S(2)}) collective-permute-start(bf16[1024,512]{1,0:T(8,128)(2,1)} %param.27), channel_id=1, source_target_pairs={{0,3},{1,0},{2,1},{3,2},{4,7},{5,4},{6,5},{7,6},{8,11},{9,8},{10,9... | collective-permute-start | bytes 3145736 | tf_op jit(solution)/shard_map/ppermute | solution.py:50
  11.1 45.1 %collective-permute-start.2 = (bf16[512]{0:T(512)(128)(2,1)}, bf16[512]{0:T(512)(128)(2,1)S(1)}, u32[]{:S(2)}, u32[]{:S(2)}) collective-permute-start(bf16[512]{0:T(512)(128)(2,1)} %param.28), channel_id=1, source_target_pairs={{0,3},{1,0},{2,1},{3,2},{4,7},{5,4},{6,5},{7,6},{8,11},{9,8},{10,9... | collective-permute-start | bytes 3080 | tf_op jit(solution)/shard_map/ppermute | solution.py:50
  12.9 43.9 %collective-permute-start.3 = (bf16[512]{0:T(512)(128)(2,1)}, bf16[512]{0:T(512)(128)(2,1)S(1)}, u32[]{:S(2)}, u32[]{:S(2)}) collective-permute-start(bf16[512]{0:T(512)(128)(2,1)} %param.28), channel_id=1, source_target_pairs={{0,2},{1,3},{2,0},{3,1},{4,6},{5,7},{6,4},{7,5},{8,10},{9,11},{10,... | collective-permute-start | bytes 3080 | tf_op jit(solution)/shard_map/ppermute | solution.py:50
  12.9 43.9 %collective-permute-start.4 = (bf16[512]{0:T(512)(128)(2,1)}, bf16[512]{0:T(512)(128)(2,1)S(1)}, u32[]{:S(2)}, u32[]{:S(2)}) collective-permute-start(bf16[512]{0:T(512)(128)(2,1)} %param.28), channel_id=1, source_target_pairs={{0,1},{1,2},{2,3},{3,0},{4,5},{5,6},{6,7},{7,4},{8,9},{9,10},{10,1... | collective-permute-start | bytes 3080 | tf_op jit(solution)/shard_map/ppermute | solution.py:50
  56.9 16.8 %collective-permute-start.5 = (bf16[512,512]{1,0:T(8,128)(2,1)S(1)}, bf16[512,512]{1,0:T(8,128)(2,1)}, u32[]{:S(2)}, u32[]{:S(2)}) collective-permute-start(bf16[512,512]{1,0:T(8,128)(2,1)S(1)} %slice.325), channel_id=1, source_target_pairs={{0,1},{1,2},{2,3},{3,0},{4,5},{5,6},{6,7},{7,4},{8,9},{9,10},{10,1... | collective-permute-start | bytes 1572872 | tf_op jit(solution)/shard_map/ppermute | solution.py:50
  57.6 24.9 %collective-permute-start.6 = (bf16[512,512]{1,0:T(8,128)(2,1)S(1)}, bf16[512,512]{1,0:T(8,128)(2,1)}, u32[]{:S(2)}, u32[]{:S(2)}) collective-permute-start(bf16[512,512]{1,0:T(8,128)(2,1)S(1)} %slice.326), channel_id=1, source_target_pairs={{0,3},{1,0},{2,1},{3,2},{4,7},{5,4},{6,5},{7,6},{8,11},{9,8},{10,9... | collective-permute-start | bytes 1572872 | tf_op jit(solution)/shard_map/ppermute | solution.py:50
  83.7 208.5 %reduce-scatter.5.cloned.1.call-start = ((), (), s32[]{:S(2)}) async-start(), calls=%async_computation.5 | async-start | bytes 5242880 | tf_op jit(solution)/shard_map/reduce_scatter | solution.py:919
  193.4 236.2 %reduce-scatter.7.cloned.1.call-start = ((), (), s32[]{:S(2)}) async-start(), calls=%async_computation.6 | async-start | bytes 4718592 | tf_op jit(solution)/shard_map/reduce_scatter | solution.py:934
  208.7 20.9 %collective-permute-start.20 = (f32[136,512]{1,0:T(8,128)S(1)}, f32[136,512]{1,0:T(8,128)S(1)}, u32[]{:S(2)}, u32[]{:S(2)}) collective-permute-start(f32[136,512]{1,0:T(8,128)S(1)} %shard_map.295), channel_id=1, source_target_pairs={{0,8},{4,12},{8,0},{12,4},{16,24},{20,28},{24,16},{28,20},{1,9},{5... | collective-permute-start | bytes 835592 | tf_op jit(solution)/shard_map/ppermute | solution.py:50
  209.0 20.6 %collective-permute-start.21 = (f32[136,512]{1,0:T(8,128)S(1)}, f32[136,512]{1,0:T(8,128)S(1)}, u32[]{:S(2)}, u32[]{:S(2)}) collective-permute-start(f32[136,512]{1,0:T(8,128)S(1)} %shard_map.295), channel_id=1, source_target_pairs={{0,16},{4,20},{8,24},{12,28},{16,0},{20,4},{24,8},{28,12},{1,17},{... | collective-permute-start | bytes 835592 | tf_op jit(solution)/shard_map/ppermute | solution.py:50
  210.7 19.0 %collective-permute-start.22 = (f32[136,512]{1,0:T(8,128)S(1)}, f32[136,512]{1,0:T(8,128)S(1)}, u32[]{:S(2)}, u32[]{:S(2)}) collective-permute-start(f32[136,512]{1,0:T(8,128)S(1)} %shard_map.295), channel_id=1, source_target_pairs={{0,24},{4,28},{8,16},{12,20},{16,8},{20,12},{24,0},{28,4},{1,25},{... | collective-permute-start | bytes 835592 | tf_op jit(solution)/shard_map/ppermute | solution.py:50
  229.7 199.9 %reduce-scatter.9.cloned.1.call-start = ((), (), s32[]{:S(2)}) async-start(), calls=%async_computation.7 | async-start | bytes 4718592 | tf_op jit(solution)/shard_map/reduce_scatter | solution.py:935
  238.6 231.0 %reduce-scatter.11.cloned.1.call-start = ((), (), s32[]{:S(2)}) async-start(), calls=%async_computation.8 | async-start | bytes 5308416 | tf_op jit(solution)/shard_map/reduce_scatter | solution.py:1010
  275.1 16.7 %collective-permute-start.24 = (bf16[256,512]{1,0:T(8,128)(2,1)S(1)}, bf16[256,512]{1,0:T(8,128)(2,1)S(1)}, u32[]{:S(2)}, u32[]{:S(2)}) collective-permute-start(bf16[256,512]{1,0:T(8,128)(2,1)S(1)} %get-tuple-element.422), channel_id=1, source_target_pairs={{0,1},{1,2},{2,3},{3,0},{4,5},{5,6},{6,7},{7,4},{8,9},{9,10},{10,1... | collective-permute-start | bytes 786440 | tf_op jit(solution)/shard_map/ppermute | solution.py:50
  292.3 29.6 %collective-permute-start.26 = (bf16[512,512]{1,0:T(8,128)(2,1)S(1)}, bf16[512,512]{1,0:T(8,128)(2,1)}, u32[]{:S(2)}, u32[]{:S(2)}) collective-permute-start(bf16[512,512]{1,0:T(8,128)(2,1)S(1)} %convert_element_type.231), channel_id=1, source_target_pairs={{0,1},{1,2},{2,3},{3,0},{4,5},{5,6},{6,7},{7,4},{8,9},{9,10},{10,1... | collective-permute-start | bytes 1572872 | tf_op jit(solution)/shard_map/ppermute | solution.py:50
  292.8 29.1 %collective-permute-start.27 = (bf16[512,512]{1,0:T(8,128)(2,1)S(1)}, bf16[512,512]{1,0:T(8,128)(2,1)}, u32[]{:S(2)}, u32[]{:S(2)}) collective-permute-start(bf16[512,512]{1,0:T(8,128)(2,1)S(1)} %convert_element_type.234), channel_id=1, source_target_pairs={{0,3},{1,0},{2,1},{3,2},{4,7},{5,4},{6,5},{7,6},{8,11},{9,8},{10,9... | collective-permute-start | bytes 1572872 | tf_op jit(solution)/shard_map/ppermute | solution.py:50
  349.9 17.9 %collective-permute-start.28 = (f32[4,256,256]{2,1,0:T(8,128)}, f32[4,256,256]{2,1,0:T(8,128)}, u32[]{:S(2)}, u32[]{:S(2)}) collective-permute-start(f32[4,256,256]{2,1,0:T(8,128)} %dynamic-slice_bitcast_fusion), channel_id=1, source_target_pairs={{0,4},{4,0},{8,12},{12,8},{16,20},{20,16},{24,28},{28,24},{1,5},{5... | collective-permute-start | bytes 3145736 | tf_op jit(solution)/shard_map/ppermute | solution.py:50
  349.9 17.9 %collective-permute-start.30 = (bf16[264,512]{1,0:T(8,128)(2,1)}, bf16[264,512]{1,0:T(8,128)(2,1)}, u32[]{:S(2)}, u32[]{:S(2)}) collective-permute-start(bf16[264,512]{1,0:T(8,128)(2,1)} %get-tuple-element.484), channel_id=1, source_target_pairs={{0,1},{1,2},{2,3},{3,0},{4,5},{5,6},{6,7},{7,4},{8,9},{9,10},{10,1... | collective-permute-start | bytes 811016 | tf_op jit(solution)/shard_map/ppermute | solution.py:50
  349.9 17.9 %collective-permute-start.31 = (bf16[264,512]{1,0:T(8,128)(2,1)}, bf16[264,512]{1,0:T(8,128)(2,1)}, u32[]{:S(2)}, u32[]{:S(2)}) collective-permute-start(bf16[264,512]{1,0:T(8,128)(2,1)} %get-tuple-element.485), channel_id=1, source_target_pairs={{0,3},{1,0},{2,1},{3,2},{4,7},{5,4},{6,5},{7,6},{8,11},{9,8},{10,9... | collective-permute-start | bytes 811016 | tf_op jit(solution)/shard_map/ppermute | solution.py:50
  400.3 28.1 %collective-permute-start.37 = (bf16[512,256]{1,0:T(8,128)(2,1)S(1)}, bf16[512,256]{1,0:T(8,128)(2,1)S(1)}, u32[]{:S(2)}, u32[]{:S(2)}) collective-permute-start(bf16[512,256]{1,0:T(8,128)(2,1)S(1)} %pad_maximum_fusion.13), channel_id=1, source_target_pairs={{0,3},{1,0},{2,1},{3,2},{4,7},{5,4},{6,5},{7,6},{8,11},{9,8},{10,9... | collective-permute-start | bytes 786440 | tf_op jit(solution)/shard_map/ppermute | solution.py:50
  402.5 25.9 %collective-permute-start.38 = (bf16[512,256]{1,0:T(8,128)(2,1)S(1)}, bf16[512,256]{1,0:T(8,128)(2,1)S(1)}, u32[]{:S(2)}, u32[]{:S(2)}) collective-permute-start(bf16[512,256]{1,0:T(8,128)(2,1)S(1)} %pad_maximum_fusion.13), channel_id=1, source_target_pairs={{0,2},{1,3},{2,0},{3,1},{4,6},{5,7},{6,4},{7,5},{8,10},{9,11},{10,... | collective-permute-start | bytes 786440 | tf_op jit(solution)/shard_map/ppermute | solution.py:50
  402.8 25.6 %collective-permute-start.39 = (bf16[512,256]{1,0:T(8,128)(2,1)S(1)}, bf16[512,256]{1,0:T(8,128)(2,1)S(1)}, u32[]{:S(2)}, u32[]{:S(2)}) collective-permute-start(bf16[512,256]{1,0:T(8,128)(2,1)S(1)} %pad_maximum_fusion.13), channel_id=1, source_target_pairs={{0,1},{1,2},{2,3},{3,0},{4,5},{5,6},{6,7},{7,4},{8,9},{9,10},{10,1... | collective-permute-start | bytes 786440 | tf_op jit(solution)/shard_map/ppermute | solution.py:50
  (86 other events, 709.5 us)
Sparse Core Ops, SparseCore 0:
  83.9 80.6 all-gather.1
  193.6 75.4 reduce-scatter.4
  272.8 51.7 reduce-scatter.6
  327.8 51.3 reduce-scatter.8
  384.2 58.2 reduce-scatter.10
